TPU v7x, 32 devices: a whole 2x2x4 slice. The times are simulated.
32 devices in a mesh: row: 8 (over y, x, core), col: 4 (over z).
Axes of the slice: x: 2, y: 2, z: 4, core: 2. Of those that a mesh axis runs over, the one named last changes fastest.
Arguments:
- enc_out: bfloat16 [2048, 4096], P(('row', 'col')), may hold values from -6 to 6
- keep: int32 [32, 64], P('row'), may hold values from 0 to 255, as said below
- pos_ids: int32 [32, 256], P('row'), may hold values from 0 to 1023
- mask_token: bfloat16 [4096], P('col'), may hold values from -5 to 5
- pos_table: bfloat16 [1024, 4096], P(None, 'col'), may hold values from -4 to 4
- gain: bfloat16 [4096], P('col'), may hold values from 0.25 to 1.75
- w_query: bfloat16 [4096, 4096], P('row', 'col')
- w_key: bfloat16 [4096, 4096], P('row', 'col')
- w_value: bfloat16 [4096, 4096], P('row', 'col'), may hold values from -0.09375 to 0.09375
- w_out: bfloat16 [4096, 4096], P('row', 'col'), may hold values from -0.75 to 0.75
Outputs:
- update: bfloat16 [8192, 4096], P('row', 'col')
Inputs may be any that keep to these rules, and one draw needn't show every extreme that they name: `keep`: each row holds 64 different patch indices.
All inputs are finite; a program needn't handle non-finite values.
Results may differ from a plain program's by a relative error of at most 0.019.
Values may be sent and summed in bfloat16 or wider, within the bound.
No kernel may reach another device: no remote copies, remote signals or barrier semaphores. Data moves between devices by JAX's collectives and lax.ppermute only.
A program may use at most 128 MiB of HBM per device.

v0:
```python
import jax
import jax.numpy as jnp
from jax import lax
from jax.sharding import PartitionSpec as P

D = 4096
HEADS = 32
L = 256
KEEP = 64


EPS = 1e-05


def add_rows(left, piece):
    return jnp.dot(left, piece, preferred_element_type=jnp.float32)


def on_device(enc_out, keep, pos_ids, mask_token, pos_table, gain, w_query, w_key, w_value, w_out):
    visible = lax.all_to_all(enc_out, "col", split_axis=1, concat_axis=0, tiled=True)
    images = keep.shape[0]
    width = visible.shape[1]
    visible = visible.reshape(images, KEEP, width)
    places = lax.broadcasted_iota(jnp.int32, (images, L, KEEP), 1)
    onehot = (places == keep[:, None, :]).astype(jnp.bfloat16)
    placed = jnp.einsum("spk,skd->spd", onehot, visible, preferred_element_type=jnp.float32)
    present = jnp.sum(onehot.astype(jnp.float32), axis=2, keepdims=True)
    base = placed + (1.0 - present) * mask_token.astype(jnp.float32)[None, None, :]
    position = jnp.take(pos_table, pos_ids, axis=0).astype(jnp.float32)
    filled = (base + position).astype(jnp.bfloat16).reshape(images * L, width)
    values = filled.astype(jnp.float32)
    sums, squares = lax.psum((jnp.sum(values, axis=1), jnp.sum(values * values, axis=1)), "col")
    mean = (sums / D)[:, None]
    var = (squares / D)[:, None] - mean * mean
    local = ((values - mean) * lax.rsqrt(var + EPS) * gain.astype(jnp.float32)[None, :]).astype(
        jnp.bfloat16
    )
    normed = lax.all_gather(local, "col", axis=1, tiled=True)

    def add_one(piece):
        return add_rows(normed, piece)

    query = add_one(lax.all_gather(w_query, "row", axis=0, tiled=True))
    key = add_one(lax.all_gather(w_key, "row", axis=0, tiled=True))
    value = add_one(lax.all_gather(w_value, "row", axis=0, tiled=True))
    head_dim = D // HEADS
    local_heads = w_query.shape[1] // head_dim
    shape = (images, L, local_heads, head_dim)
    query = query.astype(jnp.bfloat16).reshape(shape)
    key = key.astype(jnp.bfloat16).reshape(shape)
    value = value.astype(jnp.bfloat16).reshape(shape)
    scores = jnp.einsum(
        "sqhd,skhd->shqk", query, key, preferred_element_type=jnp.float32
    ) / jnp.sqrt(jnp.float32(head_dim))
    probs = jax.nn.softmax(scores, axis=-1).astype(jnp.bfloat16)
    attended = jnp.einsum(
        "shqk,skhd->sqhd", probs, value, preferred_element_type=jnp.float32
    ).astype(jnp.bfloat16)
    attended = attended.reshape(images * L, local_heads * head_dim)
    all_heads = lax.all_gather(attended, "col", axis=1, tiled=True)
    result = add_rows(all_heads, lax.all_gather(w_out, "row", axis=0, tiled=True))
    return result.astype(jnp.bfloat16)


def solution(mesh):
    in_specs = (
        P(("row", "col"), None),
        P("row", None),
        P("row", None),
        P("col"),
        P(None, "col"),
        P("col"),
        P("row", "col"),
        P("row", "col"),
        P("row", "col"),
        P("row", "col"),
    )
    out_specs = P("row", "col")
    return jax.shard_map(
        on_device, mesh=mesh, in_specs=in_specs, out_specs=out_specs, check_vma=False
    )
```

profile of v0, /device:TPU:0, one launch (start us, length us, event | category | flops | bytes accessed | tf_op | source)
XLA Modules:
  0.0 588.5 jit_solution(18114408391825959600)
XLA Ops:
  6.5 2.0 copy.41
  8.6 6.3 %all-to-all-start = ((bf16[64,4,1024]{2,0,1:T(8,128)(2,1)}), bf16[64,4,1024]{2,0,1:T(8,128)(2,1)S(1)}, u32[]{:S(2)}, u32[]{:S(2)}) async-start(bf16[64,4,1024]{2,0,1:T(8,128)(2,1)} %bitcast.51), calls=%async_computation | async-start | bytes 1048576 | tf_op jit(solution)/shard_map/all_to_all | solution.py:20
  17.0 5.3 gather_fusion
  22.5 6.9 %all-to-all-done = bf16[64,4,1024]{2,0,1:T(8,128)(2,1)S(1)} async-done(((bf16[64,4,1024]{2,0,1:T(8,128)(2,1)}), bf16[64,4,1024]{2,0,1:T(8,128)(2,1)S(1)}, u32[]{:S(2)}, u32[]{:S(2)}) %all-to-all-start) | async-done | bytes 524320 | tf_op jit(solution)/shard_map/all_to_all | solution.py:20
  29.4 3.3 convert_reduce_fusion
  32.7 10.0 %all-reduce = (f32[1024]{0:T(1024)S(1)}, f32[1024]{0:T(1024)S(1)}) all-reduce(f32[1024]{0:T(1024)S(1)} %bitcast.59, f32[1024]{0:T(1024)S(1)} %bitcast.60), channel_id=1, replica_groups=mesh['row'=8,'col'=4] {'col'}, use_global_device_ids=true, to_apply=%region_4.5 | all-reduce | flops 2048 | bytes 16384 | tf_op jit(solution)/shard_map/psum | solution.py:32
  42.7 2.0 fusion.6
  47.6 145.1 %all-gather.7.cloned.1.call-done = bf16[1024,4096]{1,0:T(8,128)(2,1)} async-done(((bf16[1024,1024]{1,0:T(8,128)(2,1)}), bf16[1024,4096]{1,0:T(8,128)(2,1)}) %all-gather.7.cloned.1.call-update) | async-done | bytes 8388624 | tf_op jit(solution)/shard_map/all_gather | solution.py:38
  192.7 54.5 %all-gather.11.cloned.1.call-done = bf16[4096,1024]{1,0:T(8,128)(2,1)} async-done(((bf16[512,1024]{1,0:T(8,128)(2,1)}), bf16[4096,1024]{1,0:T(8,128)(2,1)}) %all-gather.11.cloned.1.call-update) | async-done | bytes 8388624 | tf_op jit(solution)/shard_map/all_gather | solution.py:43
  247.2 13.7 %convert_bitcast_fusion.2 = bf16[128,8,8,128]{3,1,2,0:T(8,128)(2,1)S(1)} fusion(bf16[1024,4096]{1,0:T(8,128)(2,1)} %all-gather.7.cloned.1.call-done, bf16[4096,1024]{1,0:T(8,128)(2,1)} %all-gather.11.cloned.1.call-done), kind=kOutput, calls=%fused_computation.22 | convolution fusion | flops 8590983168 | bytes 18874368 | tf_op jit(solution)/shard_map/dot_general | solution.py:16
  261.5 42.0 %all-gather.13.cloned.1.call-done = bf16[4096,1024]{1,0:T(8,128)(2,1)} async-done(((bf16[512,1024]{1,0:T(8,128)(2,1)}), bf16[4096,1024]{1,0:T(8,128)(2,1)}) %all-gather.13.cloned.1.call-update) | async-done | bytes 8388624 | tf_op jit(solution)/shard_map/all_gather | solution.py:44
  303.5 13.7 %convert_bitcast_fusion.1 = bf16[128,8,8,128]{3,1,2,0:T(8,128)(2,1)S(1)} fusion(bf16[1024,4096]{1,0:T(8,128)(2,1)} %all-gather.7.cloned.1.call-done, bf16[4096,1024]{1,0:T(8,128)(2,1)} %all-gather.13.cloned.1.call-done), kind=kOutput, calls=%fused_computation.21 | convolution fusion | flops 8590983168 | bytes 18874368 | tf_op jit(solution)/shard_map/dot_general | solution.py:16
  317.2 1.9 copy.28
  319.1 40.5 %all-gather.9.cloned.1.call-done = bf16[4096,1024]{1,0:T(8,128)(2,1)} async-done(((bf16[512,1024]{1,0:T(8,128)(2,1)}), bf16[4096,1024]{1,0:T(8,128)(2,1)}) %all-gather.9.cloned.1.call-update) | async-done | bytes 8388624 | tf_op jit(solution)/shard_map/all_gather | solution.py:45
  359.7 13.7 %convert_bitcast_fusion.3 = bf16[128,8,8,128]{3,1,2,0:T(8,128)(2,1)S(1)} fusion(bf16[1024,4096]{1,0:T(8,128)(2,1)} %all-gather.7.cloned.1.call-done, bf16[4096,1024]{1,0:T(8,128)(2,1)} %all-gather.9.cloned.1.call-done), kind=kOutput, calls=%fused_computation.23 | convolution fusion | flops 8590983168 | bytes 18874368 | tf_op jit(solution)/shard_map/dot_general | solution.py:16
  374.0 0.9 copy-done.2
  375.0 1.3 fusion.10
  376.2 6.3 %fusion.20 = (f32[4,8,256]{2,1,0:T(8,128)S(1)}, f32[4,8,256,256]{2,3,1,0:T(8,128)S(1)}) fusion(f32[4,8,256,256]{2,3,1,0:T(8,128)S(1)} %fusion.10), kind=kOutput, calls=%fused_computation.39 | output fusion | flops 8388863 | bytes 16809984 | tf_op jit(solution)/shard_map/sub | solution.py:55
  382.5 2.4 convert_bitcast_fusion
  385.0 3.1 copy.20
  388.1 2.0 copy.40
  390.2 25.7 %all-gather.17.cloned.1.call-done = bf16[4096,1024]{1,0:T(8,128)(2,1)} async-done(((bf16[512,1024]{1,0:T(8,128)(2,1)}), bf16[4096,1024]{1,0:T(8,128)(2,1)}) %all-gather.17.cloned.1.call-update) | async-done | bytes 8388624 | tf_op jit(solution)/shard_map/all_gather | solution.py:61
  415.9 151.1 %all-gather.15.cloned.1.call-done = bf16[1024,4096]{1,0:T(8,128)(2,1)} async-done(((bf16[1024,1024]{1,0:T(8,128)(2,1)}), bf16[1024,4096]{1,0:T(8,128)(2,1)}) %all-gather.15.cloned.1.call-update) | async-done | bytes 8388624 | tf_op jit(solution)/shard_map/all_gather | solution.py:60
  566.9 14.7 %convolution_convert_fusion = bf16[1024,1024]{1,0:T(8,128)(2,1)} fusion(bf16[1024,4096]{1,0:T(8,128)(2,1)} %all-gather.15.cloned.1.call-done, bf16[4096,1024]{1,0:T(8,128)(2,1)} %all-gather.17.cloned.1.call-done), kind=kOutput, calls=%fused_computation.24 | convolution fusion | flops 8590983168 | bytes 18874368 | tf_op jit(solution)/shard_map/dot_general | solution.py:16
  (34 shorter events, 6.3 us)
Async XLA Ops:
  6.5 10.4 %copy-start = (bf16[1024,1024]{1,0:T(8,128)(2,1)S(1)}, bf16[1024,1024]{1,0:T(8,128)(2,1)}, u32[]{:S(2)}) copy-start(bf16[1024,1024]{1,0:T(8,128)(2,1)} %param.14) | copy-start | bytes 6291460
  8.6 20.8 %all-to-all-start = ((bf16[64,4,1024]{2,0,1:T(8,128)(2,1)}), bf16[64,4,1024]{2,0,1:T(8,128)(2,1)S(1)}, u32[]{:S(2)}, u32[]{:S(2)}) async-start(bf16[64,4,1024]{2,0,1:T(8,128)(2,1)} %bitcast.51), calls=%async_computation | async-start | bytes 1048576 | tf_op jit(solution)/shard_map/all_to_all | solution.py:20
  14.9 177.8 %all-gather.7.cloned.1.call-start = ((), (), s32[]{:S(2)}) async-start(), calls=%async_computation.1 | async-start | bytes 10485760 | tf_op jit(solution)/shard_map/all_gather | solution.py:38
  16.9 5.4 copy-start.4
  17.0 5.5 copy-start.3
  44.7 202.5 %all-gather.11.cloned.1.call-start = ((), (), s32[]{:S(2)}) async-start(), calls=%async_computation.3 | async-start | bytes 9437184 | tf_op jit(solution)/shard_map/all_gather | solution.py:43
  45.5 258.1 %all-gather.13.cloned.1.call-start = ((), (), s32[]{:S(2)}) async-start(), calls=%async_computation.4 | async-start | bytes 9437184 | tf_op jit(solution)/shard_map/all_gather | solution.py:44
  46.2 313.5 %all-gather.9.cloned.1.call-start = ((), (), s32[]{:S(2)}) async-start(), calls=%async_computation.2 | async-start | bytes 9437184 | tf_op jit(solution)/shard_map/all_gather | solution.py:45
  46.8 369.1 %all-gather.17.cloned.1.call-start = ((), (), s32[]{:S(2)}) async-start(), calls=%async_computation.6 | async-start | bytes 9437184 | tf_op jit(solution)/shard_map/all_gather | solution.py:61
  47.4 519.6 %all-gather.15.cloned.1.call-start = ((), (), s32[]{:S(2)}) async-start(), calls=%async_computation.5 | async-start | bytes 10485760 | tf_op jit(solution)/shard_map/all_gather | solution.py:60
  373.4 1.6 copy-start.2
  566.9 14.8 %copy-start.1 = (bf16[1024,1024]{1,0:T(8,128)(2,1)S(1)}, bf16[1024,1024]{1,0:T(8,128)(2,1)}, u32[]{:S(2)}) copy-start(bf16[1024,1024]{1,0:T(8,128)(2,1)} %param.14) | copy-start | bytes 6291460
Sparse Core Ops, SparseCore 0:
  44.8 147.8 all-gather.6
  194.6 52.5 all-gather.10
  249.1 54.3 all-gather.12
  305.3 54.3 all-gather.8
  361.4 54.3 all-gather.16
  417.3 149.6 all-gather.14
where the time goes:
time: 589 us
  waiting for transfers between devices  468 us (79%)
  matrix products  62.7 us (11%)
  local copies, waits for them, and re-layouts  16.7 us (3%)
  between operations  13.6 us (2%)
  other arithmetic  10.5 us (2%)
  blocking collectives  9.98 us (2%)
  starting transfers between devices  6.69 us (1%)
    all_gather x1, waiting for transfers between devices, on_device(): all_heads = lax.all_gather(attended, 'col', axis=1, tiled=True)  151 us
    all_gather x1, waiting for transfers between devices, on_device(): normed = lax.all_gather(local, 'col', axis=1, tiled=True)  145 us
    dot_general x4, matrix products, add_rows(): return jnp.dot(left, piece, preferred_element_type=jnp.float32)  55.7 us
    all_gather x1, waiting for transfers between devices, on_device(): query = add_one(lax.all_gather(w_query, 'row', axis=0, tiled=True))  54.5 us
    all_gather x1, waiting for transfers between devices, on_device(): key = add_one(lax.all_gather(w_key, 'row', axis=0, tiled=True))  42 us
    all_gather x1, waiting for transfers between devices, on_device(): value = add_one(lax.all_gather(w_value, 'row', axis=0, tiled=True))  40.5 us
    all_gather x1, waiting for transfers between devices, on_device(): lax.all_gather(w_out, 'row', axis=0, tiled=True)  25.7 us
  transfers between devices with their start and end apart: 7, of which 7 were waited for; matrix products, arithmetic and copies ran while one was open for 11% of the time, Pallas kernels for 0%

commit v1 on v0

v1 whole, which is shorter than its diff:
```python
import functools

import jax
import jax.numpy as jnp
import numpy as np
from jax import lax
from jax.experimental import pallas as pl
from jax.experimental.pallas import tpu as pltpu
from jax.sharding import PartitionSpec as P

L = 256
HEAD_DIM = 128
EPS = 1e-05
BF = jnp.bfloat16
F32 = jnp.float32
MIB = 1 << 20


def after(x, *deps):
    return lax.optimization_barrier((x,) + deps)[0]


def row_offsets(rows):
    if rows == 8:
        even, odd = [0, 2, 4, 6, 1, 5, 3, 7], [0, 4, 2, 6, 1, 3, 5, 7]
        return [odd if r % 2 else even for r in range(rows)]
    return [list(range(rows)) for _ in range(rows)]


def row_slots(rows):
    slots = np.zeros((rows, rows), np.int32)
    for r, offsets in enumerate(row_offsets(rows)):
        for place, offset in enumerate(offsets):
            slots[r, r ^ offset] = place
    return slots


def swap(x, pairs):
    return lax.ppermute(x, "row", pairs)


def row_gather(x, rows):
    if rows == 8:
        first = [(r, r ^ (4 if r % 2 else 2)) for r in range(rows)]
        second = [(r, r ^ (2 if r % 2 else 4)) for r in range(rows)]
        sibling = [(r, r ^ 1) for r in range(rows)]
        a = swap(x, first)
        b = swap(x, second)
        c = swap(a, second)
        near = [x, a, b, c]
        return near + [swap(t, sibling) for t in near]
    blocks, bit = [x], 1
    while bit < rows:
        pairs = [(r, r ^ bit) for r in range(rows)]
        blocks = blocks + [swap(t, pairs) for t in blocks]
        bit *= 2
    return blocks


def shift(x, cols, step):
    return lax.ppermute(x, "col", [(c, (c + step) % cols) for c in range(cols)])


def col_gather(x, cols):
    blocks = [x] + [None] * (cols - 1)
    for k in range(1, cols // 2 + 1):
        blocks[k] = shift(blocks[k - 1], cols, 1)
    for k in range(cols - 1, cols // 2, -1):
        blocks[k] = shift(blocks[(k + 1) % cols], cols, -1)
    return blocks


def norm_kernel(
    rows, cols, slot_ref, col_ref, ids_ref, keep_ref, own_ref, *refs
):
    images = 4
    del images
    n_piece = (cols - 1) * rows
    pieces = refs[:n_piece]
    encs = refs[n_piece : n_piece + cols]
    gms = refs[n_piece + cols : n_piece + 2 * cols]
    out_ref, table, extra, held = refs[n_piece + 2 * cols :]
    image = pl.program_id(0)
    positions, width = own_ref.shape
    part = positions // rows
    vis = encs[0].shape[0]
    block = out_ref.shape[2]
    per = width // block

    @pl.when(image == 0)
    def _():
        me = col_ref[0]
        for b in range(rows):
            start = pl.multiple_of(slot_ref[b] * part, part)
            table[me, pl.ds(start, part), :] = own_ref[b * part : (b + 1) * part, :]
        for k in range(1, cols):
            source = col_ref[k]
            for p in range(rows):
                table[source, p * part : (p + 1) * part, :] = pieces[(k - 1) * rows + p][...]
        for k in range(cols):
            extra[col_ref[k]] = gms[k][...]
            for z in range(cols):
                low = positions + k * vis
                table[z, low : low + vis, :] = encs[k][:, z * width : (z + 1) * width]

    ids = ids_ref[...]
    wide = lax.broadcasted_iota(jnp.int32, (L, positions), 1)
    place = jnp.where(wide == ids, 1.0, 0.0).astype(BF)
    here = lax.broadcasted_iota(jnp.int32, (L, cols * vis), 0) + image * L
    seen = jnp.where(here == keep_ref[...], 1.0, 0.0)
    hidden = 1.0 - jnp.max(seen, axis=1, keepdims=True)
    pick = jnp.concatenate([place, seen.astype(BF)], axis=1)
    total = jnp.zeros((L, 1), F32)
    squares = jnp.zeros((L, 1), F32)
    for z in range(cols):
        x = jnp.dot(pick, table[z], preferred_element_type=F32)
        x = x + hidden * extra[z, 1:2, :].astype(F32)
        xb = x.astype(BF)
        held[z] = xb
        x = xb.astype(F32)
        total = total + jnp.sum(x, axis=1, keepdims=True)
        squares = squares + jnp.sum(x * x, axis=1, keepdims=True)
    mean = total / (cols * width)
    var = squares / (cols * width) - mean * mean
    scale = lax.rsqrt(var + EPS)
    for z in range(cols):
        x = held[z].astype(F32)
        y = ((x - mean) * scale * extra[z, 0:1, :].astype(F32)).astype(BF)
        for h in range(per):
            out_ref[slot_ref[z * per + h]] = y[:, h * block : (h + 1) * block]


def fill_and_norm(rows, cols, images, slot, order, ids, keep, own, pieces, encs, gms):
    positions, width = own.shape
    block = width * cols // rows
    vis = encs[0].shape[0]
    whole = lambda a: pl.BlockSpec(a.shape, lambda i, *_: (0,) * a.ndim)
    operands = [ids, keep, own] + pieces + encs + gms
    specs = [pl.BlockSpec((L, 1), lambda i, *_: (i, 0))] + [whole(a) for a in operands[1:]]
    return pl.pallas_call(
        functools.partial(norm_kernel, rows, cols),
        out_shape=jax.ShapeDtypeStruct((rows, images * L, block), BF),
        grid_spec=pltpu.PrefetchScalarGridSpec(
            num_scalar_prefetch=2,
            grid=(images,),
            in_specs=specs,
            out_specs=pl.BlockSpec((rows, L, block), lambda i, *_: (0, i, 0)),
            scratch_shapes=[
                pltpu.VMEM((cols, positions + cols * vis, width), BF),
                pltpu.VMEM((cols,) + gms[0].shape, BF),
                pltpu.VMEM((cols, L, width), BF),
            ],
        ),
        compiler_params=pltpu.CompilerParams(vmem_limit_bytes=60 * MIB),
        cost_estimate=pl.CostEstimate(
            flops=2 * images * L * (positions + cols * vis) * width * cols,
            bytes_accessed=24 * MIB,
            transcendentals=0,
        ),
        name="fill_norm",
    )(slot, order, *operands)


def heads_kernel(rows, heads, x_ref, *refs):
    weights, out_ref = refs[:rows], refs[rows]
    acc = None
    for p in range(rows):
        term = jnp.dot(x_ref[p], weights[p][...], preferred_element_type=F32)
        acc = term if acc is None else acc + term
    acc = acc.astype(BF)
    hw = heads * HEAD_DIM
    scale = HEAD_DIM**-0.5
    for h in range(heads):
        cut = lambda j: acc[:, j * hw + h * HEAD_DIM : j * hw + (h + 1) * HEAD_DIM]
        s = lax.dot_general(
            cut(0), cut(1), (((1,), (1,)), ((), ())), preferred_element_type=F32
        ) * scale
        e = jnp.exp(s - jnp.max(s, axis=1, keepdims=True))
        p = (e / jnp.sum(e, axis=1, keepdims=True)).astype(BF)
        o = jnp.dot(p, cut(2), preferred_element_type=F32)
        out_ref[:, h * HEAD_DIM : (h + 1) * HEAD_DIM] = o.astype(BF)


def some_heads(normed, weights, heads):
    rows, tokens, block = normed.shape
    hw = heads * HEAD_DIM
    return pl.pallas_call(
        functools.partial(heads_kernel, rows, heads),
        out_shape=jax.ShapeDtypeStruct((tokens, hw), BF),
        grid=(tokens // L,),
        in_specs=[pl.BlockSpec((rows, L, block), lambda i: (0, i, 0))]
        + [pl.BlockSpec(w.shape, lambda i: (0, 0)) for w in weights],
        out_specs=pl.BlockSpec((L, hw), lambda i: (i, 0)),
        compiler_params=pltpu.CompilerParams(vmem_limit_bytes=48 * MIB),
        cost_estimate=pl.CostEstimate(
            flops=2 * tokens * rows * block * 3 * hw + 4 * tokens * L * hw,
            bytes_accessed=2 * tokens * rows * block + 6 * rows * block * hw + 2 * tokens * hw,
            transcendentals=tokens * L * heads,
        ),
        name=f"heads_{heads}",
    )(normed, *weights)


def out_kernel(n, has_acc, at_ref, *refs):
    xs, ws = refs[:n], refs[n : 2 * n]
    out_ref = refs[-1]
    acc = refs[2 * n][...] if has_acc else None
    for x_ref, w_ref in zip(xs, ws):
        term = jnp.dot(x_ref[...], w_ref[0], preferred_element_type=F32)
        acc = term if acc is None else acc + term
    out_ref[...] = acc.astype(out_ref.dtype)


def project(at, xs, stacked, inner, acc, last):
    n = len(xs)
    tokens, depth = xs[0].shape
    width = stacked.shape[2]
    row = lambda i, *_: (i, 0)
    specs = [pl.BlockSpec((L, depth), row)] * n
    for k in range(n):
        specs.append(
            pl.BlockSpec((1, depth, width), lambda i, at, k=k: (at[k], inner // depth, 0))
        )
    operands = list(xs) + [stacked] * n
    alias = {}
    if acc is not None:
        specs.append(pl.BlockSpec((L, width), row))
        operands.append(acc)
        if not last:
            alias = {1 + 2 * n: 0}
    return pl.pallas_call(
        functools.partial(out_kernel, n, acc is not None),
        out_shape=jax.ShapeDtypeStruct((tokens, width), BF if last else F32),
        grid_spec=pltpu.PrefetchScalarGridSpec(
            num_scalar_prefetch=1,
            grid=(tokens // L,),
            in_specs=specs,
            out_specs=pl.BlockSpec((L, width), row),
        ),
        input_output_aliases=alias,
        compiler_params=pltpu.CompilerParams(vmem_limit_bytes=32 * MIB),
        cost_estimate=pl.CostEstimate(
            flops=2 * tokens * depth * n * width,
            bytes_accessed=2 * n * depth * (tokens + width) + 8 * tokens * width,
            transcendentals=0,
        ),
        name="out_proj",
    )(at, *operands)


def head_chunks(heads):
    chunks, low = [], 0
    for size in [1, 1] + [2] * heads:
        if low >= heads:
            break
        size = min(size, heads - low)
        chunks.append((low, size))
        low += size
    return chunks


def on_device(
    rows, cols, enc_out, keep, pos_ids, mask_token, pos_table, gain, w_query, w_key, w_value, w_out
):
    images = keep.shape[0]
    positions, width = pos_table.shape
    r, c = lax.axis_index("row"), lax.axis_index("col")
    slot = jnp.asarray(row_slots(rows))[r]
    order = (c - jnp.arange(cols, dtype=jnp.int32)) % cols
    chunks = head_chunks(width // HEAD_DIM)

    def packed(low, size):
        cut = slice(low * HEAD_DIM, (low + size) * HEAD_DIM)
        return jnp.concatenate([w_query[:, cut], w_key[:, cut], w_value[:, cut]], axis=1)

    part = positions // rows
    share = lax.dynamic_slice_in_dim(pos_table, r * part, part, axis=0)
    pad = jnp.zeros((14, width), BF)
    share = jnp.concatenate([share, gain[None], mask_token[None], pad], axis=0)
    shares = col_gather(share, cols)
    gms = [s[part : part + 16] for s in shares]

    enc = after(enc_out, shares[1], shares[cols - 1])
    encs = col_gather(enc, cols)

    gathered = []
    gathered.append(row_gather(packed(*chunks[0]), rows))
    pieces = []
    for k in range(1, cols):
        pieces.append(row_gather(shares[k][:part], rows))
    prev = [gathered[0][3], pieces[-1][3]]
    for low, size in chunks[1:]:
        w = after(packed(low, size), prev[-2])
        gathered.append(row_gather(w, rows))
        prev.append(gathered[-1][3])
    w_outs = row_gather(after(w_out, prev[-2]), rows)
    stacked = jnp.stack(w_outs)

    ids = (slot[pos_ids // part] * part + pos_ids % part).reshape(images * L, 1)
    numbers = keep + L * jnp.arange(images, dtype=jnp.int32)[:, None]
    numbers = numbers.reshape(cols, -1)[order].reshape(1, -1)

    normed = fill_and_norm(
        rows, cols, images, slot, order, ids, numbers, pos_table,
        [p for piece in pieces for p in piece], encs, gms,
    )

    acc = None
    block = w_out.shape[0]
    for (low, size), weights in zip(chunks, gathered):
        attended = some_heads(normed, weights, size)
        xs = col_gather(attended, cols)
        first = low * HEAD_DIM
        at = slot[(order * width + first) // block]
        last = (low, size) == chunks[-1]
        acc = project(at, xs, stacked, first % block, acc, last)
    return acc


def solution(mesh):
    rows, cols = mesh.shape["row"], mesh.shape["col"]
    in_specs = (
        P(("row", "col"), None),
        P("row", None),
        P("row", None),
        P("col"),
        P(None, "col"),
        P("col"),
        P("row", "col"),
        P("row", "col"),
        P("row", "col"),
        P("row", "col"),
    )
    return jax.shard_map(
        functools.partial(on_device, rows, cols),
        mesh=mesh,
        in_specs=in_specs,
        out_specs=P("row", "col"),
        check_vma=False,
    )
```

time: 589 us -> 376 us (0.64)
  waiting for transfers between devices: 468 us -> 135 us
  Pallas kernels: 0 us -> 100 us
  starting transfers between devices: 6.69 us -> 80.7 us
  matrix products: 62.7 us -> 0 us
  local copies, waits for them, and re-layouts: 16.7 us -> 50.9 us
  between operations: 13.6 us -> 0.71 us
  blocking collectives: 9.98 us -> 0 us
    all_gather x6 -> x0, waiting for transfers between devices: 459 us -> none  [the longest x1 151 us: on_device(): all_heads = lax.all_gather(attended, 'col', axis=1, tiled=True)]
    ppermute x0 -> x84, waiting for transfers between devices: none -> 135 us  [the longest x21 108 us: shift(): return lax.ppermute(x, 'col', [(c, (c + step) % cols) for c in range(cols)])]
    pallas_call x0 -> x11, Pallas kernels: none -> 100 us  [the longest x5 58.5 us: some_heads(): pl.pallas_call(functools.partial(heads_kernel, rows, heads), out_shape=ja...]
    ppermute x0 -> x84, starting transfers between devices: none -> 80.7 us  [the longest x21 41.7 us: shift(): return lax.ppermute(x, 'col', [(c, (c + step) % cols) for c in range(cols)])]
    dot_general x7 -> x0, matrix products: 62.7 us -> none  [the longest x4 55.7 us: add_rows(): return jnp.dot(left, piece, preferred_element_type=jnp.float32)]
    unnamed x17 -> x110, local copies, waits for them, and re-layouts: 6.21 us -> 25.1 us
    slice x0 -> x10, local copies, waits for them, and re-layouts: none -> 11.7 us  [the longest x3 4.11 us: on_device(): gms = [s[part:part + 16] for s in shares]]
    psum x1 -> x0, blocking collectives: 9.98 us -> none  [on_device(): lax.psum((jnp.sum(values, axis=1), jnp.sum(values * values, axis=1)), 'col')]
  transfers between devices with their start and end apart: 7 -> 84, of which waited for: 7 -> 22; matrix products, arithmetic and copies ran while one was open for 11% -> 11% of each run, Pallas kernels for 0% -> 26%
where the time goes in v1:
time: 376 us; the launch traced here: 375 us
  waiting for transfers between devices  135 us (36%)
  Pallas kernels  100 us (27%)
  starting transfers between devices  80.7 us (21%)
  local copies, waits for them, and re-layouts  50.9 us (14%)
  other arithmetic  6.53 us (2%)
    ppermute x21, waiting for transfers between devices, shift(): return lax.ppermute(x, 'col', [(c, (c + step) % cols) for c in range(cols)])  108 us
    pallas_call x5, Pallas kernels, some_heads(): pl.pallas_call(functools.partial(heads_kernel, rows, heads), out_shape=ja...  58.5 us
    ppermute x21, starting transfers between devices, shift(): return lax.ppermute(x, 'col', [(c, (c + step) % cols) for c in range(cols)])  41.7 us
    ppermute x63, starting transfers between devices, swap(): return lax.ppermute(x, 'row', pairs)  39 us
    ppermute x63, waiting for transfers between devices, swap(): return lax.ppermute(x, 'row', pairs)  27.7 us
    unnamed x110, local copies, waits for them, and re-layouts  25.1 us
    pallas_call x1, Pallas kernels, fill_and_norm(): pl.pallas_call(functools.partial(norm_kernel, rows, cols), out_shape=jax....  24.1 us
    pallas_call x5, Pallas kernels, project(): pl.pallas_call(functools.partial(out_kernel, n, acc is not None), out_sha...  17.9 us
  transfers between devices with their start and end apart: 84, of which 22 were waited for; matrix products, arithmetic and copies ran while one was open for 11% of the time, Pallas kernels for 26%

profile of v1, /device:TPU:0, one launch (start us, length us, event | category | flops | bytes accessed | tf_op | source)
XLA Modules:
  0.0 374.7 jit_solution(17683940314867339982)
XLA Ops:
  13.0 7.3 %collective-permute-done.16 = bf16[144,1024]{1,0:T(8,128)(2,1)S(1)} collective-permute-done((bf16[144,1024]{1,0:T(8,128)(2,1)S(1)}, bf16[144,1024]{1,0:T(8,128)(2,1)S(1)}, u32[]{:S(2)}, u32[]{:S(2)}) %collective-permute-start.16) | collective-permute-done | bytes 294944 | tf_op jit(solution)/shard_map/ppermute | solution.py:61
  28.0 5.6 %collective-permute-done.1.refs_1_ = bf16[128,1024]{1,0:T(8,128)(2,1)S(1)} collective-permute-done((bf16[128,1024]{1,0:T(8,128)(2,1)S(1)}, bf16[128,1024]{1,0:T(8,128)(2,1)S(1)}, u32[]{:S(2)}, u32[]{:S(2)}) %collective-permute-start.1) | collective-permute-done | bytes 262176 | tf_op jit(solution)/shard_map/ppermute | solution.py:39
  42.6 6.6 %gather_fusion.1 = s32[1024]{0:T(1024)S(1)} fusion(s32[8]{0:T(128)S(1)} %dynamic-slice_bitcast_fusion.slot_ref, s32[1024]{0:T(1024)S(1)} %broadcast_clamp_fusion), kind=kCustom, calls=%fused_computation.1 | custom fusion | bytes 12288 | tf_op jit(solution)/shard_map/gather | solution.py:299
  53.9 8.9 %collective-permute-done.26.refs_27_ = bf16[64,4096]{1,0:T(8,128)(2,1)} collective-permute-done((bf16[64,4096]{1,0:T(8,128)(2,1)}, bf16[64,4096]{1,0:T(8,128)(2,1)}, u32[]{:S(2)}, u32[]{:S(2)}) %collective-permute-start.26) | collective-permute-done | bytes 524320 | tf_op jit(solution)/shard_map/ppermute | solution.py:61
  70.2 5.2 %collective-permute-done.9.refs_9_ = bf16[128,1024]{1,0:T(8,128)(2,1)} collective-permute-done((bf16[128,1024]{1,0:T(8,128)(2,1)S(1)}, bf16[128,1024]{1,0:T(8,128)(2,1)}, u32[]{:S(2)}, u32[]{:S(2)}) %collective-permute-start.9) | collective-permute-done | bytes 262176 | tf_op jit(solution)/shard_map/ppermute | solution.py:39
  100.2 24.1 %fill_norm.1.x_ref = bf16[8,1024,512]{2,1,0:T(8,128)(2,1)} custom-call(s32[8]{0:T(128)} %copy-done.30, s32[4]{0:T(128)} %and_select_fusion.4.col_ref, s32[1024,1]{1,0:T(8,128)} %bitcast.38, s32[1,256]{1,0:T(1,128)} %reshape.351.keep_ref, bf16[1024,1024]{1,0:T(8,128)(2,1)} %own_ref.1, bf16[128,1024]{1,0:T(8,128)(2,1)} %copy-done.36, ...), custom_call_target="tpu_custom_call" | custom-call | flops 10737418240 | bytes 25165824 | tf_op jit(solution)/shard_map/fill_norm/pallas_call | solution.py:140
  130.6 8.6 %heads_1.3.refs_0_ = bf16[1024,128]{1,0:T(8,128)(2,1)S(1)} custom-call(bf16[8,1024,512]{2,1,0:T(8,128)(2,1)} %fill_norm.1.x_ref, bf16[512,384]{1,0:T(8,128)(2,1)S(1)} %pad_maximum_fusion.4.refs_0_, bf16[512,384]{1,0:T(8,128)(2,1)S(1)} %collective-permute-done.39.refs_1_, bf16[512,384]{1,0:T(8,128)(2,1)S(1)} %collective-permute-done.76.refs_2_, ...), custom_call_target="tpu_custom_call" | custom-call | flops 3355443200 | bytes 11796480 | tf_op jit(solution)/shard_map/heads_1/pallas_call | solution.py:187
  143.3 7.2 %collective-permute-done.81.refs_1_ = bf16[1024,128]{1,0:T(8,128)(2,1)S(1)} collective-permute-done((bf16[1024,128]{1,0:T(8,128)(2,1)S(1)}, bf16[1024,128]{1,0:T(8,128)(2,1)S(1)}, u32[]{:S(2)}, u32[]{:S(2)}) %collective-permute-start.81) | collective-permute-done | bytes 262176 | tf_op jit(solution)/shard_map/ppermute | solution.py:61
  158.0 4.6 %collective-permute-done.52.refs_2_ = bf16[512,768]{1,0:T(8,128)(2,1)} collective-permute-done((bf16[512,768]{1,0:T(8,128)(2,1)S(1)}, bf16[512,768]{1,0:T(8,128)(2,1)}, u32[]{:S(2)}, u32[]{:S(2)}) %collective-permute-start.52) | collective-permute-done | bytes 786464 | tf_op jit(solution)/shard_map/ppermute | solution.py:39
  168.7 5.4 %collective-permute-done.44.refs_3_ = bf16[512,768]{1,0:T(8,128)(2,1)} collective-permute-done((bf16[512,768]{1,0:T(8,128)(2,1)}, bf16[512,768]{1,0:T(8,128)(2,1)}, u32[]{:S(2)}, u32[]{:S(2)}) %collective-permute-start.44) | collective-permute-done | bytes 786464 | tf_op jit(solution)/shard_map/ppermute | solution.py:39
  176.4 9.3 %heads_1.2.refs_0_ = bf16[1024,128]{1,0:T(8,128)(2,1)S(1)} custom-call(bf16[8,1024,512]{2,1,0:T(8,128)(2,1)} %fill_norm.1.x_ref, bf16[512,384]{1,0:T(8,128)(2,1)S(1)} %pad_maximum_fusion.3.refs_0_, bf16[512,384]{1,0:T(8,128)(2,1)} %collective-permute-done.41.refs_1_, bf16[512,384]{1,0:T(8,128)(2,1)} %collective-permute-done.68.refs_2_, ...), custom_call_target="tpu_custom_call" | custom-call | flops 3355443200 | bytes 11796480 | tf_op jit(solution)/shard_map/heads_1/pallas_call | solution.py:187
  193.6 13.3 %heads_2.5.refs_0_ = bf16[1024,256]{1,0:T(8,128)(2,1)S(1)} custom-call(bf16[8,1024,512]{2,1,0:T(8,128)(2,1)} %fill_norm.1.x_ref, bf16[512,768]{1,0:T(8,128)(2,1)S(1)} %pad_maximum_fusion.1.refs_0_, bf16[512,768]{1,0:T(8,128)(2,1)} %collective-permute-done.27.refs_1_, bf16[512,768]{1,0:T(8,128)(2,1)} %collective-permute-done.60.refs_2_, ...), custom_call_target="tpu_custom_call" | custom-call | flops 6710886400 | bytes 15204352 | tf_op jit(solution)/shard_map/heads_2/pallas_call | solution.py:187
  208.7 13.6 %heads_2.4.refs_0_ = bf16[1024,256]{1,0:T(8,128)(2,1)S(1)} custom-call(bf16[8,1024,512]{2,1,0:T(8,128)(2,1)} %fill_norm.1.x_ref, bf16[512,768]{1,0:T(8,128)(2,1)S(1)} %pad_maximum_fusion.2.refs_0_, bf16[512,768]{1,0:T(8,128)(2,1)} %collective-permute-done.43.refs_1_, bf16[512,768]{1,0:T(8,128)(2,1)} %collective-permute-done.52.refs_2_, ...), custom_call_target="tpu_custom_call" | custom-call | flops 6710886400 | bytes 15204352 | tf_op jit(solution)/shard_map/heads_2/pallas_call | solution.py:187
  230.8 13.8 %heads_2.3.refs_0_ = bf16[1024,256]{1,0:T(8,128)(2,1)S(1)} custom-call(bf16[8,1024,512]{2,1,0:T(8,128)(2,1)} %fill_norm.1.x_ref, bf16[512,768]{1,0:T(8,128)(2,1)} %pad_maximum_fusion.refs_0_, bf16[512,768]{1,0:T(8,128)(2,1)} %collective-permute-done.29.refs_1_, bf16[512,768]{1,0:T(8,128)(2,1)} %collective-permute-done.30.refs_2_, ...), custom_call_target="tpu_custom_call" | custom-call | flops 6710886400 | bytes 15204352 | tf_op jit(solution)/shard_map/heads_2/pallas_call | solution.py:187
  248.5 6.3 %collective-permute-done.73.refs_1_ = bf16[1024,128]{1,0:T(8,128)(2,1)S(1)} collective-permute-done((bf16[1024,128]{1,0:T(8,128)(2,1)S(1)}, bf16[1024,128]{1,0:T(8,128)(2,1)S(1)}, u32[]{:S(2)}, u32[]{:S(2)}) %collective-permute-start.73) | collective-permute-done | bytes 262176 | tf_op jit(solution)/shard_map/ppermute | solution.py:61
  258.2 5.0 %collective-permute-done.75.refs_3_ = bf16[1024,128]{1,0:T(8,128)(2,1)S(1)} collective-permute-done((bf16[1024,128]{1,0:T(8,128)(2,1)S(1)}, bf16[1024,128]{1,0:T(8,128)(2,1)S(1)}, u32[]{:S(2)}, u32[]{:S(2)}) %collective-permute-start.75) | collective-permute-done | bytes 262176 | tf_op jit(solution)/shard_map/ppermute | solution.py:61
  267.8 14.5 %collective-permute-done.74.refs_2_ = bf16[1024,128]{1,0:T(8,128)(2,1)S(1)} collective-permute-done((bf16[1024,128]{1,0:T(8,128)(2,1)S(1)}, bf16[1024,128]{1,0:T(8,128)(2,1)S(1)}, u32[]{:S(2)}, u32[]{:S(2)}) %collective-permute-start.74) | collective-permute-done | bytes 262176 | tf_op jit(solution)/shard_map/ppermute | solution.py:61
  285.9 7.6 %collective-permute-done.57.refs_1_ = bf16[1024,256]{1,0:T(8,128)(2,1)S(1)} collective-permute-done((bf16[1024,256]{1,0:T(8,128)(2,1)S(1)}, bf16[1024,256]{1,0:T(8,128)(2,1)S(1)}, u32[]{:S(2)}, u32[]{:S(2)}) %collective-permute-start.57) | collective-permute-done | bytes 524320 | tf_op jit(solution)/shard_map/ppermute | solution.py:61
  293.5 10.8 %collective-permute-start.59 = (bf16[1024,256]{1,0:T(8,128)(2,1)S(1)}, bf16[1024,256]{1,0:T(8,128)(2,1)S(1)}, u32[]{:S(2)}, u32[]{:S(2)}) collective-permute-start(bf16[1024,256]{1,0:T(8,128)(2,1)S(1)} %heads_2.4.refs_0_), channel_id=1, source_target_pairs={{0,3},{1,0},{2,1},{3,2},{4,7},{5,4},{6,5},{7,6},{8,11},{9,8},{10,9... | collective-permute-start | bytes 1572872 | tf_op jit(solution)/shard_map/ppermute | solution.py:61
  308.2 19.0 %collective-permute-done.36.refs_1_ = bf16[1024,256]{1,0:T(8,128)(2,1)S(1)} collective-permute-done((bf16[1024,256]{1,0:T(8,128)(2,1)S(1)}, bf16[1024,256]{1,0:T(8,128)(2,1)S(1)}, u32[]{:S(2)}, u32[]{:S(2)}) %collective-permute-start.36) | collective-permute-done | bytes 524320 | tf_op jit(solution)/shard_map/ppermute | solution.py:61
  338.5 11.2 %collective-permute-done.58.refs_2_ = bf16[1024,256]{1,0:T(8,128)(2,1)S(1)} collective-permute-done((bf16[1024,256]{1,0:T(8,128)(2,1)S(1)}, bf16[1024,256]{1,0:T(8,128)(2,1)S(1)}, u32[]{:S(2)}, u32[]{:S(2)}) %collective-permute-start.58) | collective-permute-done | bytes 524320 | tf_op jit(solution)/shard_map/ppermute | solution.py:61
  353.2 7.5 %collective-permute-done.38.refs_3_ = bf16[1024,256]{1,0:T(8,128)(2,1)S(1)} collective-permute-done((bf16[1024,256]{1,0:T(8,128)(2,1)S(1)}, bf16[1024,256]{1,0:T(8,128)(2,1)S(1)}, u32[]{:S(2)}, u32[]{:S(2)}) %collective-permute-start.38) | collective-permute-done | bytes 524320 | tf_op jit(solution)/shard_map/ppermute | solution.py:61
  360.7 9.7 %collective-permute-done.37.refs_2_ = bf16[1024,256]{1,0:T(8,128)(2,1)S(1)} collective-permute-done((bf16[1024,256]{1,0:T(8,128)(2,1)S(1)}, bf16[1024,256]{1,0:T(8,128)(2,1)S(1)}, u32[]{:S(2)}, u32[]{:S(2)}) %collective-permute-start.37) | collective-permute-done | bytes 524320 | tf_op jit(solution)/shard_map/ppermute | solution.py:61
  370.4 4.3 %out_proj.9 = bf16[1024,1024]{1,0:T(8,128)(2,1)} custom-call(s32[4]{0:T(128)S(1)} %gather_fusion, bf16[1024,256]{1,0:T(8,128)(2,1)S(1)} %heads_2.3.refs_0_, bf16[1024,256]{1,0:T(8,128)(2,1)S(1)} %collective-permute-done.36.refs_1_, bf16[1024,256]{1,0:T(8,128)(2,1)S(1)} %collective-permute-done.37.refs_2_, ...), custom_call_target="tpu_custom_call" | custom-call | flops 2147483648 | bytes 12582912 | tf_op jit(solution)/shard_map/out_proj/pallas_call | solution.py:231
  (313 shorter events, 144.8 us)
Async XLA Ops:
  37.2 25.6 %collective-permute-start.26 = (bf16[64,4096]{1,0:T(8,128)(2,1)}, bf16[64,4096]{1,0:T(8,128)(2,1)}, u32[]{:S(2)}, u32[]{:S(2)}) collective-permute-start(bf16[64,4096]{1,0:T(8,128)(2,1)} %refs_24_), channel_id=1, source_target_pairs={{0,3},{1,0},{2,1},{3,2},{4,7},{5,4},{6,5},{7,6},{8,11},{9,8},{10,9... | collective-permute-start | bytes 1572872 | tf_op jit(solution)/shard_map/ppermute | solution.py:61
  96.9 29.0 %collective-permute-start.27 = (bf16[512,768]{1,0:T(8,128)(2,1)S(1)}, bf16[512,768]{1,0:T(8,128)(2,1)}, u32[]{:S(2)}, u32[]{:S(2)}) collective-permute-start(bf16[512,768]{1,0:T(8,128)(2,1)S(1)} %pad_maximum_fusion.1.refs_0_), channel_id=1, source_target_pairs={{0,8},{4,20},{8,0},{12,28},{16,24},{20,4},{24,16},{28,12},{1,9},{5... | collective-permute-start | bytes 2359304 | tf_op jit(solution)/shard_map/ppermute | solution.py:39
  97.5 41.7 %collective-permute-start.60 = (bf16[512,768]{1,0:T(8,128)(2,1)S(1)}, bf16[512,768]{1,0:T(8,128)(2,1)}, u32[]{:S(2)}, u32[]{:S(2)}) collective-permute-start(bf16[512,768]{1,0:T(8,128)(2,1)S(1)} %pad_maximum_fusion.1.refs_0_), channel_id=1, source_target_pairs={{0,16},{4,12},{8,24},{12,4},{16,0},{20,28},{24,8},{28,20},{1,17},{... | collective-permute-start | bytes 2359304 | tf_op jit(solution)/shard_map/ppermute | solution.py:39
  99.5 40.1 %collective-permute-start.61 = (bf16[512,768]{1,0:T(8,128)(2,1)S(1)}, bf16[512,768]{1,0:T(8,128)(2,1)}, u32[]{:S(2)}, u32[]{:S(2)}) collective-permute-start(bf16[512,768]{1,0:T(8,128)(2,1)S(1)} %pad_maximum_fusion.1.refs_0_), channel_id=1, source_target_pairs={{0,4},{4,0},{8,12},{12,8},{16,20},{20,16},{24,28},{28,24},{1,5},{5... | collective-permute-start | bytes 2359304 | tf_op jit(solution)/shard_map/ppermute | solution.py:39
  99.5 24.8 %collective-permute-start.70 = (bf16[512,384]{1,0:T(8,128)(2,1)}, bf16[512,384]{1,0:T(8,128)(2,1)}, u32[]{:S(2)}, u32[]{:S(2)}) collective-permute-start(bf16[512,384]{1,0:T(8,128)(2,1)} %collective-permute-done.41.refs_1_), channel_id=1, source_target_pairs={{0,4},{4,0},{8,12},{12,8},{16,20},{20,16},{24,28},{28,24},{1,5},{5... | collective-permute-start | bytes 1179656 | tf_op jit(solution)/shard_map/ppermute | solution.py:39
  100.0 25.8 %collective-permute-start.71 = (bf16[512,384]{1,0:T(8,128)(2,1)}, bf16[512,384]{1,0:T(8,128)(2,1)}, u32[]{:S(2)}, u32[]{:S(2)}) collective-permute-start(bf16[512,384]{1,0:T(8,128)(2,1)} %collective-permute-done.68.refs_2_), channel_id=1, source_target_pairs={{0,4},{4,0},{8,12},{12,8},{16,20},{20,16},{24,28},{28,24},{1,5},{5... | collective-permute-start | bytes 1179656 | tf_op jit(solution)/shard_map/ppermute | solution.py:39
  124.3 30.4 %collective-permute-start.43 = (bf16[512,768]{1,0:T(8,128)(2,1)S(1)}, bf16[512,768]{1,0:T(8,128)(2,1)}, u32[]{:S(2)}, u32[]{:S(2)}) collective-permute-start(bf16[512,768]{1,0:T(8,128)(2,1)S(1)} %pad_maximum_fusion.2.refs_0_), channel_id=1, source_target_pairs={{0,8},{4,20},{8,0},{12,28},{16,24},{20,4},{24,16},{28,12},{1,9},{5... | collective-permute-start | bytes 2359304 | tf_op jit(solution)/shard_map/ppermute | solution.py:39
  125.8 27.6 %collective-permute-start.72 = (bf16[512,384]{1,0:T(8,128)(2,1)}, bf16[512,384]{1,0:T(8,128)(2,1)S(1)}, u32[]{:S(2)}, u32[]{:S(2)}) collective-permute-start(bf16[512,384]{1,0:T(8,128)(2,1)} %collective-permute-done.42.refs_3_), channel_id=1, source_target_pairs={{0,4},{4,0},{8,12},{12,8},{16,20},{20,16},{24,28},{28,24},{1,5},{5... | collective-permute-start | bytes 1179656 | tf_op jit(solution)/shard_map/ppermute | solution.py:39
  125.9 28.9 %collective-permute-start.28 = (bf16[512,768]{1,0:T(8,128)(2,1)}, bf16[512,768]{1,0:T(8,128)(2,1)S(1)}, u32[]{:S(2)}, u32[]{:S(2)}) collective-permute-start(bf16[512,768]{1,0:T(8,128)(2,1)} %collective-permute-done.27.refs_1_), channel_id=1, source_target_pairs={{0,16},{4,12},{8,24},{12,4},{16,0},{20,28},{24,8},{28,20},{1,17},{... | collective-permute-start | bytes 2359304 | tf_op jit(solution)/shard_map/ppermute | solution.py:39
  189.0 33.3 %collective-permute-start.45 = (bf16[512,1024]{1,0:T(8,128)(2,1)}, bf16[512,1024]{1,0:T(8,128)(2,1)}, u32[]{:S(2)}, u32[]{:S(2)}) collective-permute-start(bf16[512,1024]{1,0:T(8,128)(2,1)} %param.20), channel_id=1, source_target_pairs={{0,8},{4,20},{8,0},{12,28},{16,24},{20,4},{24,16},{28,12},{1,9},{5... | collective-permute-start | bytes 3145736 | tf_op jit(solution)/shard_map/ppermute | solution.py:39
  189.6 34.4 %collective-permute-start.46 = (bf16[512,1024]{1,0:T(8,128)(2,1)}, bf16[512,1024]{1,0:T(8,128)(2,1)}, u32[]{:S(2)}, u32[]{:S(2)}) collective-permute-start(bf16[512,1024]{1,0:T(8,128)(2,1)} %param.20), channel_id=1, source_target_pairs={{0,16},{4,12},{8,24},{12,4},{16,0},{20,28},{24,8},{28,20},{1,17},{... | collective-permute-start | bytes 3145736 | tf_op jit(solution)/shard_map/ppermute | solution.py:39
  222.3 24.9 %collective-permute-start.47 = (bf16[512,1024]{1,0:T(8,128)(2,1)}, bf16[512,1024]{1,0:T(8,128)(2,1)}, u32[]{:S(2)}, u32[]{:S(2)}) collective-permute-start(bf16[512,1024]{1,0:T(8,128)(2,1)} %collective-permute-done.45), channel_id=1, source_target_pairs={{0,16},{4,12},{8,24},{12,4},{16,0},{20,28},{24,8},{28,20},{1,17},{... | collective-permute-start | bytes 3145736 | tf_op jit(solution)/shard_map/ppermute | solution.py:39
  224.0 32.4 %collective-permute-start.48 = (bf16[512,1024]{1,0:T(8,128)(2,1)}, bf16[512,1024]{1,0:T(8,128)(2,1)}, u32[]{:S(2)}, u32[]{:S(2)}) collective-permute-start(bf16[512,1024]{1,0:T(8,128)(2,1)} %param.20), channel_id=1, source_target_pairs={{0,4},{4,0},{8,12},{12,8},{16,20},{20,16},{24,28},{28,24},{1,5},{5... | collective-permute-start | bytes 3145736 | tf_op jit(solution)/shard_map/ppermute | solution.py:39
  229.2 34.4 %collective-permute-start.49 = (bf16[512,1024]{1,0:T(8,128)(2,1)}, bf16[512,1024]{1,0:T(8,128)(2,1)}, u32[]{:S(2)}, u32[]{:S(2)}) collective-permute-start(bf16[512,1024]{1,0:T(8,128)(2,1)} %collective-permute-done.45), channel_id=1, source_target_pairs={{0,4},{4,0},{8,12},{12,8},{16,20},{20,16},{24,28},{28,24},{1,5},{5... | collective-permute-start | bytes 3145736 | tf_op jit(solution)/shard_map/ppermute | solution.py:39
  229.3 55.1 %collective-permute-start.50 = (bf16[512,1024]{1,0:T(8,128)(2,1)}, bf16[512,1024]{1,0:T(8,128)(2,1)}, u32[]{:S(2)}, u32[]{:S(2)}) collective-permute-start(bf16[512,1024]{1,0:T(8,128)(2,1)} %collective-permute-done.46), channel_id=1, source_target_pairs={{0,4},{4,0},{8,12},{12,8},{16,20},{20,16},{24,28},{28,24},{1,5},{5... | collective-permute-start | bytes 3145736 | tf_op jit(solution)/shard_map/ppermute | solution.py:39
  247.2 57.0 %collective-permute-start.51 = (bf16[512,1024]{1,0:T(8,128)(2,1)}, bf16[512,1024]{1,0:T(8,128)(2,1)S(1)}, u32[]{:S(2)}, u32[]{:S(2)}) collective-permute-start(bf16[512,1024]{1,0:T(8,128)(2,1)} %collective-permute-done.47), channel_id=1, source_target_pairs={{0,4},{4,0},{8,12},{12,8},{16,20},{20,16},{24,28},{28,24},{1,5},{5... | collective-permute-start | bytes 3145736 | tf_op jit(solution)/shard_map/ppermute | solution.py:39
  256.4 26.6 %collective-permute-start.65 = (bf16[1024,256]{1,0:T(8,128)(2,1)S(1)}, bf16[1024,256]{1,0:T(8,128)(2,1)S(1)}, u32[]{:S(2)}, u32[]{:S(2)}) collective-permute-start(bf16[1024,256]{1,0:T(8,128)(2,1)S(1)} %heads_2.5.refs_0_), channel_id=1, source_target_pairs={{0,1},{1,2},{2,3},{3,0},{4,5},{5,6},{6,7},{7,4},{8,9},{9,10},{10,1... | collective-permute-start | bytes 1572872 | tf_op jit(solution)/shard_map/ppermute | solution.py:61
  263.5 29.9 %collective-permute-start.57 = (bf16[1024,256]{1,0:T(8,128)(2,1)S(1)}, bf16[1024,256]{1,0:T(8,128)(2,1)S(1)}, u32[]{:S(2)}, u32[]{:S(2)}) collective-permute-start(bf16[1024,256]{1,0:T(8,128)(2,1)S(1)} %heads_2.4.refs_0_), channel_id=1, source_target_pairs={{0,1},{1,2},{2,3},{3,0},{4,5},{5,6},{6,7},{7,4},{8,9},{9,10},{10,1... | collective-permute-start | bytes 1572872 | tf_op jit(solution)/shard_map/ppermute | solution.py:61
  283.1 51.1 %collective-permute-start.66 = (bf16[1024,256]{1,0:T(8,128)(2,1)S(1)}, bf16[1024,256]{1,0:T(8,128)(2,1)S(1)}, u32[]{:S(2)}, u32[]{:S(2)}) collective-permute-start(bf16[1024,256]{1,0:T(8,128)(2,1)S(1)} %collective-permute-done.65.refs_1_), channel_id=1, source_target_pairs={{0,1},{1,2},{2,3},{3,0},{4,5},{5,6},{6,7},{7,4},{8,9},{9,10},{10,1... | collective-permute-start | bytes 1572872 | tf_op jit(solution)/shard_map/ppermute | solution.py:61
  284.3 42.9 %collective-permute-start.36 = (bf16[1024,256]{1,0:T(8,128)(2,1)S(1)}, bf16[1024,256]{1,0:T(8,128)(2,1)S(1)}, u32[]{:S(2)}, u32[]{:S(2)}) collective-permute-start(bf16[1024,256]{1,0:T(8,128)(2,1)S(1)} %heads_2.3.refs_0_), channel_id=1, source_target_pairs={{0,1},{1,2},{2,3},{3,0},{4,5},{5,6},{6,7},{7,4},{8,9},{9,10},{10,1... | collective-permute-start | bytes 1572872 | tf_op jit(solution)/shard_map/ppermute | solution.py:61
  293.5 45.1 %collective-permute-start.59 = (bf16[1024,256]{1,0:T(8,128)(2,1)S(1)}, bf16[1024,256]{1,0:T(8,128)(2,1)S(1)}, u32[]{:S(2)}, u32[]{:S(2)}) collective-permute-start(bf16[1024,256]{1,0:T(8,128)(2,1)S(1)} %heads_2.4.refs_0_), channel_id=1, source_target_pairs={{0,3},{1,0},{2,1},{3,2},{4,7},{5,4},{6,5},{7,6},{8,11},{9,8},{10,9... | collective-permute-start | bytes 1572872 | tf_op jit(solution)/shard_map/ppermute | solution.py:61
  304.2 45.5 %collective-permute-start.58 = (bf16[1024,256]{1,0:T(8,128)(2,1)S(1)}, bf16[1024,256]{1,0:T(8,128)(2,1)S(1)}, u32[]{:S(2)}, u32[]{:S(2)}) collective-permute-start(bf16[1024,256]{1,0:T(8,128)(2,1)S(1)} %collective-permute-done.57.refs_1_), channel_id=1, source_target_pairs={{0,1},{1,2},{2,3},{3,0},{4,5},{5,6},{6,7},{7,4},{8,9},{9,10},{10,1... | collective-permute-start | bytes 1572872 | tf_op jit(solution)/shard_map/ppermute | solution.py:61
  304.9 55.8 %collective-permute-start.38 = (bf16[1024,256]{1,0:T(8,128)(2,1)S(1)}, bf16[1024,256]{1,0:T(8,128)(2,1)S(1)}, u32[]{:S(2)}, u32[]{:S(2)}) collective-permute-start(bf16[1024,256]{1,0:T(8,128)(2,1)S(1)} %heads_2.3.refs_0_), channel_id=1, source_target_pairs={{0,3},{1,0},{2,1},{3,2},{4,7},{5,4},{6,5},{7,6},{8,11},{9,8},{10,9... | collective-permute-start | bytes 1572872 | tf_op jit(solution)/shard_map/ppermute | solution.py:61
  327.2 43.2 %collective-permute-start.37 = (bf16[1024,256]{1,0:T(8,128)(2,1)S(1)}, bf16[1024,256]{1,0:T(8,128)(2,1)S(1)}, u32[]{:S(2)}, u32[]{:S(2)}) collective-permute-start(bf16[1024,256]{1,0:T(8,128)(2,1)S(1)} %collective-permute-done.36.refs_1_), channel_id=1, source_target_pairs={{0,1},{1,2},{2,3},{3,0},{4,5},{5,6},{6,7},{7,4},{8,9},{9,10},{10,1... | collective-permute-start | bytes 1572872 | tf_op jit(solution)/shard_map/ppermute | solution.py:61
  (110 other events, 1774.3 us)

commit v2 on v0

v2 whole, which is shorter than its diff:
```python
import functools

import jax
import jax.numpy as jnp
import numpy as np
from jax import lax
from jax.experimental import pallas as pl
from jax.experimental.pallas import tpu as pltpu
from jax.sharding import PartitionSpec as P

L = 256
HEAD_DIM = 128
EPS = 1e-05
BF = jnp.bfloat16
F32 = jnp.float32
MIB = 1 << 20
VMEM = 60 * MIB
LIGHT = pl.CostEstimate(flops=1, bytes_accessed=1, transcendentals=0)


def after(x, *deps):
    return lax.optimization_barrier((x,) + deps)[0]


def row_offsets(rows):
    if rows == 8:
        even, odd = [0, 2, 4, 6, 1, 5, 3, 7], [0, 4, 2, 6, 1, 3, 5, 7]
        return [odd if r % 2 else even for r in range(rows)]
    offsets, bit = [0], rows // 2
    while bit:
        offsets = offsets + [t ^ bit for t in offsets]
        bit //= 2
    return [offsets] * rows


def row_slots(rows):
    slots = np.zeros((rows, rows), np.int32)
    for r, offsets in enumerate(row_offsets(rows)):
        for place, offset in enumerate(offsets):
            slots[r, r ^ offset] = place
    return slots


def row_sources(rows):
    return np.array([[r ^ t for t in row] for r, row in enumerate(row_offsets(rows))], np.int32)


def swap(x, pairs):
    return lax.ppermute(x, "row", pairs)


class Rows:
    def __init__(self, x, rows):
        self.rows, self.x = rows, x
        self.parts = {0: x}
        self.first = [(r, r ^ (4 if r % 2 else 2)) for r in range(rows)]
        self.second = [(r, r ^ (2 if r % 2 else 4)) for r in range(rows)]
        self.sibling = [(r, r ^ 1) for r in range(rows)]

    def fetch(self, *places):
        for p in places:
            pairs = {1: self.first, 2: self.second, 3: self.second}.get(p, self.sibling)
            origin = {1: 0, 2: 0, 3: 1}.get(p, p - 4)
            self.parts[p] = swap(self.parts[origin], pairs)

    def start(self):
        if self.rows == 8:
            self.fetch(1, 2, 4)
            return
        blocks, bit = [self.x], self.rows // 2
        while bit:
            pairs = [(r, r ^ bit) for r in range(self.rows)]
            blocks = blocks + [swap(t, pairs) for t in blocks]
            bit //= 2
        self.parts = dict(enumerate(blocks))

    def forward(self):
        if self.rows == 8:
            self.fetch(3, 5, 6)

    def finish(self):
        if self.rows == 8:
            self.fetch(7)

    def blocks(self, places):
        return [self.parts[p] for p in places]


def early_places(rows):
    return [0, 1, 2, 4] if rows == 8 else list(range(rows // 2))


def shift(x, cols, step):
    return lax.ppermute(x, "col", [(c, (c + step) % cols) for c in range(cols)])


def near_cols(x, cols):
    blocks = [x] + [None] * (cols - 1)
    blocks[1] = shift(x, cols, 1)
    if cols > 2:
        blocks[cols - 1] = shift(x, cols, -1)
    return blocks


def far_cols(blocks, cols):
    blocks = list(blocks)
    for k in range(2, cols // 2 + 1):
        if blocks[k] is None:
            blocks[k] = shift(blocks[k - 1], cols, 1)
    for k in range(cols - 2, cols // 2, -1):
        blocks[k] = shift(blocks[k + 1], cols, -1)
    return blocks


def col_gather(x, cols):
    return far_cols(near_cols(x, cols), cols)


def place_kernel(parts, ids_ref, *refs):
    tables, out_ref, held = refs[: sum(parts)], refs[-2], refs[-1]
    width = out_ref.shape[1]

    @pl.when(pl.program_id(0) == 0)
    def _():
        column, at = 0, 0
        for count in parts:
            low = 0
            for block in tables[at : at + count]:
                held[low : low + block.shape[0], column : column + block.shape[1]] = block[...]
                low += block.shape[0]
            at += count
            column += block.shape[1]

    wide = lax.broadcasted_iota(jnp.int32, (L, held.shape[0]), 1)
    pick = jnp.where(wide == ids_ref[...], 1.0, 0.0).astype(BF)
    step = min(width, 1024)
    for low in range(0, width, step):
        out_ref[:, low : low + step] = jnp.dot(
            pick, held[:, low : low + step], preferred_element_type=F32
        ).astype(BF)


def place(ids, *tables):
    tokens = ids.shape[0]
    positions = sum(t.shape[0] for t in tables[0])
    width = sum(t[0].shape[1] for t in tables)
    operands = [t for table in tables for t in table]
    return pl.pallas_call(
        functools.partial(place_kernel, [len(t) for t in tables]),
        out_shape=jax.ShapeDtypeStruct((tokens, width), BF),
        grid=(tokens // L,),
        in_specs=[pl.BlockSpec((L, 1), lambda i: (i, 0))]
        + [pl.BlockSpec(t.shape, lambda i: (0, 0)) for t in operands],
        out_specs=pl.BlockSpec((L, width), lambda i: (i, 0)),
        scratch_shapes=[pltpu.VMEM((positions, width), BF)],
        compiler_params=pltpu.CompilerParams(vmem_limit_bytes=VMEM),
        cost_estimate=LIGHT,
        name="place",
    )(ids, *operands)


def norm_kernel(cols, part, n_late, col_ref, keep_ref, ids_ref, own_ref, near_ref, *refs):
    late, refs = refs[:n_late], refs[n_late:]
    encs, shares = refs[:cols], refs[cols : 2 * cols]
    out_ref, extra, table, held = refs[2 * cols :]
    image = pl.program_id(0)
    width = held.shape[2]
    vis = encs[0].shape[0]
    seen_all = cols * vis
    base = seen_all + 128

    @pl.when(image == 0)
    def _():
        for k in range(cols):
            both = shares[k][part : part + 16, :]
            extra[k] = both
            at = col_ref[k]
            table[at, seen_all : seen_all + 16, :] = both
            table[at, seen_all + 16 : base, :] = jnp.zeros((112, width), BF)
            for z in range(cols):
                table[z, k * vis : (k + 1) * vis, :] = encs[k][:, z * width : (z + 1) * width]
            if k:
                for p in range(n_late):
                    low = base + p * part
                    table[at, low : low + part, :] = late[p][:, (k - 1) * width : k * width]

    here = lax.broadcasted_iota(jnp.int32, (L, seen_all), 0) + image * L
    seen = jnp.where(here == keep_ref[...], 1.0, 0.0)
    hidden = 1.0 - jnp.max(seen, axis=1, keepdims=True)
    lane = lax.broadcasted_iota(jnp.int32, (L, 128), 1)
    wide = lax.broadcasted_iota(jnp.int32, (L, n_late * part), 1)
    rest = jnp.where(wide == ids_ref[...], 1.0, 0.0)
    pick = jnp.concatenate([seen, jnp.where(lane == 1, hidden, 0.0), rest], axis=1).astype(BF)
    ones = jnp.ones((width, 128), BF)
    total = jnp.zeros((L, 128), F32)
    squares = jnp.zeros((L, 1), F32)
    for k in range(cols):
        at = col_ref[k]
        if k == 0:
            x = jnp.dot(pick[:, :base], table[at, :base, :], preferred_element_type=F32)
            x = x + own_ref[...].astype(F32)
        else:
            x = jnp.dot(pick, table[at], preferred_element_type=F32)
            x = x + near_ref[:, (k - 1) * width : k * width].astype(F32)
        xb = x.astype(BF)
        held[k] = xb
        total = total + jnp.dot(xb, ones, preferred_element_type=F32)
        x = xb.astype(F32)
        squares = squares + jnp.sum(x * x, axis=1, keepdims=True)
    mean = total[:, :1] / (cols * width)
    var = squares / (cols * width) - mean * mean
    scale = lax.rsqrt(var + EPS)
    for k in range(cols):
        x = held[k].astype(F32)
        low = pl.multiple_of(col_ref[k] * width, width)
        out_ref[:, pl.ds(low, width)] = (
            (x - mean) * scale * extra[k, 0:1, :].astype(F32)
        ).astype(BF)


def fill_and_norm(part, order, keep, ids, own, near, late, encs, shares):
    tokens, width = own.shape
    cols = len(encs)
    vis = encs[0].shape[0]
    whole = lambda a: pl.BlockSpec(a.shape, lambda i, *_: (0, 0))
    row = lambda i, *_: (i, 0)
    return pl.pallas_call(
        functools.partial(norm_kernel, cols, part, len(late)),
        out_shape=jax.ShapeDtypeStruct((tokens, cols * width), BF),
        grid_spec=pltpu.PrefetchScalarGridSpec(
            num_scalar_prefetch=1,
            grid=(tokens // L,),
            in_specs=[whole(keep)]
            + [pl.BlockSpec((L, p.shape[1]), row) for p in (ids, own, near)]
            + [whole(a) for a in late + encs + shares],
            out_specs=pl.BlockSpec((L, cols * width), row),
            scratch_shapes=[
                pltpu.VMEM((cols, 16, width), BF),
                pltpu.VMEM((cols, cols * vis + 128 + len(late) * part, width), BF),
                pltpu.VMEM((cols, L, width), BF),
            ],
        ),
        compiler_params=pltpu.CompilerParams(vmem_limit_bytes=VMEM),
        cost_estimate=LIGHT,
        name="fill_norm",
    )(order, keep, ids, own, near, *late, *encs, *shares)


def attend(projected, heads, out_ref):
    hw = heads * HEAD_DIM
    scale = HEAD_DIM**-0.5
    for h in range(heads):
        cut = lambda j: projected[:, j * hw + h * HEAD_DIM : j * hw + (h + 1) * HEAD_DIM]
        s = lax.dot_general(
            cut(0), cut(1), (((1,), (1,)), ((), ())), preferred_element_type=F32
        ) * scale
        e = jnp.exp(s - jnp.max(s, axis=1, keepdims=True))
        p = (e / jnp.sum(e, axis=1, keepdims=True)).astype(BF)
        o = jnp.dot(p, cut(2), preferred_element_type=F32)
        out_ref[:, h * HEAD_DIM : (h + 1) * HEAD_DIM] = o.astype(BF)


def heads_kernel(heads, source_ref, x_ref, *refs):
    weights, out_ref = refs[:-1], refs[-1]
    if len(weights) == 1:
        acc = jnp.dot(x_ref[...], weights[0][...], preferred_element_type=F32)
    else:
        acc = None
        for p, w_ref in enumerate(weights):
            block = w_ref.shape[0]
            low = pl.multiple_of(source_ref[p] * block, block)
            term = jnp.dot(x_ref[:, pl.ds(low, block)], w_ref[...], preferred_element_type=F32)
            acc = term if acc is None else acc + term
    attend(acc.astype(BF), heads, out_ref)


def some_heads(source, normed, weights, heads):
    tokens, depth = normed.shape
    hw = heads * HEAD_DIM
    return pl.pallas_call(
        functools.partial(heads_kernel, heads),
        out_shape=jax.ShapeDtypeStruct((tokens, hw), BF),
        grid_spec=pltpu.PrefetchScalarGridSpec(
            num_scalar_prefetch=1,
            grid=(tokens // L,),
            in_specs=[pl.BlockSpec((L, depth), lambda i, *_: (i, 0))]
            + [pl.BlockSpec(w.shape, lambda i, *_: (0, 0)) for w in weights],
            out_specs=pl.BlockSpec((L, hw), lambda i, *_: (i, 0)),
        ),
        compiler_params=pltpu.CompilerParams(vmem_limit_bytes=VMEM),
        cost_estimate=LIGHT,
        name=f"heads_{heads}",
    )(source, normed, *weights)


def out_kernel(n, has_acc, at_ref, *refs):
    xs, ws = refs[:n], refs[n : 2 * n]
    out_ref = refs[-1]
    acc = refs[2 * n][...] if has_acc else None
    for x_ref, w_ref in zip(xs, ws):
        term = jnp.dot(x_ref[...], w_ref[...], preferred_element_type=F32)
        acc = term if acc is None else acc + term
    out_ref[...] = acc.astype(out_ref.dtype)


def project(order, groups, weight, acc, last):
    tokens = next(iter(groups[0][1].values())).shape[0]
    width = weight.shape[1]
    row = lambda i, *_: (i, 0)
    xs, x_specs, w_specs = [], [], []
    for first, parts in groups:
        depth = parts[min(parts)].shape[1]
        for k, x in sorted(parts.items()):
            xs.append(x)
            x_specs.append(pl.BlockSpec((L, depth), row))
            w_specs.append(
                pl.BlockSpec(
                    (depth, width),
                    lambda i, at, k=k, first=first, depth=depth: (
                        at[k] * (width // depth) + first // depth, 0
                    ),
                )
            )
    n = len(xs)
    operands = xs + [weight] * n
    specs = x_specs + w_specs
    alias = {}
    if acc is not None:
        specs.append(pl.BlockSpec((L, width), row))
        operands.append(acc)
        if not last:
            alias = {1 + 2 * n: 0}
    depths = sum(x.shape[1] for x in xs)
    return pl.pallas_call(
        functools.partial(out_kernel, n, acc is not None),
        out_shape=jax.ShapeDtypeStruct((tokens, width), BF if last else F32),
        grid_spec=pltpu.PrefetchScalarGridSpec(
            num_scalar_prefetch=1,
            grid=(tokens // L,),
            in_specs=specs,
            out_specs=pl.BlockSpec((L, width), row),
        ),
        input_output_aliases=alias,
        compiler_params=pltpu.CompilerParams(vmem_limit_bytes=VMEM),
        cost_estimate=LIGHT,
        name="out_proj",
    )(order, *operands)


def head_chunks(heads):
    return [(low, 2) for low in range(0, heads, 2)]


def gate(*trees):
    return lax.optimization_barrier(trees)


def on_device(
    rows, cols, enc_out, keep, pos_ids, mask_token, pos_table, gain, w_query, w_key, w_value, w_out
):
    images = keep.shape[0]
    positions, width = pos_table.shape
    r, c = lax.axis_index("row"), lax.axis_index("col")
    slot = jnp.asarray(row_slots(rows))[r]
    order = (c - jnp.arange(cols, dtype=jnp.int32)) % cols
    chunks = head_chunks(width // HEAD_DIM)
    n = len(chunks)

    def packed(k):
        low, size = chunks[k]
        cut = slice(low * HEAD_DIM, (low + size) * HEAD_DIM)
        return jnp.concatenate([w_query[:, cut], w_key[:, cut], w_value[:, cut]], axis=1)

    part = positions // rows
    owner, inner = pos_ids // part, pos_ids % part
    early = early_places(rows)
    later = [p for p in range(rows) if p not in early]

    def ids_of(places):
        rank = np.full((rows,), -rows, np.int32)
        rank[places] = np.arange(len(places))
        rank = jnp.asarray(rank[row_slots(rows)])[r]
        ids = inner
        for b in range(rows):
            ids = ids + jnp.where(owner == b, rank[b] * part, 0)
        return ids.reshape(images * L, 1)

    small = (
        pos_ids.reshape(images * L, 1),
        ids_of(early),
        ids_of(later),
        (keep + L * jnp.arange(images, dtype=jnp.int32)[:, None]).reshape(cols, -1)[order].reshape(1, -1),
        jnp.asarray(row_sources(rows))[r],
        order,
    )

    share = lax.dynamic_slice_in_dim(pos_table, r * part, part, axis=0)
    pad = jnp.zeros((14, width), BF)
    share = jnp.concatenate([share, gain[None], mask_token[None], pad], axis=0)
    others = range(1, cols)

    gather = lambda w: lax.all_gather(w, "row", axis=0, tiled=True)
    split = rows == 8 and n >= 4
    weights = [[gather(packed(0))]]
    shares = [share] + [shift(share, cols, k) for k in others]
    placed_own = place(small[0], [pos_table])
    packs = [packed(k) for k in range(1, n)]
    shares, placed_own, enc, packs, w_out, small = gate(
        shares, placed_own, enc_out, packs, w_out, small
    )
    _, early_ids, later_ids, numbers, source, order = small

    weights += [[gather(p)] for p in (packs[:-1] if split else packs)]
    w_full = gather(w_out)
    late = Rows(packs[-1], rows)

    table = Rows(jnp.concatenate([shares[k][:part] for k in others], axis=1), rows)
    table.start()
    encs = near_cols(enc, cols)
    table.parts, encs = gate(table.parts, encs)

    encs = far_cols(encs, cols)
    table.forward()
    placed = place(early_ids, table.blocks(early))
    table.parts, encs, placed = gate(table.parts, encs, placed)

    table.finish()
    if split:
        late.fetch(1, 2)
    normed = fill_and_norm(
        part, order, numbers, later_ids, placed_own, placed, table.blocks(later), encs, shares
    )
    attended = some_heads(source, normed, weights[0], chunks[0][1])
    attended, normed, late.parts = gate(attended, normed, late.parts)

    sent, half = [], None
    for k in range(1, n):
        whole = far_cols(half, cols) if half else None
        half = near_cols(attended, cols)
        if split and k == 1:
            late.fetch(3, 5)
        if split and k == 2:
            late.fetch(4, 6, 7)
        if split and k == n - 1:
            weights.append(late.blocks(range(rows)))
        attended = some_heads(source, normed, weights[k], chunks[k][1])
        attended, normed, half, whole, late.parts = gate(attended, normed, half, whole, late.parts)
        if whole:
            sent.append(whole)
    group = lambda k: (chunks[k][0] * HEAD_DIM, dict(enumerate(sent[k])))
    whole = far_cols(half, cols)
    half = near_cols(attended, cols)
    acc = None
    if n > 2:
        acc = project(order, [group(k) for k in range(n - 2)], w_full, None, False)
    half, whole, acc = gate(half, whole, acc)
    sent.append(whole)
    first = chunks[n - 1][0] * HEAD_DIM
    here = {k: x for k, x in enumerate(half) if x is not None}
    acc = project(order, [group(n - 2), (first, here)], w_full, acc, False)
    far = {k: x for k, x in enumerate(far_cols(half, cols)) if k not in here}
    return project(order, [(first, far)], w_full, acc, True)


def solution(mesh):
    rows, cols = mesh.shape["row"], mesh.shape["col"]
    in_specs = (
        P(("row", "col"), None),
        P("row", None),
        P("row", None),
        P("col"),
        P(None, "col"),
        P("col"),
        P("row", "col"),
        P("row", "col"),
        P("row", "col"),
        P("row", "col"),
    )
    return jax.shard_map(
        functools.partial(on_device, rows, cols),
        mesh=mesh,
        in_specs=in_specs,
        out_specs=P("row", "col"),
        check_vma=False,
    )
```

time: 589 us -> 300 us (0.51)
  waiting for transfers between devices: 468 us -> 98.5 us
  Pallas kernels: 0 us -> 122 us
  matrix products: 62.7 us -> 0 us
  starting transfers between devices: 6.69 us -> 34.8 us
  between operations: 13.6 us -> 23.7 us
  blocking collectives: 9.98 us -> 0 us
  other arithmetic: 10.5 us -> 4.42 us
    all_gather x6 -> x4, waiting for transfers between devices: 459 us -> 1.74 us  [on_device(): gather = lambda w: lax.all_gather(w, 'row', axis=0, tiled=True)]
    pallas_call x0 -> x10, Pallas kernels: none -> 122 us  [the longest x4 61.2 us: some_heads(): pl.pallas_call(functools.partial(heads_kernel, heads), out_shape=jax.Shap...]
    ppermute x0 -> x32, waiting for transfers between devices: none -> 95.6 us  [the longest x18 92.2 us: shift(): return lax.ppermute(x, 'col', [(c, (c + step) % cols) for c in range(cols)])]
    dot_general x7 -> x0, matrix products: 62.7 us -> none  [the longest x4 55.7 us: add_rows(): return jnp.dot(left, piece, preferred_element_type=jnp.float32)]
    ppermute x0 -> x32, starting transfers between devices: none -> 34.6 us  [the longest x18 27.7 us: shift(): return lax.ppermute(x, 'col', [(c, (c + step) % cols) for c in range(cols)])]
    psum x1 -> x0, blocking collectives: 9.98 us -> none  [on_device(): lax.psum((jnp.sum(values, axis=1), jnp.sum(values * values, axis=1)), 'col')]
    all_to_all x1 -> x0, waiting for transfers between devices: 6.9 us -> none  [on_device(): lax.all_to_all(enc_out, 'col', split_axis=1, concat_axis=0, tiled=True)]
    all_to_all x1 -> x0, starting transfers between devices: 6.32 us -> none  [on_device(): lax.all_to_all(enc_out, 'col', split_axis=1, concat_axis=0, tiled=True)]
  transfers between devices with their start and end apart: 7 -> 36, of which waited for: 7 -> 15; matrix products, arithmetic and copies ran while one was open for 11% -> 4% of each run, Pallas kernels for 0% -> 39%
where the time goes in v2:
time: 300 us
  Pallas kernels  122 us (41%)
  waiting for transfers between devices  98.5 us (33%)
  starting transfers between devices  34.8 us (12%)
  between operations  23.7 us (8%)
  local copies, waits for them, and re-layouts  16 us (5%)
  other arithmetic  4.42 us (1%)
    ppermute x18, waiting for transfers between devices, shift(): return lax.ppermute(x, 'col', [(c, (c + step) % cols) for c in range(cols)])  92.2 us
    pallas_call x4, Pallas kernels, some_heads(): pl.pallas_call(functools.partial(heads_kernel, heads), out_shape=jax.Shap...  61.2 us
    ppermute x18, starting transfers between devices, shift(): return lax.ppermute(x, 'col', [(c, (c + step) % cols) for c in range(cols)])  27.7 us
    pallas_call x3, Pallas kernels, project(): pl.pallas_call(functools.partial(out_kernel, n, acc is not None), out_sha...  25.7 us
    pallas_call x1, Pallas kernels, fill_and_norm(): pl.pallas_call(functools.partial(norm_kernel, cols, part, len(late)), out...  21.4 us
    pallas_call x2, Pallas kernels, place(): pl.pallas_call(functools.partial(place_kernel, [len(t) for t in tables]),...  14.1 us
    ppermute x14, starting transfers between devices, swap(): return lax.ppermute(x, 'row', pairs)  6.9 us
  transfers between devices with their start and end apart: 36, of which 15 were waited for; matrix products, arithmetic and copies ran while one was open for 4% of the time, Pallas kernels for 39%

profile of v2, /device:TPU:0, one launch (start us, length us, event | category | flops | bytes accessed | tf_op | source)
XLA Modules:
  0.0 299.7 jit_solution(248607674715462681)
XLA Ops:
  12.5 3.1 %collective-permute-start = (bf16[144,1024]{1,0:T(8,128)(2,1)S(1)}, bf16[144,1024]{1,0:T(8,128)(2,1)S(1)}, u32[]{:S(2)}, u32[]{:S(2)}) collective-permute-start(bf16[144,1024]{1,0:T(8,128)(2,1)S(1)} %maximum_maximum_fusion.refs_8_), channel_id=1, source_target_pairs={{0,1},{1,2},{2,3},{3,0},{4,5},{5,6},{6,7},{7,4},{8,9},{9,10},{10,1... | collective-permute-start | bytes 884744 | tf_op jit(solution)/shard_map/ppermute | solution.py:94
  34.8 6.1 %place.2.own_ref = bf16[1024,1024]{1,0:T(8,128)(2,1)} custom-call(s32[1024,1]{1,0:T(8,128)} %copy.15.ids_ref, bf16[1024,1024]{1,0:T(8,128)(2,1)} %refs_0_.1), custom_call_target="tpu_custom_call" | custom-call | flops 1 | bytes 1 | tf_op jit(solution)/shard_map/place/pallas_call | solution.py:148
  50.0 3.2 %collective-permute-start.7 = (bf16[64,4096]{1,0:T(8,128)(2,1)S(1)}, bf16[64,4096]{1,0:T(8,128)(2,1)S(1)}, u32[]{:S(2)}, u32[]{:S(2)}) collective-permute-start(bf16[64,4096]{1,0:T(8,128)(2,1)S(1)} %copy-done.23), channel_id=1, source_target_pairs={{0,3},{1,0},{2,1},{3,2},{4,7},{5,4},{6,5},{7,6},{8,11},{9,8},{10,9... | collective-permute-start | bytes 1572872 | tf_op jit(solution)/shard_map/ppermute | solution.py:94
  53.1 12.8 %collective-permute-done.6.refs_5_ = bf16[64,4096]{1,0:T(8,128)(2,1)} collective-permute-done((bf16[64,4096]{1,0:T(8,128)(2,1)S(1)}, bf16[64,4096]{1,0:T(8,128)(2,1)}, u32[]{:S(2)}, u32[]{:S(2)}) %collective-permute-start.6) | collective-permute-done | bytes 524320 | tf_op jit(solution)/shard_map/ppermute | solution.py:94
  66.0 9.3 %collective-permute-done.7.refs_7_ = bf16[64,4096]{1,0:T(8,128)(2,1)S(1)} collective-permute-done((bf16[64,4096]{1,0:T(8,128)(2,1)S(1)}, bf16[64,4096]{1,0:T(8,128)(2,1)S(1)}, u32[]{:S(2)}, u32[]{:S(2)}) %collective-permute-start.7) | collective-permute-done | bytes 524320 | tf_op jit(solution)/shard_map/ppermute | solution.py:94
  79.5 8.0 %place.3.near_ref = bf16[1024,3072]{1,0:T(8,128)(2,1)} custom-call(s32[1024,1]{1,0:T(8,128)} %copy.16.ids_ref, bf16[128,3072]{1,0:T(8,128)(2,1)} %copy-done.1, bf16[128,3072]{1,0:T(8,128)(2,1)} %copy-done.12, bf16[128,3072]{1,0:T(8,128)(2,1)} %copy-done.13, bf16[128,3072]{1,0:T(8,128)(2,1)} %copy-done.14), custom_call_target="tpu_custom_call" | custom-call | flops 1 | bytes 1 | tf_op jit(solution)/shard_map/place/pallas_call | solution.py:148
  87.5 5.9 %collective-permute-done.11.refs_6_ = bf16[64,4096]{1,0:T(8,128)(2,1)} collective-permute-done((bf16[64,4096]{1,0:T(8,128)(2,1)}, bf16[64,4096]{1,0:T(8,128)(2,1)}, u32[]{:S(2)}, u32[]{:S(2)}) %collective-permute-start.11) | collective-permute-done | bytes 524320 | tf_op jit(solution)/shard_map/ppermute | solution.py:94
  99.8 21.4 %fill_norm.1.x_ref = bf16[1024,4096]{1,0:T(8,128)(2,1)} custom-call(s32[4]{0:T(128)} %and_select_fusion.col_ref.at_ref, s32[1,256]{1,0:T(1,128)} %reshape.133.keep_ref, s32[1024,1]{1,0:T(8,128)} %copy.17.ids_ref, bf16[1024,1024]{1,0:T(8,128)(2,1)} %place.2.own_ref, bf16[1024,3072]{1,0:T(8,128)(2,1)} %place.3.near_ref, ...), custom_call_target="tpu_custom_call" | custom-call | flops 1 | bytes 1 | tf_op jit(solution)/shard_map/fill_norm/pallas_call | solution.py:227
  121.2 15.0 %heads_2.4.refs_0_ = bf16[1024,256]{1,0:T(8,128)(2,1)} custom-call(s32[8]{0:T(128)} %fusion.1.source_ref, bf16[1024,4096]{1,0:T(8,128)(2,1)} %fill_norm.1.x_ref, bf16[4096,768]{1,0:T(8,128)(2,1)} %all-gather.5.cloned.1.call-done.refs_0_), custom_call_target="tpu_custom_call" | custom-call | flops 1 | bytes 1 | tf_op jit(solution)/shard_map/heads_2/pallas_call | solution.py:280
  141.6 15.7 %heads_2.5.refs_4_ = bf16[1024,256]{1,0:T(8,128)(2,1)} custom-call(s32[8]{0:T(128)} %fusion.1.source_ref, bf16[1024,4096]{1,0:T(8,128)(2,1)} %fill_norm.1.x_ref, bf16[4096,768]{1,0:T(8,128)(2,1)} %all-gather.7.cloned.1.call-done.refs_0_), custom_call_target="tpu_custom_call" | custom-call | flops 1 | bytes 1 | tf_op jit(solution)/shard_map/heads_2/pallas_call | solution.py:280
  157.3 7.0 %collective-permute-done.16.refs_3_ = bf16[1024,256]{1,0:T(8,128)(2,1)} collective-permute-done((bf16[1024,256]{1,0:T(8,128)(2,1)}, bf16[1024,256]{1,0:T(8,128)(2,1)}, u32[]{:S(2)}, u32[]{:S(2)}) %collective-permute-start.16) | collective-permute-done | bytes 524320 | tf_op jit(solution)/shard_map/ppermute | solution.py:94
  168.8 12.6 %collective-permute-done.19.refs_5_ = bf16[1024,256]{1,0:T(8,128)(2,1)} collective-permute-done((bf16[1024,256]{1,0:T(8,128)(2,1)}, bf16[1024,256]{1,0:T(8,128)(2,1)}, u32[]{:S(2)}, u32[]{:S(2)}) %collective-permute-start.19) | collective-permute-done | bytes 524320 | tf_op jit(solution)/shard_map/ppermute | solution.py:94
  183.1 15.0 %heads_2.6.refs_0_ = bf16[1024,256]{1,0:T(8,128)(2,1)} custom-call(s32[8]{0:T(128)} %fusion.1.source_ref, bf16[1024,4096]{1,0:T(8,128)(2,1)} %fill_norm.1.x_ref, bf16[4096,768]{1,0:T(8,128)(2,1)} %all-gather.9.cloned.1.call-done.refs_0_), custom_call_target="tpu_custom_call" | custom-call | flops 1 | bytes 1 | tf_op jit(solution)/shard_map/heads_2/pallas_call | solution.py:280
  198.2 3.9 %collective-permute-done.21.refs_2_ = bf16[1024,256]{1,0:T(8,128)(2,1)} collective-permute-done((bf16[1024,256]{1,0:T(8,128)(2,1)}, bf16[1024,256]{1,0:T(8,128)(2,1)}, u32[]{:S(2)}, u32[]{:S(2)}) %collective-permute-start.21) | collective-permute-done | bytes 524320 | tf_op jit(solution)/shard_map/ppermute | solution.py:94
  202.5 3.4 %collective-permute-start.26 = (bf16[1024,256]{1,0:T(8,128)(2,1)}, bf16[1024,256]{1,0:T(8,128)(2,1)S(1)}, u32[]{:S(2)}, u32[]{:S(2)}) collective-permute-start(bf16[1024,256]{1,0:T(8,128)(2,1)} %heads_2.6.refs_0_), channel_id=1, source_target_pairs={{0,3},{1,0},{2,1},{3,2},{4,7},{5,4},{6,5},{7,6},{8,11},{9,8},{10,9... | collective-permute-start | bytes 1572872 | tf_op jit(solution)/shard_map/ppermute | solution.py:94
  205.9 15.4 %heads_2.7.refs_4_ = bf16[1024,256]{1,0:T(8,128)(2,1)} custom-call(s32[8]{0:T(128)} %fusion.1.source_ref, bf16[1024,4096]{1,0:T(8,128)(2,1)} %fill_norm.1.x_ref, bf16[512,768]{1,0:T(8,128)(2,1)} %copy-done, bf16[512,768]{1,0:T(8,128)(2,1)} %copy-done.8, bf16[512,768]{1,0:T(8,128)(2,1)} %copy-done.9, bf16[512,768]{1,0:T(8,128)(2,1)} %copy-done.10, ...), custom_call_target="tpu_custom_call" | custom-call | flops 1 | bytes 1 | tf_op jit(solution)/shard_map/heads_2/pallas_call | solution.py:280
  221.4 8.2 %collective-permute-done.26.refs_3_ = bf16[1024,256]{1,0:T(8,128)(2,1)S(1)} collective-permute-done((bf16[1024,256]{1,0:T(8,128)(2,1)}, bf16[1024,256]{1,0:T(8,128)(2,1)S(1)}, u32[]{:S(2)}, u32[]{:S(2)}) %collective-permute-start.26) | collective-permute-done | bytes 524320 | tf_op jit(solution)/shard_map/ppermute | solution.py:94
  229.5 9.2 %collective-permute-done.27.refs_6_ = bf16[1024,256]{1,0:T(8,128)(2,1)S(1)} collective-permute-done((bf16[1024,256]{1,0:T(8,128)(2,1)}, bf16[1024,256]{1,0:T(8,128)(2,1)S(1)}, u32[]{:S(2)}, u32[]{:S(2)}) %collective-permute-start.27) | collective-permute-done | bytes 524320 | tf_op jit(solution)/shard_map/ppermute | solution.py:94
  238.8 3.8 %collective-permute-start.29 = (bf16[1024,256]{1,0:T(8,128)(2,1)}, bf16[1024,256]{1,0:T(8,128)(2,1)S(1)}, u32[]{:S(2)}, u32[]{:S(2)}) collective-permute-start(bf16[1024,256]{1,0:T(8,128)(2,1)} %heads_2.7.refs_4_), channel_id=1, source_target_pairs={{0,3},{1,0},{2,1},{3,2},{4,7},{5,4},{6,5},{7,6},{8,11},{9,8},{10,9... | collective-permute-start | bytes 1572872 | tf_op jit(solution)/shard_map/ppermute | solution.py:94
  242.6 10.0 %out_proj.3.refs_14_ = f32[1024,1024]{1,0:T(8,128)} custom-call(s32[4]{0:T(128)} %and_select_fusion.col_ref.at_ref, bf16[1024,256]{1,0:T(8,128)(2,1)} %heads_2.4.refs_0_, bf16[1024,256]{1,0:T(8,128)(2,1)} %collective-permute-done.15.refs_1_, bf16[1024,256]{1,0:T(8,128)(2,1)} %collective-permute-done.21.refs_2_, ...), custom_call_target="tpu_custom_call" | custom-call | flops 1 | bytes 1 | tf_op jit(solution)/shard_map/out_proj/pallas_call | solution.py:334
  255.6 10.5 %collective-permute-done.29.refs_6_ = bf16[1024,256]{1,0:T(8,128)(2,1)S(1)} collective-permute-done((bf16[1024,256]{1,0:T(8,128)(2,1)}, bf16[1024,256]{1,0:T(8,128)(2,1)S(1)}, u32[]{:S(2)}, u32[]{:S(2)}) %collective-permute-start.29) | collective-permute-done | bytes 524320 | tf_op jit(solution)/shard_map/ppermute | solution.py:94
  266.2 8.4 %collective-permute-done.30.refs_2_ = bf16[1024,256]{1,0:T(8,128)(2,1)S(1)} collective-permute-done((bf16[1024,256]{1,0:T(8,128)(2,1)S(1)}, bf16[1024,256]{1,0:T(8,128)(2,1)S(1)}, u32[]{:S(2)}, u32[]{:S(2)}) %collective-permute-start.30) | collective-permute-done | bytes 524320 | tf_op jit(solution)/shard_map/ppermute | solution.py:94
  275.3 10.0 %out_proj.4.refs_2_ = f32[1024,1024]{1,0:T(8,128)} custom-call(s32[4]{0:T(128)} %and_select_fusion.col_ref.at_ref, bf16[1024,256]{1,0:T(8,128)(2,1)} %heads_2.6.refs_0_, bf16[1024,256]{1,0:T(8,128)(2,1)} %copy-done.16, bf16[1024,256]{1,0:T(8,128)(2,1)} %copy-done.21, bf16[1024,256]{1,0:T(8,128)(2,1)} %copy-done.17, ...), custom_call_target="tpu_custom_call", output_to_operand_aliasing={{}: (15, {})} | custom-call | flops 1 | bytes 1 | tf_op jit(solution)/shard_map/out_proj/pallas_call | solution.py:334
  287.5 5.7 %out_proj.5 = bf16[1024,1024]{1,0:T(8,128)(2,1)} custom-call(s32[4]{0:T(128)} %and_select_fusion.col_ref.at_ref, bf16[1024,256]{1,0:T(8,128)(2,1)} %copy-done.22, bf16[4096,1024]{1,0:T(8,128)(2,1)} %all-gather.11.cloned.1.call-done.refs_8_.refs_9_.refs_10_.refs_11_.refs_12_.refs_13_.refs_14_.refs_15_.refs_7_.refs_1_, f32[1024,1024]{1,0:T(8,128)} %out_proj.4.refs_2_), custom_call_target="tpu_custom_call" | custom-call | flops 1 | bytes 1 | tf_op jit(solution)/shard_map/out_proj/pallas_call | solution.py:334
  (155 shorter events, 52.3 us)
Async XLA Ops:
  6.5 114.7 %all-gather.5.cloned.1.call-start = ((), (), s32[]{:S(2)}) async-start(), calls=%async_computation | async-start | bytes 7077888 | tf_op jit(solution)/shard_map/all_gather | solution.py:402
  11.2 130.3 %all-gather.7.cloned.1.call-start = ((), (), s32[]{:S(2)}) async-start(), calls=%async_computation.1 | async-start | bytes 7077888 | tf_op jit(solution)/shard_map/all_gather | solution.py:402
  12.5 32.2 %collective-permute-start = (bf16[144,1024]{1,0:T(8,128)(2,1)S(1)}, bf16[144,1024]{1,0:T(8,128)(2,1)S(1)}, u32[]{:S(2)}, u32[]{:S(2)}) collective-permute-start(bf16[144,1024]{1,0:T(8,128)(2,1)S(1)} %maximum_maximum_fusion.refs_8_), channel_id=1, source_target_pairs={{0,1},{1,2},{2,3},{3,0},{4,5},{5,6},{6,7},{7,4},{8,9},{9,10},{10,1... | collective-permute-start | bytes 884744 | tf_op jit(solution)/shard_map/ppermute | solution.py:94
  15.6 29.1 %collective-permute-start.1 = (bf16[144,1024]{1,0:T(8,128)(2,1)S(1)}, bf16[144,1024]{1,0:T(8,128)(2,1)S(1)}, u32[]{:S(2)}, u32[]{:S(2)}) collective-permute-start(bf16[144,1024]{1,0:T(8,128)(2,1)S(1)} %maximum_maximum_fusion.refs_8_), channel_id=1, source_target_pairs={{0,2},{1,3},{2,0},{3,1},{4,6},{5,7},{6,4},{7,5},{8,10},{9,11},{10,... | collective-permute-start | bytes 884744 | tf_op jit(solution)/shard_map/ppermute | solution.py:94
  18.2 26.5 %collective-permute-start.2 = (bf16[144,1024]{1,0:T(8,128)(2,1)S(1)}, bf16[144,1024]{1,0:T(8,128)(2,1)S(1)}, u32[]{:S(2)}, u32[]{:S(2)}) collective-permute-start(bf16[144,1024]{1,0:T(8,128)(2,1)S(1)} %maximum_maximum_fusion.refs_8_), channel_id=1, source_target_pairs={{0,3},{1,0},{2,1},{3,2},{4,7},{5,4},{6,5},{7,6},{8,11},{9,8},{10,9... | collective-permute-start | bytes 884744 | tf_op jit(solution)/shard_map/ppermute | solution.py:94
  44.8 138.4 %all-gather.9.cloned.1.call-start = ((), (), s32[]{:S(2)}) async-start(), calls=%async_computation.2 | async-start | bytes 7077888 | tf_op jit(solution)/shard_map/all_gather | solution.py:402
  45.5 197.1 %all-gather.11.cloned.1.call-start = ((), (), s32[]{:S(2)}) async-start(), calls=%async_computation.3 | async-start | bytes 9437184 | tf_op jit(solution)/shard_map/all_gather | solution.py:402
  46.3 29.0 %collective-permute-start.3 = (bf16[128,3072]{1,0:T(8,128)(2,1)S(1)}, bf16[128,3072]{1,0:T(8,128)(2,1)S(1)}, u32[]{:S(2)}, u32[]{:S(2)}) collective-permute-start(bf16[128,3072]{1,0:T(8,128)(2,1)S(1)} %pad_maximum_fusion.3.refs_0_), channel_id=1, source_target_pairs={{0,8},{4,20},{8,0},{12,28},{16,24},{20,4},{24,16},{28,12},{1,9},{5... | collective-permute-start | bytes 2359304 | tf_op jit(solution)/shard_map/ppermute | solution.py:49
  47.8 27.5 %collective-permute-start.4 = (bf16[128,3072]{1,0:T(8,128)(2,1)S(1)}, bf16[128,3072]{1,0:T(8,128)(2,1)S(1)}, u32[]{:S(2)}, u32[]{:S(2)}) collective-permute-start(bf16[128,3072]{1,0:T(8,128)(2,1)S(1)} %pad_maximum_fusion.3.refs_0_), channel_id=1, source_target_pairs={{0,16},{4,12},{8,24},{12,4},{16,0},{20,28},{24,8},{28,20},{1,17},{... | collective-permute-start | bytes 2359304 | tf_op jit(solution)/shard_map/ppermute | solution.py:49
  49.3 26.0 %collective-permute-start.5 = (bf16[128,3072]{1,0:T(8,128)(2,1)S(1)}, bf16[128,3072]{1,0:T(8,128)(2,1)S(1)}, u32[]{:S(2)}, u32[]{:S(2)}) collective-permute-start(bf16[128,3072]{1,0:T(8,128)(2,1)S(1)} %pad_maximum_fusion.3.refs_0_), channel_id=1, source_target_pairs={{0,4},{4,0},{8,12},{12,8},{16,20},{20,16},{24,28},{28,24},{1,5},{5... | collective-permute-start | bytes 2359304 | tf_op jit(solution)/shard_map/ppermute | solution.py:49
  50.0 25.3 %collective-permute-start.7 = (bf16[64,4096]{1,0:T(8,128)(2,1)S(1)}, bf16[64,4096]{1,0:T(8,128)(2,1)S(1)}, u32[]{:S(2)}, u32[]{:S(2)}) collective-permute-start(bf16[64,4096]{1,0:T(8,128)(2,1)S(1)} %copy-done.23), channel_id=1, source_target_pairs={{0,3},{1,0},{2,1},{3,2},{4,7},{5,4},{6,5},{7,6},{8,11},{9,8},{10,9... | collective-permute-start | bytes 1572872 | tf_op jit(solution)/shard_map/ppermute | solution.py:94
  96.5 39.8 %collective-permute-start.13 = (bf16[512,768]{1,0:T(8,128)(2,1)S(1)}, bf16[512,768]{1,0:T(8,128)(2,1)S(1)}, u32[]{:S(2)}, u32[]{:S(2)}) collective-permute-start(bf16[512,768]{1,0:T(8,128)(2,1)S(1)} %pad_maximum_fusion.2.refs_0_), channel_id=1, source_target_pairs={{0,8},{4,20},{8,0},{12,28},{16,24},{20,4},{24,16},{28,12},{1,9},{5... | collective-permute-start | bytes 2359304 | tf_op jit(solution)/shard_map/ppermute | solution.py:49
  96.5 39.8 %collective-permute-start.14 = (bf16[512,768]{1,0:T(8,128)(2,1)S(1)}, bf16[512,768]{1,0:T(8,128)(2,1)S(1)}, u32[]{:S(2)}, u32[]{:S(2)}) collective-permute-start(bf16[512,768]{1,0:T(8,128)(2,1)S(1)} %pad_maximum_fusion.2.refs_0_), channel_id=1, source_target_pairs={{0,16},{4,12},{8,24},{12,4},{16,0},{20,28},{24,8},{28,20},{1,17},{... | collective-permute-start | bytes 2359304 | tf_op jit(solution)/shard_map/ppermute | solution.py:49
  136.3 28.0 %collective-permute-start.17 = (bf16[512,768]{1,0:T(8,128)(2,1)S(1)}, bf16[512,768]{1,0:T(8,128)(2,1)S(1)}, u32[]{:S(2)}, u32[]{:S(2)}) collective-permute-start(bf16[512,768]{1,0:T(8,128)(2,1)S(1)} %collective-permute-done.13.refs_1_), channel_id=1, source_target_pairs={{0,16},{4,12},{8,24},{12,4},{16,0},{20,28},{24,8},{28,20},{1,17},{... | collective-permute-start | bytes 2359304 | tf_op jit(solution)/shard_map/ppermute | solution.py:49
  137.4 26.9 %collective-permute-start.18 = (bf16[512,768]{1,0:T(8,128)(2,1)S(1)}, bf16[512,768]{1,0:T(8,128)(2,1)}, u32[]{:S(2)}, u32[]{:S(2)}) collective-permute-start(bf16[512,768]{1,0:T(8,128)(2,1)S(1)} %collective-permute-done.13.refs_1_), channel_id=1, source_target_pairs={{0,4},{4,0},{8,12},{12,8},{16,20},{20,16},{24,28},{28,24},{1,5},{5... | collective-permute-start | bytes 2359304 | tf_op jit(solution)/shard_map/ppermute | solution.py:49
  139.0 25.3 %collective-permute-start.16 = (bf16[1024,256]{1,0:T(8,128)(2,1)}, bf16[1024,256]{1,0:T(8,128)(2,1)}, u32[]{:S(2)}, u32[]{:S(2)}) collective-permute-start(bf16[1024,256]{1,0:T(8,128)(2,1)} %heads_2.4.refs_0_), channel_id=1, source_target_pairs={{0,3},{1,0},{2,1},{3,2},{4,7},{5,4},{6,5},{7,6},{8,11},{9,8},{10,9... | collective-permute-start | bytes 1572872 | tf_op jit(solution)/shard_map/ppermute | solution.py:94
  165.7 36.3 %collective-permute-start.22 = (bf16[512,768]{1,0:T(8,128)(2,1)S(1)}, bf16[512,768]{1,0:T(8,128)(2,1)S(1)}, u32[]{:S(2)}, u32[]{:S(2)}) collective-permute-start(bf16[512,768]{1,0:T(8,128)(2,1)S(1)} %pad_maximum_fusion.2.refs_0_), channel_id=1, source_target_pairs={{0,4},{4,0},{8,12},{12,8},{16,20},{20,16},{24,28},{28,24},{1,5},{5... | collective-permute-start | bytes 2359304 | tf_op jit(solution)/shard_map/ppermute | solution.py:49
  165.8 36.3 %collective-permute-start.23 = (bf16[512,768]{1,0:T(8,128)(2,1)S(1)}, bf16[512,768]{1,0:T(8,128)(2,1)}, u32[]{:S(2)}, u32[]{:S(2)}) collective-permute-start(bf16[512,768]{1,0:T(8,128)(2,1)S(1)} %collective-permute-done.14.refs_2_), channel_id=1, source_target_pairs={{0,4},{4,0},{8,12},{12,8},{16,20},{20,16},{24,28},{28,24},{1,5},{5... | collective-permute-start | bytes 2359304 | tf_op jit(solution)/shard_map/ppermute | solution.py:49
  166.3 35.8 %collective-permute-start.24 = (bf16[512,768]{1,0:T(8,128)(2,1)S(1)}, bf16[512,768]{1,0:T(8,128)(2,1)}, u32[]{:S(2)}, u32[]{:S(2)}) collective-permute-start(bf16[512,768]{1,0:T(8,128)(2,1)S(1)} %collective-permute-done.17.refs_3_), channel_id=1, source_target_pairs={{0,4},{4,0},{8,12},{12,8},{16,20},{20,16},{24,28},{28,24},{1,5},{5... | collective-permute-start | bytes 2359304 | tf_op jit(solution)/shard_map/ppermute | solution.py:49
  166.3 31.8 %collective-permute-start.20 = (bf16[1024,256]{1,0:T(8,128)(2,1)}, bf16[1024,256]{1,0:T(8,128)(2,1)}, u32[]{:S(2)}, u32[]{:S(2)}) collective-permute-start(bf16[1024,256]{1,0:T(8,128)(2,1)} %heads_2.5.refs_4_), channel_id=1, source_target_pairs={{0,3},{1,0},{2,1},{3,2},{4,7},{5,4},{6,5},{7,6},{8,11},{9,8},{10,9... | collective-permute-start | bytes 1572872 | tf_op jit(solution)/shard_map/ppermute | solution.py:94
  202.5 27.0 %collective-permute-start.26 = (bf16[1024,256]{1,0:T(8,128)(2,1)}, bf16[1024,256]{1,0:T(8,128)(2,1)S(1)}, u32[]{:S(2)}, u32[]{:S(2)}) collective-permute-start(bf16[1024,256]{1,0:T(8,128)(2,1)} %heads_2.6.refs_0_), channel_id=1, source_target_pairs={{0,3},{1,0},{2,1},{3,2},{4,7},{5,4},{6,5},{7,6},{8,11},{9,8},{10,9... | collective-permute-start | bytes 1572872 | tf_op jit(solution)/shard_map/ppermute | solution.py:94
  205.9 32.8 %collective-permute-start.27 = (bf16[1024,256]{1,0:T(8,128)(2,1)}, bf16[1024,256]{1,0:T(8,128)(2,1)S(1)}, u32[]{:S(2)}, u32[]{:S(2)}) collective-permute-start(bf16[1024,256]{1,0:T(8,128)(2,1)} %collective-permute-done.19.refs_5_), channel_id=1, source_target_pairs={{0,1},{1,2},{2,3},{3,0},{4,5},{5,6},{6,7},{7,4},{8,9},{9,10},{10,1... | collective-permute-start | bytes 1572872 | tf_op jit(solution)/shard_map/ppermute | solution.py:94
  238.8 27.4 %collective-permute-start.29 = (bf16[1024,256]{1,0:T(8,128)(2,1)}, bf16[1024,256]{1,0:T(8,128)(2,1)S(1)}, u32[]{:S(2)}, u32[]{:S(2)}) collective-permute-start(bf16[1024,256]{1,0:T(8,128)(2,1)} %heads_2.7.refs_4_), channel_id=1, source_target_pairs={{0,3},{1,0},{2,1},{3,2},{4,7},{5,4},{6,5},{7,6},{8,11},{9,8},{10,9... | collective-permute-start | bytes 1572872 | tf_op jit(solution)/shard_map/ppermute | solution.py:94
  242.6 31.9 %collective-permute-start.30 = (bf16[1024,256]{1,0:T(8,128)(2,1)S(1)}, bf16[1024,256]{1,0:T(8,128)(2,1)S(1)}, u32[]{:S(2)}, u32[]{:S(2)}) collective-permute-start(bf16[1024,256]{1,0:T(8,128)(2,1)S(1)} %collective-permute-done.25.refs_1_), channel_id=1, source_target_pairs={{0,1},{1,2},{2,3},{3,0},{4,5},{5,6},{6,7},{7,4},{8,9},{9,10},{10,1... | collective-permute-start | bytes 1572872 | tf_op jit(solution)/shard_map/ppermute | solution.py:94
  (41 other events, 628.9 us)
Sparse Core Ops, SparseCore 0:
  11.3 57.1 all-gather.4
  70.4 64.8 all-gather.6
  137.2 45.8 all-gather.8
  184.9 54.3 all-gather.10

commit v3 on v2

--- a/solution.py
+++ b/solution.py
@@ -31,18 +31,6 @@
         offsets = offsets + [t ^ bit for t in offsets]
         bit //= 2
     return [offsets] * rows
-
-
-def row_slots(rows):
-    slots = np.zeros((rows, rows), np.int32)
-    for r, offsets in enumerate(row_offsets(rows)):
-        for place, offset in enumerate(offsets):
-            slots[r, r ^ offset] = place
-    return slots
-
-
-def row_sources(rows):
-    return np.array([[r ^ t for t in row] for r, row in enumerate(row_offsets(rows))], np.int32)
 
 
 def swap(x, pairs):
@@ -116,7 +104,53 @@
     return far_cols(near_cols(x, cols), cols)
 
 
-def place_kernel(parts, ids_ref, *refs):
+def pack_kernel(count, *refs):
+    for k in range(len(refs) // (count + 1)):
+        out_ref = refs[len(refs) * count // (count + 1) + k]
+        width = out_ref.shape[1] // count
+        for j in range(count):
+            out_ref[:, j * width : (j + 1) * width] = refs[k * count + j][...]
+
+
+def pack(weights, chunks):
+    depth = weights[0].shape[0]
+    in_specs, out_specs, shapes = [], [], []
+    for low, size in chunks:
+        width = size * HEAD_DIM
+        spec = pl.BlockSpec((depth, width), lambda i, at=low // size: (0, at))
+        in_specs += [spec] * len(weights)
+        wide = (depth, width * len(weights))
+        out_specs.append(pl.BlockSpec(wide, lambda i: (0, 0)))
+        shapes.append(jax.ShapeDtypeStruct(wide, BF))
+    return pl.pallas_call(
+        functools.partial(pack_kernel, len(weights)),
+        out_shape=shapes,
+        grid=(1,),
+        in_specs=in_specs,
+        out_specs=out_specs,
+        compiler_params=pltpu.CompilerParams(vmem_limit_bytes=VMEM),
+        cost_estimate=LIGHT,
+        name="pack",
+    )(*(list(weights) * len(chunks)))
+
+
+def attend(projected, heads, out_ref):
+    hw = heads * HEAD_DIM
+    scale = HEAD_DIM**-0.5
+    cut = lambda j, h: projected[:, j * hw + h * HEAD_DIM : j * hw + (h + 1) * HEAD_DIM]
+    scores = [
+        lax.dot_general(
+            cut(0, h), cut(1, h), (((1,), (1,)), ((), ())), preferred_element_type=F32
+        ) * scale
+        for h in range(heads)
+    ]
+    raised = [jnp.exp(s - jnp.max(s, axis=1, keepdims=True)) for s in scores]
+    probs = [(e * (1.0 / jnp.sum(e, axis=1, keepdims=True))).astype(BF) for e in raised]
+    out = [jnp.dot(p, cut(2, h), preferred_element_type=F32) for h, p in enumerate(probs)]
+    out_ref[...] = jnp.concatenate(out, axis=1).astype(BF)
+
+
+def place_kernel(parts, column_of_ids, ids_ref, *refs):
     tables, out_ref, held = refs[: sum(parts)], refs[-2], refs[-1]
     width = out_ref.shape[1]
 
@@ -132,7 +166,8 @@
             column += block.shape[1]
 
     wide = lax.broadcasted_iota(jnp.int32, (L, held.shape[0]), 1)
-    pick = jnp.where(wide == ids_ref[...], 1.0, 0.0).astype(BF)
+    ids = ids_ref[:, column_of_ids : column_of_ids + 1]
+    pick = jnp.where(wide == ids, 1.0, 0.0).astype(BF)
     step = min(width, 1024)
     for low in range(0, width, step):
         out_ref[:, low : low + step] = jnp.dot(
@@ -140,16 +175,16 @@
         ).astype(BF)
 
 
-def place(ids, *tables):
+def place(ids, which, *tables):
     tokens = ids.shape[0]
     positions = sum(t.shape[0] for t in tables[0])
     width = sum(t[0].shape[1] for t in tables)
     operands = [t for table in tables for t in table]
     return pl.pallas_call(
-        functools.partial(place_kernel, [len(t) for t in tables]),
+        functools.partial(place_kernel, [len(t) for t in tables], which),
         out_shape=jax.ShapeDtypeStruct((tokens, width), BF),
         grid=(tokens // L,),
-        in_specs=[pl.BlockSpec((L, 1), lambda i: (i, 0))]
+        in_specs=[pl.BlockSpec((L, ids.shape[1]), lambda i: (i, 0))]
         + [pl.BlockSpec(t.shape, lambda i: (0, 0)) for t in operands],
         out_specs=pl.BlockSpec((L, width), lambda i: (i, 0)),
         scratch_shapes=[pltpu.VMEM((positions, width), BF)],
@@ -160,9 +195,9 @@
 
 
 def norm_kernel(cols, part, n_late, col_ref, keep_ref, ids_ref, own_ref, near_ref, *refs):
-    late, refs = refs[:n_late], refs[n_late:]
+    late, weights, refs = refs[:n_late], refs[n_late], refs[n_late + 1 :]
     encs, shares = refs[:cols], refs[cols : 2 * cols]
-    out_ref, extra, table, held = refs[2 * cols :]
+    out_ref, attended_ref, extra, table, held = refs[2 * cols :]
     image = pl.program_id(0)
     width = held.shape[2]
     vis = encs[0].shape[0]
@@ -189,25 +224,27 @@
     hidden = 1.0 - jnp.max(seen, axis=1, keepdims=True)
     lane = lax.broadcasted_iota(jnp.int32, (L, 128), 1)
     wide = lax.broadcasted_iota(jnp.int32, (L, n_late * part), 1)
-    rest = jnp.where(wide == ids_ref[...], 1.0, 0.0)
+    rest = jnp.where(wide == ids_ref[:, 2:3], 1.0, 0.0)
     pick = jnp.concatenate([seen, jnp.where(lane == 1, hidden, 0.0), rest], axis=1).astype(BF)
-    ones = jnp.ones((width, 128), BF)
-    total = jnp.zeros((L, 128), F32)
-    squares = jnp.zeros((L, 1), F32)
-    for k in range(cols):
+    def filled(k):
         at = col_ref[k]
         if k == 0:
-            x = jnp.dot(pick[:, :base], table[at, :base, :], preferred_element_type=F32)
-            x = x + own_ref[...].astype(F32)
-        else:
-            x = jnp.dot(pick, table[at], preferred_element_type=F32)
-            x = x + near_ref[:, (k - 1) * width : k * width].astype(F32)
-        xb = x.astype(BF)
+            return jnp.dot(pick[:, :base], table[at, :base, :], preferred_element_type=F32)
+        return jnp.dot(pick, table[at], preferred_element_type=F32)
+
+    squares = jnp.zeros((L, 1), F32)
+    total = jnp.zeros((L, 1), F32)
+    products = [filled(0)]
+    for k in range(cols):
+        if k + 1 < cols:
+            products.append(filled(k + 1))
+        placed = own_ref[...] if k == 0 else near_ref[:, (k - 1) * width : k * width]
+        xb = (products[k] + placed.astype(F32)).astype(BF)
         held[k] = xb
-        total = total + jnp.dot(xb, ones, preferred_element_type=F32)
         x = xb.astype(F32)
+        total = total + jnp.sum(x, axis=1, keepdims=True)
         squares = squares + jnp.sum(x * x, axis=1, keepdims=True)
-    mean = total[:, :1] / (cols * width)
+    mean = total / (cols * width)
     var = squares / (cols * width) - mean * mean
     scale = lax.rsqrt(var + EPS)
     for k in range(cols):
@@ -216,9 +253,11 @@
         out_ref[:, pl.ds(low, width)] = (
             (x - mean) * scale * extra[k, 0:1, :].astype(F32)
         ).astype(BF)
-
-
-def fill_and_norm(part, order, keep, ids, own, near, late, encs, shares):
+    projected = jnp.dot(out_ref[...], weights[...], preferred_element_type=F32)
+    attend(projected.astype(BF), weights.shape[1] // (3 * HEAD_DIM), attended_ref)
+
+
+def fill_and_norm(part, order, keep, ids, own, near, late, weights, encs, shares):
     tokens, width = own.shape
     cols = len(encs)
     vis = encs[0].shape[0]
@@ -226,38 +265,30 @@
     row = lambda i, *_: (i, 0)
     return pl.pallas_call(
         functools.partial(norm_kernel, cols, part, len(late)),
-        out_shape=jax.ShapeDtypeStruct((tokens, cols * width), BF),
+        out_shape=[
+            jax.ShapeDtypeStruct((tokens, cols * width), BF),
+            jax.ShapeDtypeStruct((tokens, weights.shape[1] // 3), BF),
+        ],
         grid_spec=pltpu.PrefetchScalarGridSpec(
             num_scalar_prefetch=1,
             grid=(tokens // L,),
             in_specs=[whole(keep)]
             + [pl.BlockSpec((L, p.shape[1]), row) for p in (ids, own, near)]
-            + [whole(a) for a in late + encs + shares],
-            out_specs=pl.BlockSpec((L, cols * width), row),
+            + [whole(a) for a in late + [weights] + encs + shares],
+            out_specs=[
+                pl.BlockSpec((L, cols * width), row),
+                pl.BlockSpec((L, weights.shape[1] // 3), row),
+            ],
             scratch_shapes=[
                 pltpu.VMEM((cols, 16, width), BF),
                 pltpu.VMEM((cols, cols * vis + 128 + len(late) * part, width), BF),
                 pltpu.VMEM((cols, L, width), BF),
             ],
         ),
-        compiler_params=pltpu.CompilerParams(vmem_limit_bytes=VMEM),
+        compiler_params=pltpu.CompilerParams(vmem_limit_bytes=50 * MIB),
         cost_estimate=LIGHT,
         name="fill_norm",
-    )(order, keep, ids, own, near, *late, *encs, *shares)
-
-
-def attend(projected, heads, out_ref):
-    hw = heads * HEAD_DIM
-    scale = HEAD_DIM**-0.5
-    for h in range(heads):
-        cut = lambda j: projected[:, j * hw + h * HEAD_DIM : j * hw + (h + 1) * HEAD_DIM]
-        s = lax.dot_general(
-            cut(0), cut(1), (((1,), (1,)), ((), ())), preferred_element_type=F32
-        ) * scale
-        e = jnp.exp(s - jnp.max(s, axis=1, keepdims=True))
-        p = (e / jnp.sum(e, axis=1, keepdims=True)).astype(BF)
-        o = jnp.dot(p, cut(2), preferred_element_type=F32)
-        out_ref[:, h * HEAD_DIM : (h + 1) * HEAD_DIM] = o.astype(BF)
+    )(order, keep, ids, own, near, *late, weights, *encs, *shares)
 
 
 def heads_kernel(heads, source_ref, x_ref, *refs):
@@ -341,7 +372,7 @@
             out_specs=pl.BlockSpec((L, width), row),
         ),
         input_output_aliases=alias,
-        compiler_params=pltpu.CompilerParams(vmem_limit_bytes=VMEM),
+        compiler_params=pltpu.CompilerParams(vmem_limit_bytes=40 * MIB),
         cost_estimate=LIGHT,
         name="out_proj",
     )(order, *operands)
@@ -361,36 +392,34 @@
     images = keep.shape[0]
     positions, width = pos_table.shape
     r, c = lax.axis_index("row"), lax.axis_index("col")
-    slot = jnp.asarray(row_slots(rows))[r]
     order = (c - jnp.arange(cols, dtype=jnp.int32)) % cols
     chunks = head_chunks(width // HEAD_DIM)
     n = len(chunks)
 
-    def packed(k):
-        low, size = chunks[k]
-        cut = slice(low * HEAD_DIM, (low + size) * HEAD_DIM)
-        return jnp.concatenate([w_query[:, cut], w_key[:, cut], w_value[:, cut]], axis=1)
+    projections = (w_query, w_key, w_value)
 
     part = positions // rows
     owner, inner = pos_ids // part, pos_ids % part
     early = early_places(rows)
     later = [p for p in range(rows) if p not in early]
 
+    offsets = row_offsets(rows)
+    sources = [r ^ jnp.where(r % 2 == 1, odd, even) for even, odd in zip(offsets[0], offsets[1])]
+
     def ids_of(places):
-        rank = np.full((rows,), -rows, np.int32)
-        rank[places] = np.arange(len(places))
-        rank = jnp.asarray(rank[row_slots(rows)])[r]
-        ids = inner
-        for b in range(rows):
-            ids = ids + jnp.where(owner == b, rank[b] * part, 0)
+        ids = inner - positions
+        for i, p in enumerate(places):
+            ids = ids + jnp.where(owner == sources[p], positions + i * part, 0)
         return ids.reshape(images * L, 1)
 
+    lane = lax.broadcasted_iota(jnp.int32, (images * L, 128), 1)
+    own_ids = pos_ids.reshape(images * L, 1)
+    ids = jnp.where(lane == 0, own_ids, jnp.where(lane == 1, ids_of(early), ids_of(later)))
+
     small = (
-        pos_ids.reshape(images * L, 1),
-        ids_of(early),
-        ids_of(later),
+        ids,
         (keep + L * jnp.arange(images, dtype=jnp.int32)[:, None]).reshape(cols, -1)[order].reshape(1, -1),
-        jnp.asarray(row_sources(rows))[r],
+        jnp.stack(sources).astype(jnp.int32),
         order,
     )
 
@@ -401,36 +430,35 @@
 
     gather = lambda w: lax.all_gather(w, "row", axis=0, tiled=True)
     split = rows == 8 and n >= 4
-    weights = [[gather(packed(0))]]
+    weights = [[gather(pack(projections, chunks[:1])[0])]]
     shares = [share] + [shift(share, cols, k) for k in others]
-    placed_own = place(small[0], [pos_table])
-    packs = [packed(k) for k in range(1, n)]
+    packs = list(pack(projections, chunks[1:]))
+    placed_own = place(ids, 0, [pos_table])
     shares, placed_own, enc, packs, w_out, small = gate(
         shares, placed_own, enc_out, packs, w_out, small
     )
-    _, early_ids, later_ids, numbers, source, order = small
+    ids, numbers, source, order = small
 
     weights += [[gather(p)] for p in (packs[:-1] if split else packs)]
     w_full = gather(w_out)
     late = Rows(packs[-1], rows)
 
     table = Rows(jnp.concatenate([shares[k][:part] for k in others], axis=1), rows)
+    encs = near_cols(enc, cols)
     table.start()
-    encs = near_cols(enc, cols)
     table.parts, encs = gate(table.parts, encs)
 
     encs = far_cols(encs, cols)
     table.forward()
-    placed = place(early_ids, table.blocks(early))
+    placed = place(ids, 1, table.blocks(early))
     table.parts, encs, placed = gate(table.parts, encs, placed)
 
     table.finish()
     if split:
         late.fetch(1, 2)
-    normed = fill_and_norm(
-        part, order, numbers, later_ids, placed_own, placed, table.blocks(later), encs, shares
+    normed, attended = fill_and_norm(
+        part, order, numbers, ids, placed_own, placed, table.blocks(later), weights[0][0], encs, shares
     )
-    attended = some_heads(source, normed, weights[0], chunks[0][1])
     attended, normed, late.parts = gate(attended, normed, late.parts)
 
     sent, half = [], None

time: 300 us -> 293 us (0.977)
  starting transfers between devices: 34.8 us -> 49.7 us
  Pallas kernels: 122 us -> 110 us
  between operations: 23.7 us -> 13.4 us
  waiting for transfers between devices: 98.5 us -> 108 us
  local copies, waits for them, and re-layouts: 16 us -> 8.74 us
    pallas_call x4 -> x3, Pallas kernels: 61.2 us -> 42.1 us  [some_heads(): pl.pallas_call(functools.partial(heads_kernel, heads), out_shape=jax.Shap...]
    ppermute x18, starting transfers between devices: 27.7 us -> 41.6 us  [shift(): return lax.ppermute(x, 'col', [(c, (c + step) % cols) for c in range(cols)])]
    ppermute x18, waiting for transfers between devices: 92.2 us -> 104 us  [shift(): return lax.ppermute(x, 'col', [(c, (c + step) % cols) for c in range(cols)])]
    pallas_call x1, Pallas kernels: 21.4 us -> 30.2 us  [fill_and_norm(): pl.pallas_call(functools.partial(norm_kernel, cols, part, len(late)), out...]
    pallas_call x3, Pallas kernels: 25.7 us -> 19.1 us  [project(): pl.pallas_call(functools.partial(out_kernel, n, acc is not None), out_sha...]
    slice x5 -> x0, local copies, waits for them, and re-layouts: 5.03 us -> none  [the longest x1 2.12 us: packed(): w_query[:, cut]]
    pallas_call x2 -> x4, Pallas kernels: 14.1 us -> 19.1 us  [the longest x2 13.6 us: place(): pl.pallas_call(functools.partial(place_kernel, [len(t) for t in tables],...]
    concatenate x3 -> x0, other arithmetic: 3.51 us -> none  [packed(): jnp.concatenate([w_query[:, cut], w_key[:, cut], w_value[:, cut]], axis=1)]
  transfers between devices with their start and end apart: 36 -> 36, of which waited for: 15 -> 15; matrix products, arithmetic and copies ran while one was open for 4% -> 1% of each run, Pallas kernels for 39% -> 36%
where the time goes in v3:
time: 293 us
  Pallas kernels  110 us (38%)
  waiting for transfers between devices  108 us (37%)
  starting transfers between devices  49.7 us (17%)
  between operations  13.4 us (5%)
  local copies, waits for them, and re-layouts  8.74 us (3%)
    ppermute x18, waiting for transfers between devices, shift(): return lax.ppermute(x, 'col', [(c, (c + step) % cols) for c in range(cols)])  104 us
    pallas_call x3, Pallas kernels, some_heads(): pl.pallas_call(functools.partial(heads_kernel, heads), out_shape=jax.Shap...  42.1 us
    ppermute x18, starting transfers between devices, shift(): return lax.ppermute(x, 'col', [(c, (c + step) % cols) for c in range(cols)])  41.6 us
    pallas_call x1, Pallas kernels, fill_and_norm(): pl.pallas_call(functools.partial(norm_kernel, cols, part, len(late)), out...  30.2 us
    pallas_call x3, Pallas kernels, project(): pl.pallas_call(functools.partial(out_kernel, n, acc is not None), out_sha...  19.1 us
    pallas_call x2, Pallas kernels, place(): pl.pallas_call(functools.partial(place_kernel, [len(t) for t in tables],...  13.6 us
    ppermute x14, starting transfers between devices, swap(): return lax.ppermute(x, 'row', pairs)  7.93 us
    unnamed x47, local copies, waits for them, and re-layouts  6.41 us
  transfers between devices with their start and end apart: 36, of which 15 were waited for; matrix products, arithmetic and copies ran while one was open for 1% of the time, Pallas kernels for 36%

profile of v3, /device:TPU:0, one launch (start us, length us, event | category | flops | bytes accessed | tf_op | source)
XLA Modules:
  0.0 292.5 jit_solution(17729638179099507748)
XLA Ops:
  18.4 3.4 %pack.2 = (bf16[512,768]{1,0:T(8,128)(2,1)}, bf16[512,768]{1,0:T(8,128)(2,1)}, bf16[512,768]{1,0:T(8,128)(2,1)}) custom-call(bf16[512,1024]{1,0:T(8,128)(2,1)} %refs_0_.5, bf16[512,1024]{1,0:T(8,128)(2,1)} %refs_1_.3, bf16[512,1024]{1,0:T(8,128)(2,1)} %refs_2_.3, bf16[512,1024]{1,0:T(8,128)(2,1)} %refs_0_.5, bf16[512,1024]{1,0:T(8,128)(2,1)} %refs_1_.3, ...), custom_call_target="tpu_custom_call" | custom-call | flops 1 | bytes 1 | tf_op jit(solution)/shard_map/pack/pallas_call | solution.py:125
  21.8 6.0 %place.2.own_ref = bf16[1024,1024]{1,0:T(8,128)(2,1)} custom-call(s32[1024,128]{1,0:T(8,128)} %select_select_fusion.ids_ref, bf16[1024,1024]{1,0:T(8,128)(2,1)} %refs_0_.3), custom_call_target="tpu_custom_call" | custom-call | flops 1 | bytes 1 | tf_op jit(solution)/shard_map/place/pallas_call | solution.py:183
  29.2 5.6 %collective-permute-done.1.refs_11_ = bf16[144,1024]{1,0:T(8,128)(2,1)S(1)} collective-permute-done((bf16[144,1024]{1,0:T(8,128)(2,1)S(1)}, bf16[144,1024]{1,0:T(8,128)(2,1)S(1)}, u32[]{:S(2)}, u32[]{:S(2)}) %collective-permute-start.1) | collective-permute-done | bytes 294944 | tf_op jit(solution)/shard_map/ppermute | solution.py:82
  39.4 6.8 %collective-permute-start.6 = (bf16[64,4096]{1,0:T(8,128)(2,1)S(1)}, bf16[64,4096]{1,0:T(8,128)(2,1)S(1)}, u32[]{:S(2)}, u32[]{:S(2)}) collective-permute-start(bf16[64,4096]{1,0:T(8,128)(2,1)S(1)} %copy-done.11), channel_id=1, source_target_pairs={{0,1},{1,2},{2,3},{3,0},{4,5},{5,6},{6,7},{7,4},{8,9},{9,10},{10,1... | collective-permute-start | bytes 1572872 | tf_op jit(solution)/shard_map/ppermute | solution.py:82
  47.3 12.8 %collective-permute-done.6.refs_6_ = bf16[64,4096]{1,0:T(8,128)(2,1)S(1)} collective-permute-done((bf16[64,4096]{1,0:T(8,128)(2,1)S(1)}, bf16[64,4096]{1,0:T(8,128)(2,1)S(1)}, u32[]{:S(2)}, u32[]{:S(2)}) %collective-permute-start.6) | collective-permute-done | bytes 524320 | tf_op jit(solution)/shard_map/ppermute | solution.py:82
  60.0 11.0 %collective-permute-done.7.refs_8_ = bf16[64,4096]{1,0:T(8,128)(2,1)S(1)} collective-permute-done((bf16[64,4096]{1,0:T(8,128)(2,1)S(1)}, bf16[64,4096]{1,0:T(8,128)(2,1)S(1)}, u32[]{:S(2)}, u32[]{:S(2)}) %collective-permute-start.7) | collective-permute-done | bytes 524320 | tf_op jit(solution)/shard_map/ppermute | solution.py:82
  75.8 7.6 %place.3.near_ref = bf16[1024,3072]{1,0:T(8,128)(2,1)} custom-call(s32[1024,128]{1,0:T(8,128)} %select_select_fusion.ids_ref, bf16[128,3072]{1,0:T(8,128)(2,1)} %copy-done.14, bf16[128,3072]{1,0:T(8,128)(2,1)} %collective-permute-done.3.refs_1_, bf16[128,3072]{1,0:T(8,128)(2,1)} %collective-permute-done.4.refs_2_, bf16[128,3072]{1,0:T(8,128)(2,1)} %copy-done.16), custom_call_target="tpu_custom_call" | custom-call | flops 1 | bytes 1 | tf_op jit(solution)/shard_map/place/pallas_call | solution.py:183
  83.4 7.0 %collective-permute-done.11.refs_7_ = bf16[64,4096]{1,0:T(8,128)(2,1)S(1)} collective-permute-done((bf16[64,4096]{1,0:T(8,128)(2,1)S(1)}, bf16[64,4096]{1,0:T(8,128)(2,1)S(1)}, u32[]{:S(2)}, u32[]{:S(2)}) %collective-permute-start.11) | collective-permute-done | bytes 524320 | tf_op jit(solution)/shard_map/ppermute | solution.py:82
  94.9 30.2 %fill_norm.1 = (bf16[1024,4096]{1,0:T(8,128)(2,1)}, bf16[1024,256]{1,0:T(8,128)(2,1)S(1)}) custom-call(s32[4]{0:T(128)S(1)} %and_select_fusion.col_ref.at_ref, s32[1,256]{1,0:T(1,128)S(1)} %reshape.63.keep_ref, s32[1024,128]{1,0:T(8,128)S(1)} %copy-done.1, bf16[1024,1024]{1,0:T(8,128)(2,1)} %place.2.own_ref, bf16[1024,3072]{1,0:T(8,128)(2,1)} %place.3.near_ref, ...), custom_call_target="tpu_custom_call" | custom-call | flops 1 | bytes 1 | tf_op jit(solution)/shard_map/fill_norm/pallas_call | solution.py:266
  125.8 3.8 %collective-permute-start.16 = (bf16[1024,256]{1,0:T(8,128)(2,1)S(1)}, bf16[1024,256]{1,0:T(8,128)(2,1)S(1)}, u32[]{:S(2)}, u32[]{:S(2)}) collective-permute-start(bf16[1024,256]{1,0:T(8,128)(2,1)S(1)} %get-tuple-element.152.refs_0_), channel_id=1, source_target_pairs={{0,3},{1,0},{2,1},{3,2},{4,7},{5,4},{6,5},{7,6},{8,11},{9,8},{10,9... | collective-permute-start | bytes 1572872 | tf_op jit(solution)/shard_map/ppermute | solution.py:82
  130.3 13.9 %heads_2.3.refs_4_ = bf16[1024,256]{1,0:T(8,128)(2,1)} custom-call(s32[8]{0:T(128)} %stack.35.source_ref, bf16[1024,4096]{1,0:T(8,128)(2,1)} %get-tuple-element.135.x_ref, bf16[4096,768]{1,0:T(8,128)(2,1)} %all-gather.7.cloned.1.call-done.refs_0_), custom_call_target="tpu_custom_call" | custom-call | flops 1 | bytes 1 | tf_op jit(solution)/shard_map/heads_2/pallas_call | solution.py:311
  144.2 7.2 %collective-permute-done.16.refs_3_ = bf16[1024,256]{1,0:T(8,128)(2,1)S(1)} collective-permute-done((bf16[1024,256]{1,0:T(8,128)(2,1)S(1)}, bf16[1024,256]{1,0:T(8,128)(2,1)S(1)}, u32[]{:S(2)}, u32[]{:S(2)}) %collective-permute-start.16) | collective-permute-done | bytes 524320 | tf_op jit(solution)/shard_map/ppermute | solution.py:82
  155.7 12.6 %collective-permute-done.19.refs_5_ = bf16[1024,256]{1,0:T(8,128)(2,1)} collective-permute-done((bf16[1024,256]{1,0:T(8,128)(2,1)}, bf16[1024,256]{1,0:T(8,128)(2,1)}, u32[]{:S(2)}, u32[]{:S(2)}) %collective-permute-start.19) | collective-permute-done | bytes 524320 | tf_op jit(solution)/shard_map/ppermute | solution.py:82
  168.4 8.7 %collective-permute-start.21 = (bf16[1024,256]{1,0:T(8,128)(2,1)S(1)}, bf16[1024,256]{1,0:T(8,128)(2,1)S(1)}, u32[]{:S(2)}, u32[]{:S(2)}) collective-permute-start(bf16[1024,256]{1,0:T(8,128)(2,1)S(1)} %collective-permute-done.15.refs_1_), channel_id=1, source_target_pairs={{0,1},{1,2},{2,3},{3,0},{4,5},{5,6},{6,7},{7,4},{8,9},{9,10},{10,1... | collective-permute-start | bytes 1572872 | tf_op jit(solution)/shard_map/ppermute | solution.py:82
  177.1 13.9 %heads_2.4.refs_0_ = bf16[1024,256]{1,0:T(8,128)(2,1)} custom-call(s32[8]{0:T(128)} %stack.35.source_ref, bf16[1024,4096]{1,0:T(8,128)(2,1)} %get-tuple-element.135.x_ref, bf16[4096,768]{1,0:T(8,128)(2,1)} %all-gather.9.cloned.1.call-done.refs_0_), custom_call_target="tpu_custom_call" | custom-call | flops 1 | bytes 1 | tf_op jit(solution)/shard_map/heads_2/pallas_call | solution.py:311
  197.6 14.3 %heads_2.5.refs_4_ = bf16[1024,256]{1,0:T(8,128)(2,1)} custom-call(s32[8]{0:T(128)} %stack.35.source_ref, bf16[1024,4096]{1,0:T(8,128)(2,1)} %get-tuple-element.135.x_ref, bf16[512,768]{1,0:T(8,128)(2,1)} %get-tuple-element.136.refs_0_, bf16[512,768]{1,0:T(8,128)(2,1)} %collective-permute-done.13.refs_1_, bf16[512,768]{1,0:T(8,128)(2,1)} %collective-permute-done.14.refs_2_, ...), custom_call_target="tpu_custom_call" | custom-call | flops 1 | bytes 1 | tf_op jit(solution)/shard_map/heads_2/pallas_call | solution.py:311
  212.0 7.6 %collective-permute-done.26.refs_3_ = bf16[1024,256]{1,0:T(8,128)(2,1)S(1)} collective-permute-done((bf16[1024,256]{1,0:T(8,128)(2,1)}, bf16[1024,256]{1,0:T(8,128)(2,1)S(1)}, u32[]{:S(2)}, u32[]{:S(2)}) %collective-permute-start.26) | collective-permute-done | bytes 524320 | tf_op jit(solution)/shard_map/ppermute | solution.py:82
  220.4 10.7 %collective-permute-done.27.refs_6_ = bf16[1024,256]{1,0:T(8,128)(2,1)} collective-permute-done((bf16[1024,256]{1,0:T(8,128)(2,1)}, bf16[1024,256]{1,0:T(8,128)(2,1)}, u32[]{:S(2)}, u32[]{:S(2)}) %collective-permute-start.27) | collective-permute-done | bytes 524320 | tf_op jit(solution)/shard_map/ppermute | solution.py:82
  231.1 3.8 %collective-permute-start.29 = (bf16[1024,256]{1,0:T(8,128)(2,1)}, bf16[1024,256]{1,0:T(8,128)(2,1)}, u32[]{:S(2)}, u32[]{:S(2)}) collective-permute-start(bf16[1024,256]{1,0:T(8,128)(2,1)} %heads_2.5.refs_4_), channel_id=1, source_target_pairs={{0,3},{1,0},{2,1},{3,2},{4,7},{5,4},{6,5},{7,6},{8,11},{9,8},{10,9... | collective-permute-start | bytes 1572872 | tf_op jit(solution)/shard_map/ppermute | solution.py:82
  237.0 8.2 %out_proj.3.refs_14_ = f32[1024,1024]{1,0:T(8,128)S(1)} custom-call(s32[4]{0:T(128)S(1)} %and_select_fusion.col_ref.at_ref, bf16[1024,256]{1,0:T(8,128)(2,1)S(1)} %get-tuple-element.152.refs_0_, bf16[1024,256]{1,0:T(8,128)(2,1)S(1)} %collective-permute-done.15.refs_1_, bf16[1024,256]{1,0:T(8,128)(2,1)S(1)} %copy-done.8, ...), custom_call_target="tpu_custom_call" | custom-call | flops 1 | bytes 1 | tf_op jit(solution)/shard_map/out_proj/pallas_call | solution.py:365
  248.1 7.6 %collective-permute-done.29.refs_6_ = bf16[1024,256]{1,0:T(8,128)(2,1)} collective-permute-done((bf16[1024,256]{1,0:T(8,128)(2,1)}, bf16[1024,256]{1,0:T(8,128)(2,1)}, u32[]{:S(2)}, u32[]{:S(2)}) %collective-permute-start.29) | collective-permute-done | bytes 524320 | tf_op jit(solution)/shard_map/ppermute | solution.py:82
  255.7 13.1 %collective-permute-done.30.refs_2_ = bf16[1024,256]{1,0:T(8,128)(2,1)} collective-permute-done((bf16[1024,256]{1,0:T(8,128)(2,1)}, bf16[1024,256]{1,0:T(8,128)(2,1)}, u32[]{:S(2)}, u32[]{:S(2)}) %collective-permute-start.30) | collective-permute-done | bytes 524320 | tf_op jit(solution)/shard_map/ppermute | solution.py:82
  268.8 7.9 %out_proj.4.refs_2_ = f32[1024,1024]{1,0:T(8,128)S(1)} custom-call(s32[4]{0:T(128)S(1)} %and_select_fusion.col_ref.at_ref, bf16[1024,256]{1,0:T(8,128)(2,1)S(1)} %copy-done.3, bf16[1024,256]{1,0:T(8,128)(2,1)} %collective-permute-done.25.refs_1_, bf16[1024,256]{1,0:T(8,128)(2,1)} %collective-permute-done.30.refs_2_, ...), custom_call_target="tpu_custom_call", output_to_operand_aliasing={{}: (15, {})} | custom-call | flops 1 | bytes 1 | tf_op jit(solution)/shard_map/out_proj/pallas_call | solution.py:365
  276.7 6.2 %collective-permute-done.31.refs_0_ = bf16[1024,256]{1,0:T(8,128)(2,1)S(1)} collective-permute-done((bf16[1024,256]{1,0:T(8,128)(2,1)}, bf16[1024,256]{1,0:T(8,128)(2,1)S(1)}, u32[]{:S(2)}, u32[]{:S(2)}) %collective-permute-start.31) | collective-permute-done | bytes 524320 | tf_op jit(solution)/shard_map/ppermute | solution.py:82
  (131 shorter events, 49.2 us)
Async XLA Ops:
  6.5 87.4 %all-gather.5.cloned.1.call-start = ((), (), s32[]{:S(2)}) async-start(), calls=%async_computation | async-start | bytes 7077888 | tf_op jit(solution)/shard_map/all_gather | solution.py:431
  8.6 121.6 %all-gather.7.cloned.1.call-start = ((), (), s32[]{:S(2)}) async-start(), calls=%async_computation.1 | async-start | bytes 7077888 | tf_op jit(solution)/shard_map/all_gather | solution.py:431
  13.0 21.8 %collective-permute-start.1 = (bf16[144,1024]{1,0:T(8,128)(2,1)S(1)}, bf16[144,1024]{1,0:T(8,128)(2,1)S(1)}, u32[]{:S(2)}, u32[]{:S(2)}) collective-permute-start(bf16[144,1024]{1,0:T(8,128)(2,1)S(1)} %maximum_maximum_fusion.refs_9_), channel_id=1, source_target_pairs={{0,2},{1,3},{2,0},{3,1},{4,6},{5,7},{6,4},{7,5},{8,10},{9,11},{10,... | collective-permute-start | bytes 884744 | tf_op jit(solution)/shard_map/ppermute | solution.py:82
  34.8 142.2 %all-gather.9.cloned.1.call-start = ((), (), s32[]{:S(2)}) async-start(), calls=%async_computation.2 | async-start | bytes 7077888 | tf_op jit(solution)/shard_map/all_gather | solution.py:431
  35.6 199.4 %all-gather.11.cloned.1.call-start = ((), (), s32[]{:S(2)}) async-start(), calls=%async_computation.3 | async-start | bytes 9437184 | tf_op jit(solution)/shard_map/all_gather | solution.py:431
  36.3 36.2 %collective-permute-start.3 = (bf16[128,3072]{1,0:T(8,128)(2,1)S(1)}, bf16[128,3072]{1,0:T(8,128)(2,1)}, u32[]{:S(2)}, u32[]{:S(2)}) collective-permute-start(bf16[128,3072]{1,0:T(8,128)(2,1)S(1)} %pad_maximum_fusion.refs_0_), channel_id=1, source_target_pairs={{0,8},{4,20},{8,0},{12,28},{16,24},{20,4},{24,16},{28,12},{1,9},{5... | collective-permute-start | bytes 2359304 | tf_op jit(solution)/shard_map/ppermute | solution.py:37
  37.9 34.7 %collective-permute-start.4 = (bf16[128,3072]{1,0:T(8,128)(2,1)S(1)}, bf16[128,3072]{1,0:T(8,128)(2,1)}, u32[]{:S(2)}, u32[]{:S(2)}) collective-permute-start(bf16[128,3072]{1,0:T(8,128)(2,1)S(1)} %pad_maximum_fusion.refs_0_), channel_id=1, source_target_pairs={{0,16},{4,12},{8,24},{12,4},{16,0},{20,28},{24,8},{28,20},{1,17},{... | collective-permute-start | bytes 2359304 | tf_op jit(solution)/shard_map/ppermute | solution.py:37
  39.4 33.2 %collective-permute-start.5 = (bf16[128,3072]{1,0:T(8,128)(2,1)S(1)}, bf16[128,3072]{1,0:T(8,128)(2,1)S(1)}, u32[]{:S(2)}, u32[]{:S(2)}) collective-permute-start(bf16[128,3072]{1,0:T(8,128)(2,1)S(1)} %pad_maximum_fusion.refs_0_), channel_id=1, source_target_pairs={{0,4},{4,0},{8,12},{12,8},{16,20},{20,16},{24,28},{28,24},{1,5},{5... | collective-permute-start | bytes 2359304 | tf_op jit(solution)/shard_map/ppermute | solution.py:37
  39.4 20.6 %collective-permute-start.6 = (bf16[64,4096]{1,0:T(8,128)(2,1)S(1)}, bf16[64,4096]{1,0:T(8,128)(2,1)S(1)}, u32[]{:S(2)}, u32[]{:S(2)}) collective-permute-start(bf16[64,4096]{1,0:T(8,128)(2,1)S(1)} %copy-done.11), channel_id=1, source_target_pairs={{0,1},{1,2},{2,3},{3,0},{4,5},{5,6},{6,7},{7,4},{8,9},{9,10},{10,1... | collective-permute-start | bytes 1572872 | tf_op jit(solution)/shard_map/ppermute | solution.py:82
  46.2 24.9 %collective-permute-start.7 = (bf16[64,4096]{1,0:T(8,128)(2,1)S(1)}, bf16[64,4096]{1,0:T(8,128)(2,1)S(1)}, u32[]{:S(2)}, u32[]{:S(2)}) collective-permute-start(bf16[64,4096]{1,0:T(8,128)(2,1)S(1)} %copy-done.11), channel_id=1, source_target_pairs={{0,3},{1,0},{2,1},{3,2},{4,7},{5,4},{6,5},{7,6},{8,11},{9,8},{10,9... | collective-permute-start | bytes 1572872 | tf_op jit(solution)/shard_map/ppermute | solution.py:82
  91.3 33.9 %collective-permute-start.13 = (bf16[512,768]{1,0:T(8,128)(2,1)}, bf16[512,768]{1,0:T(8,128)(2,1)}, u32[]{:S(2)}, u32[]{:S(2)}) collective-permute-start(bf16[512,768]{1,0:T(8,128)(2,1)} %get-tuple-element.136.refs_0_), channel_id=1, source_target_pairs={{0,8},{4,20},{8,0},{12,28},{16,24},{20,4},{24,16},{28,12},{1,9},{5... | collective-permute-start | bytes 2359304 | tf_op jit(solution)/shard_map/ppermute | solution.py:37
  91.9 33.3 %collective-permute-start.14 = (bf16[512,768]{1,0:T(8,128)(2,1)}, bf16[512,768]{1,0:T(8,128)(2,1)}, u32[]{:S(2)}, u32[]{:S(2)}) collective-permute-start(bf16[512,768]{1,0:T(8,128)(2,1)} %get-tuple-element.136.refs_0_), channel_id=1, source_target_pairs={{0,16},{4,12},{8,24},{12,4},{16,0},{20,28},{24,8},{28,20},{1,17},{... | collective-permute-start | bytes 2359304 | tf_op jit(solution)/shard_map/ppermute | solution.py:37
  125.2 26.2 %collective-permute-start.17 = (bf16[512,768]{1,0:T(8,128)(2,1)}, bf16[512,768]{1,0:T(8,128)(2,1)}, u32[]{:S(2)}, u32[]{:S(2)}) collective-permute-start(bf16[512,768]{1,0:T(8,128)(2,1)} %collective-permute-done.13.refs_1_), channel_id=1, source_target_pairs={{0,16},{4,12},{8,24},{12,4},{16,0},{20,28},{24,8},{28,20},{1,17},{... | collective-permute-start | bytes 2359304 | tf_op jit(solution)/shard_map/ppermute | solution.py:37
  125.8 25.6 %collective-permute-start.18 = (bf16[512,768]{1,0:T(8,128)(2,1)}, bf16[512,768]{1,0:T(8,128)(2,1)S(1)}, u32[]{:S(2)}, u32[]{:S(2)}) collective-permute-start(bf16[512,768]{1,0:T(8,128)(2,1)} %collective-permute-done.13.refs_1_), channel_id=1, source_target_pairs={{0,4},{4,0},{8,12},{12,8},{16,20},{20,16},{24,28},{28,24},{1,5},{5... | collective-permute-start | bytes 2359304 | tf_op jit(solution)/shard_map/ppermute | solution.py:37
  125.8 25.6 %collective-permute-start.16 = (bf16[1024,256]{1,0:T(8,128)(2,1)S(1)}, bf16[1024,256]{1,0:T(8,128)(2,1)S(1)}, u32[]{:S(2)}, u32[]{:S(2)}) collective-permute-start(bf16[1024,256]{1,0:T(8,128)(2,1)S(1)} %get-tuple-element.152.refs_0_), channel_id=1, source_target_pairs={{0,3},{1,0},{2,1},{3,2},{4,7},{5,4},{6,5},{7,6},{8,11},{9,8},{10,9... | collective-permute-start | bytes 1572872 | tf_op jit(solution)/shard_map/ppermute | solution.py:82
  152.3 40.3 %collective-permute-start.22 = (bf16[512,768]{1,0:T(8,128)(2,1)}, bf16[512,768]{1,0:T(8,128)(2,1)}, u32[]{:S(2)}, u32[]{:S(2)}) collective-permute-start(bf16[512,768]{1,0:T(8,128)(2,1)} %get-tuple-element.136.refs_0_), channel_id=1, source_target_pairs={{0,4},{4,0},{8,12},{12,8},{16,20},{20,16},{24,28},{28,24},{1,5},{5... | collective-permute-start | bytes 2359304 | tf_op jit(solution)/shard_map/ppermute | solution.py:37
  152.3 40.3 %collective-permute-start.23 = (bf16[512,768]{1,0:T(8,128)(2,1)}, bf16[512,768]{1,0:T(8,128)(2,1)}, u32[]{:S(2)}, u32[]{:S(2)}) collective-permute-start(bf16[512,768]{1,0:T(8,128)(2,1)} %collective-permute-done.14.refs_2_), channel_id=1, source_target_pairs={{0,4},{4,0},{8,12},{12,8},{16,20},{20,16},{24,28},{28,24},{1,5},{5... | collective-permute-start | bytes 2359304 | tf_op jit(solution)/shard_map/ppermute | solution.py:37
  152.8 39.8 %collective-permute-start.24 = (bf16[512,768]{1,0:T(8,128)(2,1)}, bf16[512,768]{1,0:T(8,128)(2,1)}, u32[]{:S(2)}, u32[]{:S(2)}) collective-permute-start(bf16[512,768]{1,0:T(8,128)(2,1)} %collective-permute-done.17.refs_3_), channel_id=1, source_target_pairs={{0,4},{4,0},{8,12},{12,8},{16,20},{20,16},{24,28},{28,24},{1,5},{5... | collective-permute-start | bytes 2359304 | tf_op jit(solution)/shard_map/ppermute | solution.py:37
  152.8 38.2 %collective-permute-start.20 = (bf16[1024,256]{1,0:T(8,128)(2,1)}, bf16[1024,256]{1,0:T(8,128)(2,1)S(1)}, u32[]{:S(2)}, u32[]{:S(2)}) collective-permute-start(bf16[1024,256]{1,0:T(8,128)(2,1)} %heads_2.3.refs_4_), channel_id=1, source_target_pairs={{0,3},{1,0},{2,1},{3,2},{4,7},{5,4},{6,5},{7,6},{8,11},{9,8},{10,9... | collective-permute-start | bytes 1572872 | tf_op jit(solution)/shard_map/ppermute | solution.py:82
  168.4 23.4 %collective-permute-start.21 = (bf16[1024,256]{1,0:T(8,128)(2,1)S(1)}, bf16[1024,256]{1,0:T(8,128)(2,1)S(1)}, u32[]{:S(2)}, u32[]{:S(2)}) collective-permute-start(bf16[1024,256]{1,0:T(8,128)(2,1)S(1)} %collective-permute-done.15.refs_1_), channel_id=1, source_target_pairs={{0,1},{1,2},{2,3},{3,0},{4,5},{5,6},{6,7},{7,4},{8,9},{9,10},{10,1... | collective-permute-start | bytes 1572872 | tf_op jit(solution)/shard_map/ppermute | solution.py:82
  195.6 24.0 %collective-permute-start.26 = (bf16[1024,256]{1,0:T(8,128)(2,1)}, bf16[1024,256]{1,0:T(8,128)(2,1)S(1)}, u32[]{:S(2)}, u32[]{:S(2)}) collective-permute-start(bf16[1024,256]{1,0:T(8,128)(2,1)} %heads_2.4.refs_0_), channel_id=1, source_target_pairs={{0,3},{1,0},{2,1},{3,2},{4,7},{5,4},{6,5},{7,6},{8,11},{9,8},{10,9... | collective-permute-start | bytes 1572872 | tf_op jit(solution)/shard_map/ppermute | solution.py:82
  196.5 34.7 %collective-permute-start.27 = (bf16[1024,256]{1,0:T(8,128)(2,1)}, bf16[1024,256]{1,0:T(8,128)(2,1)}, u32[]{:S(2)}, u32[]{:S(2)}) collective-permute-start(bf16[1024,256]{1,0:T(8,128)(2,1)} %collective-permute-done.19.refs_5_), channel_id=1, source_target_pairs={{0,1},{1,2},{2,3},{3,0},{4,5},{5,6},{6,7},{7,4},{8,9},{9,10},{10,1... | collective-permute-start | bytes 1572872 | tf_op jit(solution)/shard_map/ppermute | solution.py:82
  231.1 24.6 %collective-permute-start.29 = (bf16[1024,256]{1,0:T(8,128)(2,1)}, bf16[1024,256]{1,0:T(8,128)(2,1)}, u32[]{:S(2)}, u32[]{:S(2)}) collective-permute-start(bf16[1024,256]{1,0:T(8,128)(2,1)} %heads_2.5.refs_4_), channel_id=1, source_target_pairs={{0,3},{1,0},{2,1},{3,2},{4,7},{5,4},{6,5},{7,6},{8,11},{9,8},{10,9... | collective-permute-start | bytes 1572872 | tf_op jit(solution)/shard_map/ppermute | solution.py:82
  234.9 33.8 %collective-permute-start.30 = (bf16[1024,256]{1,0:T(8,128)(2,1)}, bf16[1024,256]{1,0:T(8,128)(2,1)}, u32[]{:S(2)}, u32[]{:S(2)}) collective-permute-start(bf16[1024,256]{1,0:T(8,128)(2,1)} %collective-permute-done.25.refs_1_), channel_id=1, source_target_pairs={{0,1},{1,2},{2,3},{3,0},{4,5},{5,6},{6,7},{7,4},{8,9},{9,10},{10,1... | collective-permute-start | bytes 1572872 | tf_op jit(solution)/shard_map/ppermute | solution.py:82
  (34 other events, 530.8 us)
Sparse Core Ops, SparseCore 0:
  9.2 64.1 all-gather.4
  75.4 54.8 all-gather.6
  132.2 44.5 all-gather.8
  178.6 54.3 all-gather.10

commit v4 on v3

--- a/solution.py
+++ b/solution.py
@@ -75,7 +75,7 @@
 
 
 def early_places(rows):
-    return [0, 1, 2, 4] if rows == 8 else list(range(rows // 2))
+    return [0, 1, 2, 4, 5, 6] if rows == 8 else list(range(rows // 2))
 
 
 def shift(x, cols, step):
@@ -429,7 +429,7 @@
     others = range(1, cols)
 
     gather = lambda w: lax.all_gather(w, "row", axis=0, tiled=True)
-    split = rows == 8 and n >= 4
+    turn = 2 if rows == 8 and n >= 4 else None
     weights = [[gather(pack(projections, chunks[:1])[0])]]
     shares = [share] + [shift(share, cols, k) for k in others]
     packs = list(pack(projections, chunks[1:]))
@@ -439,9 +439,9 @@
     )
     ids, numbers, source, order = small
 
-    weights += [[gather(p)] for p in (packs[:-1] if split else packs)]
+    weights += [[gather(p)] if k != turn else None for k, p in enumerate(packs, 1)]
     w_full = gather(w_out)
-    late = Rows(packs[-1], rows)
+    late = Rows(packs[(turn or n - 1) - 1], rows)
 
     table = Rows(jnp.concatenate([shares[k][:part] for k in others], axis=1), rows)
     encs = near_cols(enc, cols)
@@ -454,7 +454,7 @@
     table.parts, encs, placed = gate(table.parts, encs, placed)
 
     table.finish()
-    if split:
+    if turn:
         late.fetch(1, 2)
     normed, attended = fill_and_norm(
         part, order, numbers, ids, placed_own, placed, table.blocks(later), weights[0][0], encs, shares
@@ -465,12 +465,11 @@
     for k in range(1, n):
         whole = far_cols(half, cols) if half else None
         half = near_cols(attended, cols)
-        if split and k == 1:
-            late.fetch(3, 5)
-        if split and k == 2:
-            late.fetch(4, 6, 7)
-        if split and k == n - 1:
-            weights.append(late.blocks(range(rows)))
+        if turn and k == 1:
+            late.fetch(3, 4, 5)
+        if turn and k == 2:
+            late.fetch(6, 7)
+            weights[k] = late.blocks(range(rows))
         attended = some_heads(source, normed, weights[k], chunks[k][1])
         attended, normed, half, whole, late.parts = gate(attended, normed, half, whole, late.parts)
         if whole:

time: 293 us -> 288 us (0.983)
  starting transfers between devices: 49.7 us -> 41.4 us
    ppermute x18, starting transfers between devices: 41.6 us -> 31.7 us  [shift(): return lax.ppermute(x, 'col', [(c, (c + step) % cols) for c in range(cols)])]
    all_gather x4, waiting for transfers between devices: 0.71 us -> 6.23 us  [on_device(): gather = lambda w: lax.all_gather(w, 'row', axis=0, tiled=True)]
    ppermute x18, waiting for transfers between devices: 104 us -> 101 us  [shift(): return lax.ppermute(x, 'col', [(c, (c + step) % cols) for c in range(cols)])]
    unnamed x47 -> x49, local copies, waits for them, and re-layouts: 6.41 us -> 6.62 us
  transfers between devices with their start and end apart: 36 -> 36, of which waited for: 15 -> 16; matrix products, arithmetic and copies ran while one was open for 1% -> 1% of each run, Pallas kernels for 36% -> 37%
where the time goes in v4:
time: 288 us; the launch traced here: 287 us
  Pallas kernels  112 us (39%)
  waiting for transfers between devices  110 us (38%)
  starting transfers between devices  41.4 us (14%)
  between operations  13.4 us (5%)
  local copies, waits for them, and re-layouts  8.98 us (3%)
    ppermute x18, waiting for transfers between devices, shift(): return lax.ppermute(x, 'col', [(c, (c + step) % cols) for c in range(cols)])  101 us
    pallas_call x3, Pallas kernels, some_heads(): pl.pallas_call(functools.partial(heads_kernel, heads), out_shape=jax.Shap...  43.1 us
    ppermute x18, starting transfers between devices, shift(): return lax.ppermute(x, 'col', [(c, (c + step) % cols) for c in range(cols)])  31.7 us
    pallas_call x1, Pallas kernels, fill_and_norm(): pl.pallas_call(functools.partial(norm_kernel, cols, part, len(late)), out...  28 us
    pallas_call x3, Pallas kernels, project(): pl.pallas_call(functools.partial(out_kernel, n, acc is not None), out_sha...  19.2 us
    pallas_call x2, Pallas kernels, place(): pl.pallas_call(functools.partial(place_kernel, [len(t) for t in tables],...  15.9 us
    ppermute x14, starting transfers between devices, swap(): return lax.ppermute(x, 'row', pairs)  9.63 us
    unnamed x49, local copies, waits for them, and re-layouts  6.62 us
  transfers between devices with their start and end apart: 36, of which 16 were waited for; matrix products, arithmetic and copies ran while one was open for 1% of the time, Pallas kernels for 37%

profile of v4, /device:TPU:0, one launch (start us, length us, event | category | flops | bytes accessed | tf_op | source)
XLA Modules:
  0.0 287.3 jit_solution(7760927918203777234)
XLA Ops:
  18.5 3.4 %pack.2 = (bf16[512,768]{1,0:T(8,128)(2,1)}, bf16[512,768]{1,0:T(8,128)(2,1)}, bf16[512,768]{1,0:T(8,128)(2,1)}) custom-call(bf16[512,1024]{1,0:T(8,128)(2,1)} %refs_0_.5, bf16[512,1024]{1,0:T(8,128)(2,1)} %refs_1_.3, bf16[512,1024]{1,0:T(8,128)(2,1)} %refs_2_.3, bf16[512,1024]{1,0:T(8,128)(2,1)} %refs_0_.5, bf16[512,1024]{1,0:T(8,128)(2,1)} %refs_1_.3, ...), custom_call_target="tpu_custom_call" | custom-call | flops 1 | bytes 1 | tf_op jit(solution)/shard_map/pack/pallas_call | solution.py:125
  21.8 6.1 %place.2.own_ref = bf16[1024,1024]{1,0:T(8,128)(2,1)} custom-call(s32[1024,128]{1,0:T(8,128)} %select_select_fusion.ids_ref, bf16[1024,1024]{1,0:T(8,128)(2,1)} %refs_0_.3), custom_call_target="tpu_custom_call" | custom-call | flops 1 | bytes 1 | tf_op jit(solution)/shard_map/place/pallas_call | solution.py:183
  29.3 5.6 %collective-permute-done.1.refs_9_ = bf16[144,1024]{1,0:T(8,128)(2,1)S(1)} collective-permute-done((bf16[144,1024]{1,0:T(8,128)(2,1)S(1)}, bf16[144,1024]{1,0:T(8,128)(2,1)S(1)}, u32[]{:S(2)}, u32[]{:S(2)}) %collective-permute-start.1) | collective-permute-done | bytes 294944 | tf_op jit(solution)/shard_map/ppermute | solution.py:82
  39.4 6.8 %collective-permute-start.6 = (bf16[64,4096]{1,0:T(8,128)(2,1)S(1)}, bf16[64,4096]{1,0:T(8,128)(2,1)S(1)}, u32[]{:S(2)}, u32[]{:S(2)}) collective-permute-start(bf16[64,4096]{1,0:T(8,128)(2,1)S(1)} %copy-done.9), channel_id=1, source_target_pairs={{0,1},{1,2},{2,3},{3,0},{4,5},{5,6},{6,7},{7,4},{8,9},{9,10},{10,1... | collective-permute-start | bytes 1572872 | tf_op jit(solution)/shard_map/ppermute | solution.py:82
  47.3 12.8 %collective-permute-done.6.refs_4_ = bf16[64,4096]{1,0:T(8,128)(2,1)S(1)} collective-permute-done((bf16[64,4096]{1,0:T(8,128)(2,1)S(1)}, bf16[64,4096]{1,0:T(8,128)(2,1)S(1)}, u32[]{:S(2)}, u32[]{:S(2)}) %collective-permute-start.6) | collective-permute-done | bytes 524320 | tf_op jit(solution)/shard_map/ppermute | solution.py:82
  60.1 11.0 %collective-permute-done.7.refs_6_ = bf16[64,4096]{1,0:T(8,128)(2,1)S(1)} collective-permute-done((bf16[64,4096]{1,0:T(8,128)(2,1)S(1)}, bf16[64,4096]{1,0:T(8,128)(2,1)S(1)}, u32[]{:S(2)}, u32[]{:S(2)}) %collective-permute-start.7) | collective-permute-done | bytes 524320 | tf_op jit(solution)/shard_map/ppermute | solution.py:82
  77.1 9.9 %place.3.near_ref = bf16[1024,3072]{1,0:T(8,128)(2,1)} custom-call(s32[1024,128]{1,0:T(8,128)} %select_select_fusion.ids_ref, bf16[128,3072]{1,0:T(8,128)(2,1)} %copy-done.12, bf16[128,3072]{1,0:T(8,128)(2,1)} %collective-permute-done.3.refs_1_, bf16[128,3072]{1,0:T(8,128)(2,1)} %copy-done.15, bf16[128,3072]{1,0:T(8,128)(2,1)} %copy-done.16, ...), custom_call_target="tpu_custom_call" | custom-call | flops 1 | bytes 1 | tf_op jit(solution)/shard_map/place/pallas_call | solution.py:183
  94.5 28.0 %fill_norm.1 = (bf16[1024,4096]{1,0:T(8,128)(2,1)}, bf16[1024,256]{1,0:T(8,128)(2,1)S(1)}) custom-call(s32[4]{0:T(128)S(1)} %and_select_fusion.col_ref.at_ref, s32[1,256]{1,0:T(1,128)S(1)} %reshape.63.keep_ref, s32[1024,128]{1,0:T(8,128)S(1)} %copy-done.1, bf16[1024,1024]{1,0:T(8,128)(2,1)} %place.2.own_ref, bf16[1024,3072]{1,0:T(8,128)(2,1)} %place.3.near_ref, ...), custom_call_target="tpu_custom_call" | custom-call | flops 1 | bytes 1 | tf_op jit(solution)/shard_map/fill_norm/pallas_call | solution.py:266
  128.1 3.2 %all-gather.7.cloned.1.call-done.refs_0_ = bf16[4096,768]{1,0:T(8,128)(2,1)} async-done(((bf16[512,768]{1,0:T(8,128)(2,1)}), bf16[4096,768]{1,0:T(8,128)(2,1)}) %all-gather.7.cloned.1.call-update) | async-done | bytes 6291472 | tf_op jit(solution)/shard_map/all_gather | solution.py:431
  131.3 13.9 %heads_2.3.refs_4_ = bf16[1024,256]{1,0:T(8,128)(2,1)} custom-call(s32[8]{0:T(128)} %stack.35.source_ref, bf16[1024,4096]{1,0:T(8,128)(2,1)} %get-tuple-element.124.x_ref, bf16[4096,768]{1,0:T(8,128)(2,1)} %all-gather.7.cloned.1.call-done.refs_0_), custom_call_target="tpu_custom_call" | custom-call | flops 1 | bytes 1 | tf_op jit(solution)/shard_map/heads_2/pallas_call | solution.py:311
  145.2 4.8 %collective-permute-done.16.refs_3_ = bf16[1024,256]{1,0:T(8,128)(2,1)S(1)} collective-permute-done((bf16[1024,256]{1,0:T(8,128)(2,1)S(1)}, bf16[1024,256]{1,0:T(8,128)(2,1)S(1)}, u32[]{:S(2)}, u32[]{:S(2)}) %collective-permute-start.16) | collective-permute-done | bytes 524320 | tf_op jit(solution)/shard_map/ppermute | solution.py:82
  154.5 15.3 %heads_2.4.refs_0_ = bf16[1024,256]{1,0:T(8,128)(2,1)} custom-call(s32[8]{0:T(128)} %stack.35.source_ref, bf16[1024,4096]{1,0:T(8,128)(2,1)} %get-tuple-element.124.x_ref, bf16[512,768]{1,0:T(8,128)(2,1)} %get-tuple-element.114.refs_0_, bf16[512,768]{1,0:T(8,128)(2,1)} %collective-permute-done.13.refs_1_, bf16[512,768]{1,0:T(8,128)(2,1)} %collective-permute-done.14.refs_2_, ...), custom_call_target="tpu_custom_call" | custom-call | flops 1 | bytes 1 | tf_op jit(solution)/shard_map/heads_2/pallas_call | solution.py:311
  169.8 7.7 %collective-permute-done.23.refs_7_ = bf16[1024,256]{1,0:T(8,128)(2,1)S(1)} collective-permute-done((bf16[1024,256]{1,0:T(8,128)(2,1)}, bf16[1024,256]{1,0:T(8,128)(2,1)S(1)}, u32[]{:S(2)}, u32[]{:S(2)}) %collective-permute-start.23) | collective-permute-done | bytes 524320 | tf_op jit(solution)/shard_map/ppermute | solution.py:82
  178.2 10.8 %collective-permute-done.24.refs_2_ = bf16[1024,256]{1,0:T(8,128)(2,1)S(1)} collective-permute-done((bf16[1024,256]{1,0:T(8,128)(2,1)S(1)}, bf16[1024,256]{1,0:T(8,128)(2,1)S(1)}, u32[]{:S(2)}, u32[]{:S(2)}) %collective-permute-start.24) | collective-permute-done | bytes 524320 | tf_op jit(solution)/shard_map/ppermute | solution.py:82
  189.9 3.8 %collective-permute-start.26 = (bf16[1024,256]{1,0:T(8,128)(2,1)}, bf16[1024,256]{1,0:T(8,128)(2,1)}, u32[]{:S(2)}, u32[]{:S(2)}) collective-permute-start(bf16[1024,256]{1,0:T(8,128)(2,1)} %heads_2.4.refs_0_), channel_id=1, source_target_pairs={{0,3},{1,0},{2,1},{3,2},{4,7},{5,4},{6,5},{7,6},{8,11},{9,8},{10,9... | collective-permute-start | bytes 1572872 | tf_op jit(solution)/shard_map/ppermute | solution.py:82
  193.7 13.9 %heads_2.5.refs_4_ = bf16[1024,256]{1,0:T(8,128)(2,1)} custom-call(s32[8]{0:T(128)} %stack.35.source_ref, bf16[1024,4096]{1,0:T(8,128)(2,1)} %get-tuple-element.124.x_ref, bf16[4096,768]{1,0:T(8,128)(2,1)} %all-gather.9.cloned.1.call-done.refs_0_), custom_call_target="tpu_custom_call" | custom-call | flops 1 | bytes 1 | tf_op jit(solution)/shard_map/heads_2/pallas_call | solution.py:311
  207.7 6.9 %collective-permute-done.26.refs_3_ = bf16[1024,256]{1,0:T(8,128)(2,1)} collective-permute-done((bf16[1024,256]{1,0:T(8,128)(2,1)}, bf16[1024,256]{1,0:T(8,128)(2,1)}, u32[]{:S(2)}, u32[]{:S(2)}) %collective-permute-start.26) | collective-permute-done | bytes 524320 | tf_op jit(solution)/shard_map/ppermute | solution.py:82
  214.5 13.1 %collective-permute-done.27.refs_6_ = bf16[1024,256]{1,0:T(8,128)(2,1)} collective-permute-done((bf16[1024,256]{1,0:T(8,128)(2,1)}, bf16[1024,256]{1,0:T(8,128)(2,1)}, u32[]{:S(2)}, u32[]{:S(2)}) %collective-permute-start.27) | collective-permute-done | bytes 524320 | tf_op jit(solution)/shard_map/ppermute | solution.py:82
  227.7 3.8 %collective-permute-start.29 = (bf16[1024,256]{1,0:T(8,128)(2,1)}, bf16[1024,256]{1,0:T(8,128)(2,1)}, u32[]{:S(2)}, u32[]{:S(2)}) collective-permute-start(bf16[1024,256]{1,0:T(8,128)(2,1)} %heads_2.5.refs_4_), channel_id=1, source_target_pairs={{0,3},{1,0},{2,1},{3,2},{4,7},{5,4},{6,5},{7,6},{8,11},{9,8},{10,9... | collective-permute-start | bytes 1572872 | tf_op jit(solution)/shard_map/ppermute | solution.py:82
  236.6 8.2 %out_proj.3.refs_14_ = f32[1024,1024]{1,0:T(8,128)S(1)} custom-call(s32[4]{0:T(128)S(1)} %and_select_fusion.col_ref.at_ref, bf16[1024,256]{1,0:T(8,128)(2,1)S(1)} %get-tuple-element.134.refs_0_, bf16[1024,256]{1,0:T(8,128)(2,1)S(1)} %collective-permute-done.15.refs_1_, bf16[1024,256]{1,0:T(8,128)(2,1)S(1)} %copy-done.8, ...), custom_call_target="tpu_custom_call" | custom-call | flops 1 | bytes 1 | tf_op jit(solution)/shard_map/out_proj/pallas_call | solution.py:365
  244.8 7.4 %collective-permute-done.29.refs_6_ = bf16[1024,256]{1,0:T(8,128)(2,1)} collective-permute-done((bf16[1024,256]{1,0:T(8,128)(2,1)}, bf16[1024,256]{1,0:T(8,128)(2,1)}, u32[]{:S(2)}, u32[]{:S(2)}) %collective-permute-start.29) | collective-permute-done | bytes 524320 | tf_op jit(solution)/shard_map/ppermute | solution.py:82
  252.2 12.2 %collective-permute-done.30.refs_2_ = bf16[1024,256]{1,0:T(8,128)(2,1)} collective-permute-done((bf16[1024,256]{1,0:T(8,128)(2,1)}, bf16[1024,256]{1,0:T(8,128)(2,1)}, u32[]{:S(2)}, u32[]{:S(2)}) %collective-permute-start.30) | collective-permute-done | bytes 524320 | tf_op jit(solution)/shard_map/ppermute | solution.py:82
  264.4 7.9 %out_proj.4.refs_2_ = f32[1024,1024]{1,0:T(8,128)S(1)} custom-call(s32[4]{0:T(128)S(1)} %and_select_fusion.col_ref.at_ref, bf16[1024,256]{1,0:T(8,128)(2,1)S(1)} %copy-done.3, bf16[1024,256]{1,0:T(8,128)(2,1)} %collective-permute-done.25.refs_1_, bf16[1024,256]{1,0:T(8,128)(2,1)} %collective-permute-done.30.refs_2_, ...), custom_call_target="tpu_custom_call", output_to_operand_aliasing={{}: (15, {})} | custom-call | flops 1 | bytes 1 | tf_op jit(solution)/shard_map/out_proj/pallas_call | solution.py:365
  272.4 5.3 %collective-permute-done.31.refs_0_ = bf16[1024,256]{1,0:T(8,128)(2,1)S(1)} collective-permute-done((bf16[1024,256]{1,0:T(8,128)(2,1)}, bf16[1024,256]{1,0:T(8,128)(2,1)S(1)}, u32[]{:S(2)}, u32[]{:S(2)}) %collective-permute-start.31) | collective-permute-done | bytes 524320 | tf_op jit(solution)/shard_map/ppermute | solution.py:82
  (133 shorter events, 52.1 us)
Async XLA Ops:
  6.5 86.9 %all-gather.5.cloned.1.call-start = ((), (), s32[]{:S(2)}) async-start(), calls=%async_computation | async-start | bytes 7077888 | tf_op jit(solution)/shard_map/all_gather | solution.py:431
  8.7 122.6 %all-gather.7.cloned.1.call-start = ((), (), s32[]{:S(2)}) async-start(), calls=%async_computation.1 | async-start | bytes 7077888 | tf_op jit(solution)/shard_map/all_gather | solution.py:431
  9.9 19.3 %collective-permute-start = (bf16[144,1024]{1,0:T(8,128)(2,1)S(1)}, bf16[144,1024]{1,0:T(8,128)(2,1)S(1)}, u32[]{:S(2)}, u32[]{:S(2)}) collective-permute-start(bf16[144,1024]{1,0:T(8,128)(2,1)S(1)} %maximum_maximum_fusion.refs_7_), channel_id=1, source_target_pairs={{0,1},{1,2},{2,3},{3,0},{4,5},{5,6},{6,7},{7,4},{8,9},{9,10},{10,1... | collective-permute-start | bytes 884744 | tf_op jit(solution)/shard_map/ppermute | solution.py:82
  13.0 21.8 %collective-permute-start.1 = (bf16[144,1024]{1,0:T(8,128)(2,1)S(1)}, bf16[144,1024]{1,0:T(8,128)(2,1)S(1)}, u32[]{:S(2)}, u32[]{:S(2)}) collective-permute-start(bf16[144,1024]{1,0:T(8,128)(2,1)S(1)} %maximum_maximum_fusion.refs_7_), channel_id=1, source_target_pairs={{0,2},{1,3},{2,0},{3,1},{4,6},{5,7},{6,4},{7,5},{8,10},{9,11},{10,... | collective-permute-start | bytes 884744 | tf_op jit(solution)/shard_map/ppermute | solution.py:82
  34.9 158.9 %all-gather.9.cloned.1.call-start = ((), (), s32[]{:S(2)}) async-start(), calls=%async_computation.2 | async-start | bytes 7077888 | tf_op jit(solution)/shard_map/all_gather | solution.py:431
  35.6 198.9 %all-gather.11.cloned.1.call-start = ((), (), s32[]{:S(2)}) async-start(), calls=%async_computation.3 | async-start | bytes 9437184 | tf_op jit(solution)/shard_map/all_gather | solution.py:431
  36.3 36.2 %collective-permute-start.3 = (bf16[128,3072]{1,0:T(8,128)(2,1)S(1)}, bf16[128,3072]{1,0:T(8,128)(2,1)}, u32[]{:S(2)}, u32[]{:S(2)}) collective-permute-start(bf16[128,3072]{1,0:T(8,128)(2,1)S(1)} %pad_maximum_fusion.refs_0_), channel_id=1, source_target_pairs={{0,8},{4,20},{8,0},{12,28},{16,24},{20,4},{24,16},{28,12},{1,9},{5... | collective-permute-start | bytes 2359304 | tf_op jit(solution)/shard_map/ppermute | solution.py:37
  37.9 34.7 %collective-permute-start.4 = (bf16[128,3072]{1,0:T(8,128)(2,1)S(1)}, bf16[128,3072]{1,0:T(8,128)(2,1)S(1)}, u32[]{:S(2)}, u32[]{:S(2)}) collective-permute-start(bf16[128,3072]{1,0:T(8,128)(2,1)S(1)} %pad_maximum_fusion.refs_0_), channel_id=1, source_target_pairs={{0,16},{4,12},{8,24},{12,4},{16,0},{20,28},{24,8},{28,20},{1,17},{... | collective-permute-start | bytes 2359304 | tf_op jit(solution)/shard_map/ppermute | solution.py:37
  39.4 33.2 %collective-permute-start.5 = (bf16[128,3072]{1,0:T(8,128)(2,1)S(1)}, bf16[128,3072]{1,0:T(8,128)(2,1)S(1)}, u32[]{:S(2)}, u32[]{:S(2)}) collective-permute-start(bf16[128,3072]{1,0:T(8,128)(2,1)S(1)} %pad_maximum_fusion.refs_0_), channel_id=1, source_target_pairs={{0,4},{4,0},{8,12},{12,8},{16,20},{20,16},{24,28},{28,24},{1,5},{5... | collective-permute-start | bytes 2359304 | tf_op jit(solution)/shard_map/ppermute | solution.py:37
  39.4 20.6 %collective-permute-start.6 = (bf16[64,4096]{1,0:T(8,128)(2,1)S(1)}, bf16[64,4096]{1,0:T(8,128)(2,1)S(1)}, u32[]{:S(2)}, u32[]{:S(2)}) collective-permute-start(bf16[64,4096]{1,0:T(8,128)(2,1)S(1)} %copy-done.9), channel_id=1, source_target_pairs={{0,1},{1,2},{2,3},{3,0},{4,5},{5,6},{6,7},{7,4},{8,9},{9,10},{10,1... | collective-permute-start | bytes 1572872 | tf_op jit(solution)/shard_map/ppermute | solution.py:82
  46.2 24.9 %collective-permute-start.7 = (bf16[64,4096]{1,0:T(8,128)(2,1)S(1)}, bf16[64,4096]{1,0:T(8,128)(2,1)S(1)}, u32[]{:S(2)}, u32[]{:S(2)}) collective-permute-start(bf16[64,4096]{1,0:T(8,128)(2,1)S(1)} %copy-done.9), channel_id=1, source_target_pairs={{0,3},{1,0},{2,1},{3,2},{4,7},{5,4},{6,5},{7,6},{8,11},{9,8},{10,9... | collective-permute-start | bytes 1572872 | tf_op jit(solution)/shard_map/ppermute | solution.py:82
  90.8 31.7 %collective-permute-start.13 = (bf16[512,768]{1,0:T(8,128)(2,1)}, bf16[512,768]{1,0:T(8,128)(2,1)}, u32[]{:S(2)}, u32[]{:S(2)}) collective-permute-start(bf16[512,768]{1,0:T(8,128)(2,1)} %get-tuple-element.114.refs_0_), channel_id=1, source_target_pairs={{0,8},{4,20},{8,0},{12,28},{16,24},{20,4},{24,16},{28,12},{1,9},{5... | collective-permute-start | bytes 2359304 | tf_op jit(solution)/shard_map/ppermute | solution.py:37
  91.5 31.0 %collective-permute-start.14 = (bf16[512,768]{1,0:T(8,128)(2,1)}, bf16[512,768]{1,0:T(8,128)(2,1)}, u32[]{:S(2)}, u32[]{:S(2)}) collective-permute-start(bf16[512,768]{1,0:T(8,128)(2,1)} %get-tuple-element.114.refs_0_), channel_id=1, source_target_pairs={{0,16},{4,12},{8,24},{12,4},{16,0},{20,28},{24,8},{28,20},{1,17},{... | collective-permute-start | bytes 2359304 | tf_op jit(solution)/shard_map/ppermute | solution.py:37
  122.5 27.5 %collective-permute-start.17 = (bf16[512,768]{1,0:T(8,128)(2,1)}, bf16[512,768]{1,0:T(8,128)(2,1)}, u32[]{:S(2)}, u32[]{:S(2)}) collective-permute-start(bf16[512,768]{1,0:T(8,128)(2,1)} %collective-permute-done.13.refs_1_), channel_id=1, source_target_pairs={{0,16},{4,12},{8,24},{12,4},{16,0},{20,28},{24,8},{28,20},{1,17},{... | collective-permute-start | bytes 2359304 | tf_op jit(solution)/shard_map/ppermute | solution.py:37
  123.7 26.3 %collective-permute-start.18 = (bf16[512,768]{1,0:T(8,128)(2,1)}, bf16[512,768]{1,0:T(8,128)(2,1)S(1)}, u32[]{:S(2)}, u32[]{:S(2)}) collective-permute-start(bf16[512,768]{1,0:T(8,128)(2,1)} %get-tuple-element.114.refs_0_), channel_id=1, source_target_pairs={{0,4},{4,0},{8,12},{12,8},{16,20},{20,16},{24,28},{28,24},{1,5},{5... | collective-permute-start | bytes 2359304 | tf_op jit(solution)/shard_map/ppermute | solution.py:37
  123.7 26.3 %collective-permute-start.19 = (bf16[512,768]{1,0:T(8,128)(2,1)}, bf16[512,768]{1,0:T(8,128)(2,1)S(1)}, u32[]{:S(2)}, u32[]{:S(2)}) collective-permute-start(bf16[512,768]{1,0:T(8,128)(2,1)} %collective-permute-done.13.refs_1_), channel_id=1, source_target_pairs={{0,4},{4,0},{8,12},{12,8},{16,20},{20,16},{24,28},{28,24},{1,5},{5... | collective-permute-start | bytes 2359304 | tf_op jit(solution)/shard_map/ppermute | solution.py:37
  124.2 21.0 %collective-permute-start.15 = (bf16[1024,256]{1,0:T(8,128)(2,1)S(1)}, bf16[1024,256]{1,0:T(8,128)(2,1)S(1)}, u32[]{:S(2)}, u32[]{:S(2)}) collective-permute-start(bf16[1024,256]{1,0:T(8,128)(2,1)S(1)} %get-tuple-element.134.refs_0_), channel_id=1, source_target_pairs={{0,1},{1,2},{2,3},{3,0},{4,5},{5,6},{6,7},{7,4},{8,9},{9,10},{10,1... | collective-permute-start | bytes 1572872 | tf_op jit(solution)/shard_map/ppermute | solution.py:82
  125.2 24.8 %collective-permute-start.16 = (bf16[1024,256]{1,0:T(8,128)(2,1)S(1)}, bf16[1024,256]{1,0:T(8,128)(2,1)S(1)}, u32[]{:S(2)}, u32[]{:S(2)}) collective-permute-start(bf16[1024,256]{1,0:T(8,128)(2,1)S(1)} %get-tuple-element.134.refs_0_), channel_id=1, source_target_pairs={{0,3},{1,0},{2,1},{3,2},{4,7},{5,4},{6,5},{7,6},{8,11},{9,8},{10,9... | collective-permute-start | bytes 1572872 | tf_op jit(solution)/shard_map/ppermute | solution.py:82
  152.1 25.3 %collective-permute-start.23 = (bf16[1024,256]{1,0:T(8,128)(2,1)}, bf16[1024,256]{1,0:T(8,128)(2,1)S(1)}, u32[]{:S(2)}, u32[]{:S(2)}) collective-permute-start(bf16[1024,256]{1,0:T(8,128)(2,1)} %heads_2.3.refs_4_), channel_id=1, source_target_pairs={{0,3},{1,0},{2,1},{3,2},{4,7},{5,4},{6,5},{7,6},{8,11},{9,8},{10,9... | collective-permute-start | bytes 1572872 | tf_op jit(solution)/shard_map/ppermute | solution.py:82
  154.5 34.6 %collective-permute-start.24 = (bf16[1024,256]{1,0:T(8,128)(2,1)S(1)}, bf16[1024,256]{1,0:T(8,128)(2,1)S(1)}, u32[]{:S(2)}, u32[]{:S(2)}) collective-permute-start(bf16[1024,256]{1,0:T(8,128)(2,1)S(1)} %collective-permute-done.15.refs_1_), channel_id=1, source_target_pairs={{0,1},{1,2},{2,3},{3,0},{4,5},{5,6},{6,7},{7,4},{8,9},{9,10},{10,1... | collective-permute-start | bytes 1572872 | tf_op jit(solution)/shard_map/ppermute | solution.py:82
  189.9 24.6 %collective-permute-start.26 = (bf16[1024,256]{1,0:T(8,128)(2,1)}, bf16[1024,256]{1,0:T(8,128)(2,1)}, u32[]{:S(2)}, u32[]{:S(2)}) collective-permute-start(bf16[1024,256]{1,0:T(8,128)(2,1)} %heads_2.4.refs_0_), channel_id=1, source_target_pairs={{0,3},{1,0},{2,1},{3,2},{4,7},{5,4},{6,5},{7,6},{8,11},{9,8},{10,9... | collective-permute-start | bytes 1572872 | tf_op jit(solution)/shard_map/ppermute | solution.py:82
  193.7 33.9 %collective-permute-start.27 = (bf16[1024,256]{1,0:T(8,128)(2,1)}, bf16[1024,256]{1,0:T(8,128)(2,1)}, u32[]{:S(2)}, u32[]{:S(2)}) collective-permute-start(bf16[1024,256]{1,0:T(8,128)(2,1)} %collective-permute-done.22.refs_5_), channel_id=1, source_target_pairs={{0,1},{1,2},{2,3},{3,0},{4,5},{5,6},{6,7},{7,4},{8,9},{9,10},{10,1... | collective-permute-start | bytes 1572872 | tf_op jit(solution)/shard_map/ppermute | solution.py:82
  227.7 24.5 %collective-permute-start.29 = (bf16[1024,256]{1,0:T(8,128)(2,1)}, bf16[1024,256]{1,0:T(8,128)(2,1)}, u32[]{:S(2)}, u32[]{:S(2)}) collective-permute-start(bf16[1024,256]{1,0:T(8,128)(2,1)} %heads_2.5.refs_4_), channel_id=1, source_target_pairs={{0,3},{1,0},{2,1},{3,2},{4,7},{5,4},{6,5},{7,6},{8,11},{9,8},{10,9... | collective-permute-start | bytes 1572872 | tf_op jit(solution)/shard_map/ppermute | solution.py:82
  231.5 32.9 %collective-permute-start.30 = (bf16[1024,256]{1,0:T(8,128)(2,1)}, bf16[1024,256]{1,0:T(8,128)(2,1)}, u32[]{:S(2)}, u32[]{:S(2)}) collective-permute-start(bf16[1024,256]{1,0:T(8,128)(2,1)} %collective-permute-done.25.refs_1_), channel_id=1, source_target_pairs={{0,1},{1,2},{2,3},{3,0},{4,5},{5,6},{6,7},{7,4},{8,9},{9,10},{10,1... | collective-permute-start | bytes 1572872 | tf_op jit(solution)/shard_map/ppermute | solution.py:82
  (35 other events, 464.6 us)
Sparse Core Ops, SparseCore 0:
  9.2 64.2 all-gather.4
  75.4 55.8 all-gather.6
  133.2 45.0 all-gather.8
  180.1 54.3 all-gather.10

commit v5 on v4

--- a/solution.py
+++ b/solution.py
@@ -372,7 +372,7 @@
             out_specs=pl.BlockSpec((L, width), row),
         ),
         input_output_aliases=alias,
-        compiler_params=pltpu.CompilerParams(vmem_limit_bytes=40 * MIB),
+        compiler_params=pltpu.CompilerParams(vmem_limit_bytes=24 * MIB),
         cost_estimate=LIGHT,
         name="out_proj",
     )(order, *operands)

time: 288 us -> 287 us (level)
  local copies, waits for them, and re-layouts: 8.98 us -> 12.6 us
  Pallas kernels: 112 us -> 109 us
    unnamed x49, local copies, waits for them, and re-layouts: 6.62 us -> 10.3 us
    pallas_call x3, Pallas kernels: 19.2 us -> 16.2 us  [project(): pl.pallas_call(functools.partial(out_kernel, n, acc is not None), out_sha...]
  transfers between devices with their start and end apart: 36 -> 36, of which waited for: 16 -> 16; matrix products, arithmetic and copies ran while one was open for 1% -> 1% of each run, Pallas kernels for 37% -> 36%
where the time goes in v5:
time: 287 us; the launch traced here: 286 us
  Pallas kernels  109 us (38%)
  waiting for transfers between devices  108 us (38%)
  starting transfers between devices  41.4 us (14%)
  between operations  13.4 us (5%)
  local copies, waits for them, and re-layouts  12.6 us (4%)
    ppermute x18, waiting for transfers between devices, shift(): return lax.ppermute(x, 'col', [(c, (c + step) % cols) for c in range(cols)])  98.6 us
    pallas_call x3, Pallas kernels, some_heads(): pl.pallas_call(functools.partial(heads_kernel, heads), out_shape=jax.Shap...  43.3 us
    ppermute x18, starting transfers between devices, shift(): return lax.ppermute(x, 'col', [(c, (c + step) % cols) for c in range(cols)])  31.7 us
    pallas_call x1, Pallas kernels, fill_and_norm(): pl.pallas_call(functools.partial(norm_kernel, cols, part, len(late)), out...  28 us
    pallas_call x3, Pallas kernels, project(): pl.pallas_call(functools.partial(out_kernel, n, acc is not None), out_sha...  16.2 us
    pallas_call x2, Pallas kernels, place(): pl.pallas_call(functools.partial(place_kernel, [len(t) for t in tables],...  15.9 us
    unnamed x49, local copies, waits for them, and re-layouts  10.3 us
    ppermute x14, starting transfers between devices, swap(): return lax.ppermute(x, 'row', pairs)  9.63 us
  transfers between devices with their start and end apart: 36, of which 16 were waited for; matrix products, arithmetic and copies ran while one was open for 1% of the time, Pallas kernels for 36%

profile of v5, /device:TPU:0, one launch (start us, length us, event | category | flops | bytes accessed | tf_op | source)
XLA Modules:
  0.0 286.4 jit_solution(11032600126968458227)
XLA Ops:
  18.5 3.4 %pack.2 = (bf16[512,768]{1,0:T(8,128)(2,1)}, bf16[512,768]{1,0:T(8,128)(2,1)}, bf16[512,768]{1,0:T(8,128)(2,1)}) custom-call(bf16[512,1024]{1,0:T(8,128)(2,1)} %refs_0_.5, bf16[512,1024]{1,0:T(8,128)(2,1)} %refs_1_.3, bf16[512,1024]{1,0:T(8,128)(2,1)} %refs_2_.3, bf16[512,1024]{1,0:T(8,128)(2,1)} %refs_0_.5, bf16[512,1024]{1,0:T(8,128)(2,1)} %refs_1_.3, ...), custom_call_target="tpu_custom_call" | custom-call | flops 1 | bytes 1 | tf_op jit(solution)/shard_map/pack/pallas_call | solution.py:125
  21.8 6.1 %place.2.own_ref = bf16[1024,1024]{1,0:T(8,128)(2,1)} custom-call(s32[1024,128]{1,0:T(8,128)} %select_select_fusion.ids_ref, bf16[1024,1024]{1,0:T(8,128)(2,1)} %refs_0_.3), custom_call_target="tpu_custom_call" | custom-call | flops 1 | bytes 1 | tf_op jit(solution)/shard_map/place/pallas_call | solution.py:183
  29.3 5.6 %collective-permute-done.1.refs_9_ = bf16[144,1024]{1,0:T(8,128)(2,1)S(1)} collective-permute-done((bf16[144,1024]{1,0:T(8,128)(2,1)S(1)}, bf16[144,1024]{1,0:T(8,128)(2,1)S(1)}, u32[]{:S(2)}, u32[]{:S(2)}) %collective-permute-start.1) | collective-permute-done | bytes 294944 | tf_op jit(solution)/shard_map/ppermute | solution.py:82
  39.4 6.8 %collective-permute-start.6 = (bf16[64,4096]{1,0:T(8,128)(2,1)S(1)}, bf16[64,4096]{1,0:T(8,128)(2,1)S(1)}, u32[]{:S(2)}, u32[]{:S(2)}) collective-permute-start(bf16[64,4096]{1,0:T(8,128)(2,1)S(1)} %copy-done.10), channel_id=1, source_target_pairs={{0,1},{1,2},{2,3},{3,0},{4,5},{5,6},{6,7},{7,4},{8,9},{9,10},{10,1... | collective-permute-start | bytes 1572872 | tf_op jit(solution)/shard_map/ppermute | solution.py:82
  47.3 12.8 %collective-permute-done.6.refs_4_ = bf16[64,4096]{1,0:T(8,128)(2,1)S(1)} collective-permute-done((bf16[64,4096]{1,0:T(8,128)(2,1)S(1)}, bf16[64,4096]{1,0:T(8,128)(2,1)S(1)}, u32[]{:S(2)}, u32[]{:S(2)}) %collective-permute-start.6) | collective-permute-done | bytes 524320 | tf_op jit(solution)/shard_map/ppermute | solution.py:82
  60.1 11.0 %collective-permute-done.7.refs_6_ = bf16[64,4096]{1,0:T(8,128)(2,1)S(1)} collective-permute-done((bf16[64,4096]{1,0:T(8,128)(2,1)S(1)}, bf16[64,4096]{1,0:T(8,128)(2,1)S(1)}, u32[]{:S(2)}, u32[]{:S(2)}) %collective-permute-start.7) | collective-permute-done | bytes 524320 | tf_op jit(solution)/shard_map/ppermute | solution.py:82
  77.1 9.9 %place.3.near_ref = bf16[1024,3072]{1,0:T(8,128)(2,1)} custom-call(s32[1024,128]{1,0:T(8,128)} %select_select_fusion.ids_ref, bf16[128,3072]{1,0:T(8,128)(2,1)} %copy-done.13, bf16[128,3072]{1,0:T(8,128)(2,1)} %collective-permute-done.3.refs_1_, bf16[128,3072]{1,0:T(8,128)(2,1)} %copy-done.15, bf16[128,3072]{1,0:T(8,128)(2,1)} %copy-done.16, ...), custom_call_target="tpu_custom_call" | custom-call | flops 1 | bytes 1 | tf_op jit(solution)/shard_map/place/pallas_call | solution.py:183
  94.5 28.0 %fill_norm.1 = (bf16[1024,4096]{1,0:T(8,128)(2,1)}, bf16[1024,256]{1,0:T(8,128)(2,1)S(1)}) custom-call(s32[4]{0:T(128)S(1)} %and_select_fusion.col_ref.at_ref, s32[1,256]{1,0:T(1,128)S(1)} %reshape.63.keep_ref, s32[1024,128]{1,0:T(8,128)S(1)} %copy-done.2, bf16[1024,1024]{1,0:T(8,128)(2,1)} %place.2.own_ref, bf16[1024,3072]{1,0:T(8,128)(2,1)} %place.3.near_ref, ...), custom_call_target="tpu_custom_call" | custom-call | flops 1 | bytes 1 | tf_op jit(solution)/shard_map/fill_norm/pallas_call | solution.py:266
  131.3 13.9 %heads_2.3.refs_4_ = bf16[1024,256]{1,0:T(8,128)(2,1)} custom-call(s32[8]{0:T(128)} %stack.35.source_ref, bf16[1024,4096]{1,0:T(8,128)(2,1)} %get-tuple-element.124.x_ref, bf16[4096,768]{1,0:T(8,128)(2,1)} %all-gather.7.cloned.1.call-done.refs_0_), custom_call_target="tpu_custom_call" | custom-call | flops 1 | bytes 1 | tf_op jit(solution)/shard_map/heads_2/pallas_call | solution.py:311
  145.2 4.8 %collective-permute-done.16.refs_3_ = bf16[1024,256]{1,0:T(8,128)(2,1)S(1)} collective-permute-done((bf16[1024,256]{1,0:T(8,128)(2,1)S(1)}, bf16[1024,256]{1,0:T(8,128)(2,1)S(1)}, u32[]{:S(2)}, u32[]{:S(2)}) %collective-permute-start.16) | collective-permute-done | bytes 524320 | tf_op jit(solution)/shard_map/ppermute | solution.py:82
  154.8 15.3 %heads_2.4.refs_0_ = bf16[1024,256]{1,0:T(8,128)(2,1)} custom-call(s32[8]{0:T(128)} %stack.35.source_ref, bf16[1024,4096]{1,0:T(8,128)(2,1)} %get-tuple-element.124.x_ref, bf16[512,768]{1,0:T(8,128)(2,1)} %get-tuple-element.114.refs_0_, bf16[512,768]{1,0:T(8,128)(2,1)} %collective-permute-done.13.refs_1_, bf16[512,768]{1,0:T(8,128)(2,1)} %collective-permute-done.14.refs_2_, ...), custom_call_target="tpu_custom_call" | custom-call | flops 1 | bytes 1 | tf_op jit(solution)/shard_map/heads_2/pallas_call | solution.py:311
  170.1 7.9 %collective-permute-done.23.refs_7_ = bf16[1024,256]{1,0:T(8,128)(2,1)S(1)} collective-permute-done((bf16[1024,256]{1,0:T(8,128)(2,1)}, bf16[1024,256]{1,0:T(8,128)(2,1)S(1)}, u32[]{:S(2)}, u32[]{:S(2)}) %collective-permute-start.23) | collective-permute-done | bytes 524320 | tf_op jit(solution)/shard_map/ppermute | solution.py:82
  178.8 10.2 %collective-permute-done.24.refs_2_ = bf16[1024,256]{1,0:T(8,128)(2,1)S(1)} collective-permute-done((bf16[1024,256]{1,0:T(8,128)(2,1)S(1)}, bf16[1024,256]{1,0:T(8,128)(2,1)S(1)}, u32[]{:S(2)}, u32[]{:S(2)}) %collective-permute-start.24) | collective-permute-done | bytes 524320 | tf_op jit(solution)/shard_map/ppermute | solution.py:82
  189.9 3.8 %collective-permute-start.26 = (bf16[1024,256]{1,0:T(8,128)(2,1)}, bf16[1024,256]{1,0:T(8,128)(2,1)}, u32[]{:S(2)}, u32[]{:S(2)}) collective-permute-start(bf16[1024,256]{1,0:T(8,128)(2,1)} %heads_2.4.refs_0_), channel_id=1, source_target_pairs={{0,3},{1,0},{2,1},{3,2},{4,7},{5,4},{6,5},{7,6},{8,11},{9,8},{10,9... | collective-permute-start | bytes 1572872 | tf_op jit(solution)/shard_map/ppermute | solution.py:82
  193.7 14.0 %heads_2.5.refs_4_ = bf16[1024,256]{1,0:T(8,128)(2,1)} custom-call(s32[8]{0:T(128)} %stack.35.source_ref, bf16[1024,4096]{1,0:T(8,128)(2,1)} %get-tuple-element.124.x_ref, bf16[4096,768]{1,0:T(8,128)(2,1)} %all-gather.9.cloned.1.call-done.refs_0_), custom_call_target="tpu_custom_call" | custom-call | flops 1 | bytes 1 | tf_op jit(solution)/shard_map/heads_2/pallas_call | solution.py:311
  207.8 6.6 %collective-permute-done.26.refs_3_ = bf16[1024,256]{1,0:T(8,128)(2,1)} collective-permute-done((bf16[1024,256]{1,0:T(8,128)(2,1)}, bf16[1024,256]{1,0:T(8,128)(2,1)}, u32[]{:S(2)}, u32[]{:S(2)}) %collective-permute-start.26) | collective-permute-done | bytes 524320 | tf_op jit(solution)/shard_map/ppermute | solution.py:82
  214.4 13.0 %collective-permute-done.27.refs_6_ = bf16[1024,256]{1,0:T(8,128)(2,1)} collective-permute-done((bf16[1024,256]{1,0:T(8,128)(2,1)S(1)}, bf16[1024,256]{1,0:T(8,128)(2,1)}, u32[]{:S(2)}, u32[]{:S(2)}) %collective-permute-start.27) | collective-permute-done | bytes 524320 | tf_op jit(solution)/shard_map/ppermute | solution.py:82
  227.4 3.8 %collective-permute-start.29 = (bf16[1024,256]{1,0:T(8,128)(2,1)}, bf16[1024,256]{1,0:T(8,128)(2,1)}, u32[]{:S(2)}, u32[]{:S(2)}) collective-permute-start(bf16[1024,256]{1,0:T(8,128)(2,1)} %heads_2.5.refs_4_), channel_id=1, source_target_pairs={{0,3},{1,0},{2,1},{3,2},{4,7},{5,4},{6,5},{7,6},{8,11},{9,8},{10,9... | collective-permute-start | bytes 1572872 | tf_op jit(solution)/shard_map/ppermute | solution.py:82
  234.5 3.4 %copy-done = bf16[4096,1024]{1,0:T(8,128)(2,1)S(1)} copy-done((bf16[4096,1024]{1,0:T(8,128)(2,1)S(1)}, bf16[4096,1024]{1,0:T(8,128)(2,1)}, u32[]{:S(2)}) %copy-start) | copy-done | bytes 8388632
  240.0 6.8 %out_proj.3.refs_14_ = f32[1024,1024]{1,0:T(8,128)S(1)} custom-call(s32[4]{0:T(128)S(1)} %and_select_fusion.col_ref.at_ref, bf16[1024,256]{1,0:T(8,128)(2,1)S(1)} %get-tuple-element.134.refs_0_, bf16[1024,256]{1,0:T(8,128)(2,1)S(1)} %collective-permute-done.15.refs_1_, bf16[1024,256]{1,0:T(8,128)(2,1)S(1)} %copy-done.9, ...), custom_call_target="tpu_custom_call" | custom-call | flops 1 | bytes 1 | tf_op jit(solution)/shard_map/out_proj/pallas_call | solution.py:365
  246.7 5.2 %collective-permute-done.29.refs_6_ = bf16[1024,256]{1,0:T(8,128)(2,1)} collective-permute-done((bf16[1024,256]{1,0:T(8,128)(2,1)}, bf16[1024,256]{1,0:T(8,128)(2,1)}, u32[]{:S(2)}, u32[]{:S(2)}) %collective-permute-start.29) | collective-permute-done | bytes 524320 | tf_op jit(solution)/shard_map/ppermute | solution.py:82
  251.9 11.9 %collective-permute-done.30.refs_2_ = bf16[1024,256]{1,0:T(8,128)(2,1)} collective-permute-done((bf16[1024,256]{1,0:T(8,128)(2,1)}, bf16[1024,256]{1,0:T(8,128)(2,1)}, u32[]{:S(2)}, u32[]{:S(2)}) %collective-permute-start.30) | collective-permute-done | bytes 524320 | tf_op jit(solution)/shard_map/ppermute | solution.py:82
  263.9 6.3 %out_proj.4.refs_2_ = f32[1024,1024]{1,0:T(8,128)S(1)} custom-call(s32[4]{0:T(128)S(1)} %and_select_fusion.col_ref.at_ref, bf16[1024,256]{1,0:T(8,128)(2,1)S(1)} %copy-done.4, bf16[1024,256]{1,0:T(8,128)(2,1)} %collective-permute-done.25.refs_1_, bf16[1024,256]{1,0:T(8,128)(2,1)} %collective-permute-done.30.refs_2_, ...), custom_call_target="tpu_custom_call", output_to_operand_aliasing={{}: (15, {})} | custom-call | flops 1 | bytes 1 | tf_op jit(solution)/shard_map/out_proj/pallas_call | solution.py:365
  270.2 6.6 %collective-permute-done.31.refs_0_ = bf16[1024,256]{1,0:T(8,128)(2,1)S(1)} collective-permute-done((bf16[1024,256]{1,0:T(8,128)(2,1)}, bf16[1024,256]{1,0:T(8,128)(2,1)S(1)}, u32[]{:S(2)}, u32[]{:S(2)}) %collective-permute-start.31) | collective-permute-done | bytes 524320 | tf_op jit(solution)/shard_map/ppermute | solution.py:82
  (133 shorter events, 55.9 us)
Async XLA Ops:
  6.5 86.9 %all-gather.5.cloned.1.call-start = ((), (), s32[]{:S(2)}) async-start(), calls=%async_computation | async-start | bytes 7077888 | tf_op jit(solution)/shard_map/all_gather | solution.py:431
  8.7 122.6 %all-gather.7.cloned.1.call-start = ((), (), s32[]{:S(2)}) async-start(), calls=%async_computation.1 | async-start | bytes 7077888 | tf_op jit(solution)/shard_map/all_gather | solution.py:431
  9.9 19.3 %collective-permute-start = (bf16[144,1024]{1,0:T(8,128)(2,1)S(1)}, bf16[144,1024]{1,0:T(8,128)(2,1)S(1)}, u32[]{:S(2)}, u32[]{:S(2)}) collective-permute-start(bf16[144,1024]{1,0:T(8,128)(2,1)S(1)} %maximum_maximum_fusion.refs_7_), channel_id=1, source_target_pairs={{0,1},{1,2},{2,3},{3,0},{4,5},{5,6},{6,7},{7,4},{8,9},{9,10},{10,1... | collective-permute-start | bytes 884744 | tf_op jit(solution)/shard_map/ppermute | solution.py:82
  13.0 21.8 %collective-permute-start.1 = (bf16[144,1024]{1,0:T(8,128)(2,1)S(1)}, bf16[144,1024]{1,0:T(8,128)(2,1)S(1)}, u32[]{:S(2)}, u32[]{:S(2)}) collective-permute-start(bf16[144,1024]{1,0:T(8,128)(2,1)S(1)} %maximum_maximum_fusion.refs_7_), channel_id=1, source_target_pairs={{0,2},{1,3},{2,0},{3,1},{4,6},{5,7},{6,4},{7,5},{8,10},{9,11},{10,... | collective-permute-start | bytes 884744 | tf_op jit(solution)/shard_map/ppermute | solution.py:82
  34.9 158.9 %all-gather.9.cloned.1.call-start = ((), (), s32[]{:S(2)}) async-start(), calls=%async_computation.2 | async-start | bytes 7077888 | tf_op jit(solution)/shard_map/all_gather | solution.py:431
  35.6 198.9 %all-gather.11.cloned.1.call-start = ((), (), s32[]{:S(2)}) async-start(), calls=%async_computation.3 | async-start | bytes 9437184 | tf_op jit(solution)/shard_map/all_gather | solution.py:431
  36.3 36.2 %collective-permute-start.3 = (bf16[128,3072]{1,0:T(8,128)(2,1)S(1)}, bf16[128,3072]{1,0:T(8,128)(2,1)}, u32[]{:S(2)}, u32[]{:S(2)}) collective-permute-start(bf16[128,3072]{1,0:T(8,128)(2,1)S(1)} %pad_maximum_fusion.refs_0_), channel_id=1, source_target_pairs={{0,8},{4,20},{8,0},{12,28},{16,24},{20,4},{24,16},{28,12},{1,9},{5... | collective-permute-start | bytes 2359304 | tf_op jit(solution)/shard_map/ppermute | solution.py:37
  37.9 34.7 %collective-permute-start.4 = (bf16[128,3072]{1,0:T(8,128)(2,1)S(1)}, bf16[128,3072]{1,0:T(8,128)(2,1)S(1)}, u32[]{:S(2)}, u32[]{:S(2)}) collective-permute-start(bf16[128,3072]{1,0:T(8,128)(2,1)S(1)} %pad_maximum_fusion.refs_0_), channel_id=1, source_target_pairs={{0,16},{4,12},{8,24},{12,4},{16,0},{20,28},{24,8},{28,20},{1,17},{... | collective-permute-start | bytes 2359304 | tf_op jit(solution)/shard_map/ppermute | solution.py:37
  39.4 33.2 %collective-permute-start.5 = (bf16[128,3072]{1,0:T(8,128)(2,1)S(1)}, bf16[128,3072]{1,0:T(8,128)(2,1)S(1)}, u32[]{:S(2)}, u32[]{:S(2)}) collective-permute-start(bf16[128,3072]{1,0:T(8,128)(2,1)S(1)} %pad_maximum_fusion.refs_0_), channel_id=1, source_target_pairs={{0,4},{4,0},{8,12},{12,8},{16,20},{20,16},{24,28},{28,24},{1,5},{5... | collective-permute-start | bytes 2359304 | tf_op jit(solution)/shard_map/ppermute | solution.py:37
  39.4 20.6 %collective-permute-start.6 = (bf16[64,4096]{1,0:T(8,128)(2,1)S(1)}, bf16[64,4096]{1,0:T(8,128)(2,1)S(1)}, u32[]{:S(2)}, u32[]{:S(2)}) collective-permute-start(bf16[64,4096]{1,0:T(8,128)(2,1)S(1)} %copy-done.10), channel_id=1, source_target_pairs={{0,1},{1,2},{2,3},{3,0},{4,5},{5,6},{6,7},{7,4},{8,9},{9,10},{10,1... | collective-permute-start | bytes 1572872 | tf_op jit(solution)/shard_map/ppermute | solution.py:82
  46.2 24.9 %collective-permute-start.7 = (bf16[64,4096]{1,0:T(8,128)(2,1)S(1)}, bf16[64,4096]{1,0:T(8,128)(2,1)S(1)}, u32[]{:S(2)}, u32[]{:S(2)}) collective-permute-start(bf16[64,4096]{1,0:T(8,128)(2,1)S(1)} %copy-done.10), channel_id=1, source_target_pairs={{0,3},{1,0},{2,1},{3,2},{4,7},{5,4},{6,5},{7,6},{8,11},{9,8},{10,9... | collective-permute-start | bytes 1572872 | tf_op jit(solution)/shard_map/ppermute | solution.py:82
  90.8 31.7 %collective-permute-start.13 = (bf16[512,768]{1,0:T(8,128)(2,1)}, bf16[512,768]{1,0:T(8,128)(2,1)}, u32[]{:S(2)}, u32[]{:S(2)}) collective-permute-start(bf16[512,768]{1,0:T(8,128)(2,1)} %get-tuple-element.114.refs_0_), channel_id=1, source_target_pairs={{0,8},{4,20},{8,0},{12,28},{16,24},{20,4},{24,16},{28,12},{1,9},{5... | collective-permute-start | bytes 2359304 | tf_op jit(solution)/shard_map/ppermute | solution.py:37
  91.5 31.0 %collective-permute-start.14 = (bf16[512,768]{1,0:T(8,128)(2,1)}, bf16[512,768]{1,0:T(8,128)(2,1)}, u32[]{:S(2)}, u32[]{:S(2)}) collective-permute-start(bf16[512,768]{1,0:T(8,128)(2,1)} %get-tuple-element.114.refs_0_), channel_id=1, source_target_pairs={{0,16},{4,12},{8,24},{12,4},{16,0},{20,28},{24,8},{28,20},{1,17},{... | collective-permute-start | bytes 2359304 | tf_op jit(solution)/shard_map/ppermute | solution.py:37
  122.5 27.5 %collective-permute-start.17 = (bf16[512,768]{1,0:T(8,128)(2,1)}, bf16[512,768]{1,0:T(8,128)(2,1)}, u32[]{:S(2)}, u32[]{:S(2)}) collective-permute-start(bf16[512,768]{1,0:T(8,128)(2,1)} %collective-permute-done.13.refs_1_), channel_id=1, source_target_pairs={{0,16},{4,12},{8,24},{12,4},{16,0},{20,28},{24,8},{28,20},{1,17},{... | collective-permute-start | bytes 2359304 | tf_op jit(solution)/shard_map/ppermute | solution.py:37
  123.7 26.3 %collective-permute-start.18 = (bf16[512,768]{1,0:T(8,128)(2,1)}, bf16[512,768]{1,0:T(8,128)(2,1)S(1)}, u32[]{:S(2)}, u32[]{:S(2)}) collective-permute-start(bf16[512,768]{1,0:T(8,128)(2,1)} %get-tuple-element.114.refs_0_), channel_id=1, source_target_pairs={{0,4},{4,0},{8,12},{12,8},{16,20},{20,16},{24,28},{28,24},{1,5},{5... | collective-permute-start | bytes 2359304 | tf_op jit(solution)/shard_map/ppermute | solution.py:37
  123.7 26.3 %collective-permute-start.19 = (bf16[512,768]{1,0:T(8,128)(2,1)}, bf16[512,768]{1,0:T(8,128)(2,1)}, u32[]{:S(2)}, u32[]{:S(2)}) collective-permute-start(bf16[512,768]{1,0:T(8,128)(2,1)} %collective-permute-done.13.refs_1_), channel_id=1, source_target_pairs={{0,4},{4,0},{8,12},{12,8},{16,20},{20,16},{24,28},{28,24},{1,5},{5... | collective-permute-start | bytes 2359304 | tf_op jit(solution)/shard_map/ppermute | solution.py:37
  124.2 21.0 %collective-permute-start.15 = (bf16[1024,256]{1,0:T(8,128)(2,1)S(1)}, bf16[1024,256]{1,0:T(8,128)(2,1)S(1)}, u32[]{:S(2)}, u32[]{:S(2)}) collective-permute-start(bf16[1024,256]{1,0:T(8,128)(2,1)S(1)} %get-tuple-element.134.refs_0_), channel_id=1, source_target_pairs={{0,1},{1,2},{2,3},{3,0},{4,5},{5,6},{6,7},{7,4},{8,9},{9,10},{10,1... | collective-permute-start | bytes 1572872 | tf_op jit(solution)/shard_map/ppermute | solution.py:82
  125.2 24.8 %collective-permute-start.16 = (bf16[1024,256]{1,0:T(8,128)(2,1)S(1)}, bf16[1024,256]{1,0:T(8,128)(2,1)S(1)}, u32[]{:S(2)}, u32[]{:S(2)}) collective-permute-start(bf16[1024,256]{1,0:T(8,128)(2,1)S(1)} %get-tuple-element.134.refs_0_), channel_id=1, source_target_pairs={{0,3},{1,0},{2,1},{3,2},{4,7},{5,4},{6,5},{7,6},{8,11},{9,8},{10,9... | collective-permute-start | bytes 1572872 | tf_op jit(solution)/shard_map/ppermute | solution.py:82
  152.4 25.6 %collective-permute-start.23 = (bf16[1024,256]{1,0:T(8,128)(2,1)}, bf16[1024,256]{1,0:T(8,128)(2,1)S(1)}, u32[]{:S(2)}, u32[]{:S(2)}) collective-permute-start(bf16[1024,256]{1,0:T(8,128)(2,1)} %heads_2.3.refs_4_), channel_id=1, source_target_pairs={{0,3},{1,0},{2,1},{3,2},{4,7},{5,4},{6,5},{7,6},{8,11},{9,8},{10,9... | collective-permute-start | bytes 1572872 | tf_op jit(solution)/shard_map/ppermute | solution.py:82
  154.7 34.3 %collective-permute-start.24 = (bf16[1024,256]{1,0:T(8,128)(2,1)S(1)}, bf16[1024,256]{1,0:T(8,128)(2,1)S(1)}, u32[]{:S(2)}, u32[]{:S(2)}) collective-permute-start(bf16[1024,256]{1,0:T(8,128)(2,1)S(1)} %collective-permute-done.15.refs_1_), channel_id=1, source_target_pairs={{0,1},{1,2},{2,3},{3,0},{4,5},{5,6},{6,7},{7,4},{8,9},{9,10},{10,1... | collective-permute-start | bytes 1572872 | tf_op jit(solution)/shard_map/ppermute | solution.py:82
  189.9 24.5 %collective-permute-start.26 = (bf16[1024,256]{1,0:T(8,128)(2,1)}, bf16[1024,256]{1,0:T(8,128)(2,1)}, u32[]{:S(2)}, u32[]{:S(2)}) collective-permute-start(bf16[1024,256]{1,0:T(8,128)(2,1)} %heads_2.4.refs_0_), channel_id=1, source_target_pairs={{0,3},{1,0},{2,1},{3,2},{4,7},{5,4},{6,5},{7,6},{8,11},{9,8},{10,9... | collective-permute-start | bytes 1572872 | tf_op jit(solution)/shard_map/ppermute | solution.py:82
  193.7 33.7 %collective-permute-start.27 = (bf16[1024,256]{1,0:T(8,128)(2,1)S(1)}, bf16[1024,256]{1,0:T(8,128)(2,1)}, u32[]{:S(2)}, u32[]{:S(2)}) collective-permute-start(bf16[1024,256]{1,0:T(8,128)(2,1)S(1)} %collective-permute-done.22.refs_5_), channel_id=1, source_target_pairs={{0,1},{1,2},{2,3},{3,0},{4,5},{5,6},{6,7},{7,4},{8,9},{9,10},{10,1... | collective-permute-start | bytes 1572872 | tf_op jit(solution)/shard_map/ppermute | solution.py:82
  227.4 24.5 %collective-permute-start.29 = (bf16[1024,256]{1,0:T(8,128)(2,1)}, bf16[1024,256]{1,0:T(8,128)(2,1)}, u32[]{:S(2)}, u32[]{:S(2)}) collective-permute-start(bf16[1024,256]{1,0:T(8,128)(2,1)} %heads_2.5.refs_4_), channel_id=1, source_target_pairs={{0,3},{1,0},{2,1},{3,2},{4,7},{5,4},{6,5},{7,6},{8,11},{9,8},{10,9... | collective-permute-start | bytes 1572872 | tf_op jit(solution)/shard_map/ppermute | solution.py:82
  231.2 32.6 %collective-permute-start.30 = (bf16[1024,256]{1,0:T(8,128)(2,1)}, bf16[1024,256]{1,0:T(8,128)(2,1)}, u32[]{:S(2)}, u32[]{:S(2)}) collective-permute-start(bf16[1024,256]{1,0:T(8,128)(2,1)} %collective-permute-done.25.refs_1_), channel_id=1, source_target_pairs={{0,1},{1,2},{2,3},{3,0},{4,5},{5,6},{6,7},{7,4},{8,9},{9,10},{10,1... | collective-permute-start | bytes 1572872 | tf_op jit(solution)/shard_map/ppermute | solution.py:82
  (35 other events, 458.2 us)
Sparse Core Ops, SparseCore 0:
  9.2 64.2 all-gather.4
  75.4 55.8 all-gather.6
  133.2 45.0 all-gather.8
  180.1 54.3 all-gather.10

commit v6 on v5

--- a/solution.py
+++ b/solution.py
@@ -53,7 +53,7 @@
 
     def start(self):
         if self.rows == 8:
-            self.fetch(1, 2, 4)
+            self.fetch(1, 2)
             return
         blocks, bit = [self.x], self.rows // 2
         while bit:
@@ -64,7 +64,7 @@
 
     def forward(self):
         if self.rows == 8:
-            self.fetch(3, 5, 6)
+            self.fetch(4, 5, 6, 3)
 
     def finish(self):
         if self.rows == 8:

time: 287 us -> 286 us (level)
    ppermute x18, waiting for transfers between devices: 98.6 us -> 94.6 us  [shift(): return lax.ppermute(x, 'col', [(c, (c + step) % cols) for c in range(cols)])]
    ppermute x14, waiting for transfers between devices: 1.97 us -> 5.03 us  [swap(): return lax.ppermute(x, 'row', pairs)]
  transfers between devices with their start and end apart: 36 -> 36, of which waited for: 16 -> 17; matrix products, arithmetic and copies ran while one was open for 1% -> 1% of each run, Pallas kernels for 36% -> 36%
where the time goes in v6:
time: 286 us; the launch traced here: 285 us
  waiting for transfers between devices  109 us (38%)
  Pallas kernels  108 us (38%)
  starting transfers between devices  40.9 us (14%)
  between operations  13.4 us (5%)
  local copies, waits for them, and re-layouts  12.5 us (4%)
    ppermute x18, waiting for transfers between devices, shift(): return lax.ppermute(x, 'col', [(c, (c + step) % cols) for c in range(cols)])  94.6 us
    pallas_call x3, Pallas kernels, some_heads(): pl.pallas_call(functools.partial(heads_kernel, heads), out_shape=jax.Shap...  42.4 us
    ppermute x18, starting transfers between devices, shift(): return lax.ppermute(x, 'col', [(c, (c + step) % cols) for c in range(cols)])  31.6 us
    pallas_call x1, Pallas kernels, fill_and_norm(): pl.pallas_call(functools.partial(norm_kernel, cols, part, len(late)), out...  28 us
    pallas_call x3, Pallas kernels, project(): pl.pallas_call(functools.partial(out_kernel, n, acc is not None), out_sha...  16.2 us
    pallas_call x2, Pallas kernels, place(): pl.pallas_call(functools.partial(place_kernel, [len(t) for t in tables],...  15.9 us
    unnamed x49, local copies, waits for them, and re-layouts  10.2 us
    ppermute x14, starting transfers between devices, swap(): return lax.ppermute(x, 'row', pairs)  9.17 us
  transfers between devices with their start and end apart: 36, of which 17 were waited for; matrix products, arithmetic and copies ran while one was open for 1% of the time, Pallas kernels for 36%

profile of v6, /device:TPU:0, one launch (start us, length us, event | category | flops | bytes accessed | tf_op | source)
XLA Modules:
  0.0 285.4 jit_solution(5600324445921175741)
XLA Ops:
  21.8 6.0 %place.2.own_ref = bf16[1024,1024]{1,0:T(8,128)(2,1)} custom-call(s32[1024,128]{1,0:T(8,128)} %select_select_fusion.ids_ref, bf16[1024,1024]{1,0:T(8,128)(2,1)} %refs_0_.3), custom_call_target="tpu_custom_call" | custom-call | flops 1 | bytes 1 | tf_op jit(solution)/shard_map/place/pallas_call | solution.py:183
  29.3 5.6 %collective-permute-done.1.refs_9_ = bf16[144,1024]{1,0:T(8,128)(2,1)S(1)} collective-permute-done((bf16[144,1024]{1,0:T(8,128)(2,1)S(1)}, bf16[144,1024]{1,0:T(8,128)(2,1)S(1)}, u32[]{:S(2)}, u32[]{:S(2)}) %collective-permute-start.1) | collective-permute-done | bytes 294944 | tf_op jit(solution)/shard_map/ppermute | solution.py:82
  39.4 6.8 %collective-permute-start.5 = (bf16[64,4096]{1,0:T(8,128)(2,1)S(1)}, bf16[64,4096]{1,0:T(8,128)(2,1)S(1)}, u32[]{:S(2)}, u32[]{:S(2)}) collective-permute-start(bf16[64,4096]{1,0:T(8,128)(2,1)S(1)} %copy-done.10), channel_id=1, source_target_pairs={{0,1},{1,2},{2,3},{3,0},{4,5},{5,6},{6,7},{7,4},{8,9},{9,10},{10,1... | collective-permute-start | bytes 1572872 | tf_op jit(solution)/shard_map/ppermute | solution.py:82
  47.2 12.9 %collective-permute-done.5.refs_4_ = bf16[64,4096]{1,0:T(8,128)(2,1)S(1)} collective-permute-done((bf16[64,4096]{1,0:T(8,128)(2,1)S(1)}, bf16[64,4096]{1,0:T(8,128)(2,1)S(1)}, u32[]{:S(2)}, u32[]{:S(2)}) %collective-permute-start.5) | collective-permute-done | bytes 524320 | tf_op jit(solution)/shard_map/ppermute | solution.py:82
  60.1 8.9 %collective-permute-done.6.refs_6_ = bf16[64,4096]{1,0:T(8,128)(2,1)S(1)} collective-permute-done((bf16[64,4096]{1,0:T(8,128)(2,1)S(1)}, bf16[64,4096]{1,0:T(8,128)(2,1)S(1)}, u32[]{:S(2)}, u32[]{:S(2)}) %collective-permute-start.6) | collective-permute-done | bytes 524320 | tf_op jit(solution)/shard_map/ppermute | solution.py:82
  78.0 9.9 %place.3.near_ref = bf16[1024,3072]{1,0:T(8,128)(2,1)} custom-call(s32[1024,128]{1,0:T(8,128)} %select_select_fusion.ids_ref, bf16[128,3072]{1,0:T(8,128)(2,1)} %copy-done.13, bf16[128,3072]{1,0:T(8,128)(2,1)} %collective-permute-done.3.refs_1_, bf16[128,3072]{1,0:T(8,128)(2,1)} %copy-done.15, bf16[128,3072]{1,0:T(8,128)(2,1)} %copy-done.17, ...), custom_call_target="tpu_custom_call" | custom-call | flops 1 | bytes 1 | tf_op jit(solution)/shard_map/place/pallas_call | solution.py:183
  94.8 28.0 %fill_norm.1 = (bf16[1024,4096]{1,0:T(8,128)(2,1)}, bf16[1024,256]{1,0:T(8,128)(2,1)S(1)}) custom-call(s32[4]{0:T(128)S(1)} %and_select_fusion.col_ref.at_ref, s32[1,256]{1,0:T(1,128)S(1)} %reshape.63.keep_ref, s32[1024,128]{1,0:T(8,128)S(1)} %copy-done.2, bf16[1024,1024]{1,0:T(8,128)(2,1)} %place.2.own_ref, bf16[1024,3072]{1,0:T(8,128)(2,1)} %place.3.near_ref, ...), custom_call_target="tpu_custom_call" | custom-call | flops 1 | bytes 1 | tf_op jit(solution)/shard_map/fill_norm/pallas_call | solution.py:266
  124.1 3.8 %collective-permute-start.16 = (bf16[1024,256]{1,0:T(8,128)(2,1)S(1)}, bf16[1024,256]{1,0:T(8,128)(2,1)S(1)}, u32[]{:S(2)}, u32[]{:S(2)}) collective-permute-start(bf16[1024,256]{1,0:T(8,128)(2,1)S(1)} %get-tuple-element.132.refs_0_), channel_id=1, source_target_pairs={{0,3},{1,0},{2,1},{3,2},{4,7},{5,4},{6,5},{7,6},{8,11},{9,8},{10,9... | collective-permute-start | bytes 1572872 | tf_op jit(solution)/shard_map/ppermute | solution.py:82
  131.6 13.9 %heads_2.3.refs_4_ = bf16[1024,256]{1,0:T(8,128)(2,1)} custom-call(s32[8]{0:T(128)} %stack.35.source_ref, bf16[1024,4096]{1,0:T(8,128)(2,1)} %get-tuple-element.122.x_ref, bf16[4096,768]{1,0:T(8,128)(2,1)} %all-gather.7.cloned.1.call-done.refs_0_), custom_call_target="tpu_custom_call" | custom-call | flops 1 | bytes 1 | tf_op jit(solution)/shard_map/heads_2/pallas_call | solution.py:311
  145.5 3.7 %collective-permute-done.16.refs_3_ = bf16[1024,256]{1,0:T(8,128)(2,1)S(1)} collective-permute-done((bf16[1024,256]{1,0:T(8,128)(2,1)S(1)}, bf16[1024,256]{1,0:T(8,128)(2,1)S(1)}, u32[]{:S(2)}, u32[]{:S(2)}) %collective-permute-start.16) | collective-permute-done | bytes 524320 | tf_op jit(solution)/shard_map/ppermute | solution.py:82
  153.9 14.5 %heads_2.4.refs_0_ = bf16[1024,256]{1,0:T(8,128)(2,1)} custom-call(s32[8]{0:T(128)} %stack.35.source_ref, bf16[1024,4096]{1,0:T(8,128)(2,1)} %get-tuple-element.122.x_ref, bf16[512,768]{1,0:T(8,128)(2,1)} %get-tuple-element.112.refs_0_, bf16[512,768]{1,0:T(8,128)(2,1)} %collective-permute-done.13.refs_1_, bf16[512,768]{1,0:T(8,128)(2,1)} %collective-permute-done.14.refs_2_, ...), custom_call_target="tpu_custom_call" | custom-call | flops 1 | bytes 1 | tf_op jit(solution)/shard_map/heads_2/pallas_call | solution.py:311
  168.5 8.0 %collective-permute-done.23.refs_7_ = bf16[1024,256]{1,0:T(8,128)(2,1)S(1)} collective-permute-done((bf16[1024,256]{1,0:T(8,128)(2,1)}, bf16[1024,256]{1,0:T(8,128)(2,1)S(1)}, u32[]{:S(2)}, u32[]{:S(2)}) %collective-permute-start.23) | collective-permute-done | bytes 524320 | tf_op jit(solution)/shard_map/ppermute | solution.py:82
  177.3 10.9 %collective-permute-done.24.refs_2_ = bf16[1024,256]{1,0:T(8,128)(2,1)S(1)} collective-permute-done((bf16[1024,256]{1,0:T(8,128)(2,1)S(1)}, bf16[1024,256]{1,0:T(8,128)(2,1)S(1)}, u32[]{:S(2)}, u32[]{:S(2)}) %collective-permute-start.24) | collective-permute-done | bytes 524320 | tf_op jit(solution)/shard_map/ppermute | solution.py:82
  189.0 3.8 %collective-permute-start.26 = (bf16[1024,256]{1,0:T(8,128)(2,1)}, bf16[1024,256]{1,0:T(8,128)(2,1)}, u32[]{:S(2)}, u32[]{:S(2)}) collective-permute-start(bf16[1024,256]{1,0:T(8,128)(2,1)} %heads_2.4.refs_0_), channel_id=1, source_target_pairs={{0,3},{1,0},{2,1},{3,2},{4,7},{5,4},{6,5},{7,6},{8,11},{9,8},{10,9... | collective-permute-start | bytes 1572872 | tf_op jit(solution)/shard_map/ppermute | solution.py:82
  192.9 14.0 %heads_2.5.refs_4_ = bf16[1024,256]{1,0:T(8,128)(2,1)} custom-call(s32[8]{0:T(128)} %stack.35.source_ref, bf16[1024,4096]{1,0:T(8,128)(2,1)} %get-tuple-element.122.x_ref, bf16[4096,768]{1,0:T(8,128)(2,1)} %all-gather.9.cloned.1.call-done.refs_0_), custom_call_target="tpu_custom_call" | custom-call | flops 1 | bytes 1 | tf_op jit(solution)/shard_map/heads_2/pallas_call | solution.py:311
  206.9 6.7 %collective-permute-done.26.refs_3_ = bf16[1024,256]{1,0:T(8,128)(2,1)} collective-permute-done((bf16[1024,256]{1,0:T(8,128)(2,1)}, bf16[1024,256]{1,0:T(8,128)(2,1)}, u32[]{:S(2)}, u32[]{:S(2)}) %collective-permute-start.26) | collective-permute-done | bytes 524320 | tf_op jit(solution)/shard_map/ppermute | solution.py:82
  213.6 12.9 %collective-permute-done.27.refs_6_ = bf16[1024,256]{1,0:T(8,128)(2,1)} collective-permute-done((bf16[1024,256]{1,0:T(8,128)(2,1)S(1)}, bf16[1024,256]{1,0:T(8,128)(2,1)}, u32[]{:S(2)}, u32[]{:S(2)}) %collective-permute-start.27) | collective-permute-done | bytes 524320 | tf_op jit(solution)/shard_map/ppermute | solution.py:82
  226.5 3.8 %collective-permute-start.29 = (bf16[1024,256]{1,0:T(8,128)(2,1)}, bf16[1024,256]{1,0:T(8,128)(2,1)}, u32[]{:S(2)}, u32[]{:S(2)}) collective-permute-start(bf16[1024,256]{1,0:T(8,128)(2,1)} %heads_2.5.refs_4_), channel_id=1, source_target_pairs={{0,3},{1,0},{2,1},{3,2},{4,7},{5,4},{6,5},{7,6},{8,11},{9,8},{10,9... | collective-permute-start | bytes 1572872 | tf_op jit(solution)/shard_map/ppermute | solution.py:82
  230.3 4.4 %all-gather.11.cloned.1.call-done.refs_8_.refs_9_.refs_10_.refs_11_.refs_12_.refs_13_.refs_14_.refs_15_.refs_7_.refs_1_ = bf16[4096,1024]{1,0:T(8,128)(2,1)} async-done(((bf16[512,1024]{1,0:T(8,128)(2,1)}), bf16[4096,1024]{1,0:T(8,128)(2,1)}) %all-gather.11.cloned.1.call-update) | async-done | bytes 8388624 | tf_op jit(solution)/shard_map/all_gather | solution.py:431
  240.2 6.8 %out_proj.3.refs_14_ = f32[1024,1024]{1,0:T(8,128)S(1)} custom-call(s32[4]{0:T(128)S(1)} %and_select_fusion.col_ref.at_ref, bf16[1024,256]{1,0:T(8,128)(2,1)S(1)} %get-tuple-element.132.refs_0_, bf16[1024,256]{1,0:T(8,128)(2,1)S(1)} %collective-permute-done.15.refs_1_, bf16[1024,256]{1,0:T(8,128)(2,1)S(1)} %copy-done.9, ...), custom_call_target="tpu_custom_call" | custom-call | flops 1 | bytes 1 | tf_op jit(solution)/shard_map/out_proj/pallas_call | solution.py:365
  246.9 4.1 %collective-permute-done.29.refs_6_ = bf16[1024,256]{1,0:T(8,128)(2,1)} collective-permute-done((bf16[1024,256]{1,0:T(8,128)(2,1)}, bf16[1024,256]{1,0:T(8,128)(2,1)}, u32[]{:S(2)}, u32[]{:S(2)}) %collective-permute-start.29) | collective-permute-done | bytes 524320 | tf_op jit(solution)/shard_map/ppermute | solution.py:82
  251.0 11.9 %collective-permute-done.30.refs_2_ = bf16[1024,256]{1,0:T(8,128)(2,1)} collective-permute-done((bf16[1024,256]{1,0:T(8,128)(2,1)}, bf16[1024,256]{1,0:T(8,128)(2,1)}, u32[]{:S(2)}, u32[]{:S(2)}) %collective-permute-start.30) | collective-permute-done | bytes 524320 | tf_op jit(solution)/shard_map/ppermute | solution.py:82
  262.9 6.3 %out_proj.4.refs_2_ = f32[1024,1024]{1,0:T(8,128)S(1)} custom-call(s32[4]{0:T(128)S(1)} %and_select_fusion.col_ref.at_ref, bf16[1024,256]{1,0:T(8,128)(2,1)S(1)} %copy-done.4, bf16[1024,256]{1,0:T(8,128)(2,1)} %collective-permute-done.25.refs_1_, bf16[1024,256]{1,0:T(8,128)(2,1)} %collective-permute-done.30.refs_2_, ...), custom_call_target="tpu_custom_call", output_to_operand_aliasing={{}: (15, {})} | custom-call | flops 1 | bytes 1 | tf_op jit(solution)/shard_map/out_proj/pallas_call | solution.py:365
  269.3 6.6 %collective-permute-done.31.refs_0_ = bf16[1024,256]{1,0:T(8,128)(2,1)S(1)} collective-permute-done((bf16[1024,256]{1,0:T(8,128)(2,1)}, bf16[1024,256]{1,0:T(8,128)(2,1)S(1)}, u32[]{:S(2)}, u32[]{:S(2)}) %collective-permute-start.31) | collective-permute-done | bytes 524320 | tf_op jit(solution)/shard_map/ppermute | solution.py:82
  (133 shorter events, 57.8 us)
Async XLA Ops:
  6.5 87.3 %all-gather.5.cloned.1.call-start = ((), (), s32[]{:S(2)}) async-start(), calls=%async_computation | async-start | bytes 7077888 | tf_op jit(solution)/shard_map/all_gather | solution.py:431
  8.7 122.9 %all-gather.7.cloned.1.call-start = ((), (), s32[]{:S(2)}) async-start(), calls=%async_computation.1 | async-start | bytes 7077888 | tf_op jit(solution)/shard_map/all_gather | solution.py:431
  9.9 19.3 %collective-permute-start = (bf16[144,1024]{1,0:T(8,128)(2,1)S(1)}, bf16[144,1024]{1,0:T(8,128)(2,1)S(1)}, u32[]{:S(2)}, u32[]{:S(2)}) collective-permute-start(bf16[144,1024]{1,0:T(8,128)(2,1)S(1)} %maximum_maximum_fusion.refs_7_), channel_id=1, source_target_pairs={{0,1},{1,2},{2,3},{3,0},{4,5},{5,6},{6,7},{7,4},{8,9},{9,10},{10,1... | collective-permute-start | bytes 884744 | tf_op jit(solution)/shard_map/ppermute | solution.py:82
  13.0 21.8 %collective-permute-start.1 = (bf16[144,1024]{1,0:T(8,128)(2,1)S(1)}, bf16[144,1024]{1,0:T(8,128)(2,1)S(1)}, u32[]{:S(2)}, u32[]{:S(2)}) collective-permute-start(bf16[144,1024]{1,0:T(8,128)(2,1)S(1)} %maximum_maximum_fusion.refs_7_), channel_id=1, source_target_pairs={{0,2},{1,3},{2,0},{3,1},{4,6},{5,7},{6,4},{7,5},{8,10},{9,11},{10,... | collective-permute-start | bytes 884744 | tf_op jit(solution)/shard_map/ppermute | solution.py:82
  34.9 158.0 %all-gather.9.cloned.1.call-start = ((), (), s32[]{:S(2)}) async-start(), calls=%async_computation.2 | async-start | bytes 7077888 | tf_op jit(solution)/shard_map/all_gather | solution.py:431
  35.6 199.1 %all-gather.11.cloned.1.call-start = ((), (), s32[]{:S(2)}) async-start(), calls=%async_computation.3 | async-start | bytes 9437184 | tf_op jit(solution)/shard_map/all_gather | solution.py:431
  36.3 36.2 %collective-permute-start.3 = (bf16[128,3072]{1,0:T(8,128)(2,1)S(1)}, bf16[128,3072]{1,0:T(8,128)(2,1)}, u32[]{:S(2)}, u32[]{:S(2)}) collective-permute-start(bf16[128,3072]{1,0:T(8,128)(2,1)S(1)} %pad_maximum_fusion.refs_0_), channel_id=1, source_target_pairs={{0,8},{4,20},{8,0},{12,28},{16,24},{20,4},{24,16},{28,12},{1,9},{5... | collective-permute-start | bytes 2359304 | tf_op jit(solution)/shard_map/ppermute | solution.py:37
  37.9 34.7 %collective-permute-start.4 = (bf16[128,3072]{1,0:T(8,128)(2,1)S(1)}, bf16[128,3072]{1,0:T(8,128)(2,1)S(1)}, u32[]{:S(2)}, u32[]{:S(2)}) collective-permute-start(bf16[128,3072]{1,0:T(8,128)(2,1)S(1)} %pad_maximum_fusion.refs_0_), channel_id=1, source_target_pairs={{0,16},{4,12},{8,24},{12,4},{16,0},{20,28},{24,8},{28,20},{1,17},{... | collective-permute-start | bytes 2359304 | tf_op jit(solution)/shard_map/ppermute | solution.py:37
  39.4 20.7 %collective-permute-start.5 = (bf16[64,4096]{1,0:T(8,128)(2,1)S(1)}, bf16[64,4096]{1,0:T(8,128)(2,1)S(1)}, u32[]{:S(2)}, u32[]{:S(2)}) collective-permute-start(bf16[64,4096]{1,0:T(8,128)(2,1)S(1)} %copy-done.10), channel_id=1, source_target_pairs={{0,1},{1,2},{2,3},{3,0},{4,5},{5,6},{6,7},{7,4},{8,9},{9,10},{10,1... | collective-permute-start | bytes 1572872 | tf_op jit(solution)/shard_map/ppermute | solution.py:82
  46.2 22.8 %collective-permute-start.6 = (bf16[64,4096]{1,0:T(8,128)(2,1)S(1)}, bf16[64,4096]{1,0:T(8,128)(2,1)S(1)}, u32[]{:S(2)}, u32[]{:S(2)}) collective-permute-start(bf16[64,4096]{1,0:T(8,128)(2,1)S(1)} %copy-done.10), channel_id=1, source_target_pairs={{0,3},{1,0},{2,1},{3,2},{4,7},{5,4},{6,5},{7,6},{8,11},{9,8},{10,9... | collective-permute-start | bytes 1572872 | tf_op jit(solution)/shard_map/ppermute | solution.py:82
  91.2 31.7 %collective-permute-start.13 = (bf16[512,768]{1,0:T(8,128)(2,1)}, bf16[512,768]{1,0:T(8,128)(2,1)}, u32[]{:S(2)}, u32[]{:S(2)}) collective-permute-start(bf16[512,768]{1,0:T(8,128)(2,1)} %get-tuple-element.112.refs_0_), channel_id=1, source_target_pairs={{0,8},{4,20},{8,0},{12,28},{16,24},{20,4},{24,16},{28,12},{1,9},{5... | collective-permute-start | bytes 2359304 | tf_op jit(solution)/shard_map/ppermute | solution.py:37
  91.8 31.1 %collective-permute-start.14 = (bf16[512,768]{1,0:T(8,128)(2,1)}, bf16[512,768]{1,0:T(8,128)(2,1)}, u32[]{:S(2)}, u32[]{:S(2)}) collective-permute-start(bf16[512,768]{1,0:T(8,128)(2,1)} %get-tuple-element.112.refs_0_), channel_id=1, source_target_pairs={{0,16},{4,12},{8,24},{12,4},{16,0},{20,28},{24,8},{28,20},{1,17},{... | collective-permute-start | bytes 2359304 | tf_op jit(solution)/shard_map/ppermute | solution.py:37
  122.9 26.3 %collective-permute-start.17 = (bf16[512,768]{1,0:T(8,128)(2,1)}, bf16[512,768]{1,0:T(8,128)(2,1)}, u32[]{:S(2)}, u32[]{:S(2)}) collective-permute-start(bf16[512,768]{1,0:T(8,128)(2,1)} %collective-permute-done.13.refs_1_), channel_id=1, source_target_pairs={{0,16},{4,12},{8,24},{12,4},{16,0},{20,28},{24,8},{28,20},{1,17},{... | collective-permute-start | bytes 2359304 | tf_op jit(solution)/shard_map/ppermute | solution.py:37
  123.6 25.6 %collective-permute-start.18 = (bf16[512,768]{1,0:T(8,128)(2,1)}, bf16[512,768]{1,0:T(8,128)(2,1)S(1)}, u32[]{:S(2)}, u32[]{:S(2)}) collective-permute-start(bf16[512,768]{1,0:T(8,128)(2,1)} %get-tuple-element.112.refs_0_), channel_id=1, source_target_pairs={{0,4},{4,0},{8,12},{12,8},{16,20},{20,16},{24,28},{28,24},{1,5},{5... | collective-permute-start | bytes 2359304 | tf_op jit(solution)/shard_map/ppermute | solution.py:37
  123.6 25.6 %collective-permute-start.19 = (bf16[512,768]{1,0:T(8,128)(2,1)}, bf16[512,768]{1,0:T(8,128)(2,1)}, u32[]{:S(2)}, u32[]{:S(2)}) collective-permute-start(bf16[512,768]{1,0:T(8,128)(2,1)} %collective-permute-done.13.refs_1_), channel_id=1, source_target_pairs={{0,4},{4,0},{8,12},{12,8},{16,20},{20,16},{24,28},{28,24},{1,5},{5... | collective-permute-start | bytes 2359304 | tf_op jit(solution)/shard_map/ppermute | solution.py:37
  124.1 21.3 %collective-permute-start.15 = (bf16[1024,256]{1,0:T(8,128)(2,1)S(1)}, bf16[1024,256]{1,0:T(8,128)(2,1)S(1)}, u32[]{:S(2)}, u32[]{:S(2)}) collective-permute-start(bf16[1024,256]{1,0:T(8,128)(2,1)S(1)} %get-tuple-element.132.refs_0_), channel_id=1, source_target_pairs={{0,1},{1,2},{2,3},{3,0},{4,5},{5,6},{6,7},{7,4},{8,9},{9,10},{10,1... | collective-permute-start | bytes 1572872 | tf_op jit(solution)/shard_map/ppermute | solution.py:82
  124.1 25.1 %collective-permute-start.16 = (bf16[1024,256]{1,0:T(8,128)(2,1)S(1)}, bf16[1024,256]{1,0:T(8,128)(2,1)S(1)}, u32[]{:S(2)}, u32[]{:S(2)}) collective-permute-start(bf16[1024,256]{1,0:T(8,128)(2,1)S(1)} %get-tuple-element.132.refs_0_), channel_id=1, source_target_pairs={{0,3},{1,0},{2,1},{3,2},{4,7},{5,4},{6,5},{7,6},{8,11},{9,8},{10,9... | collective-permute-start | bytes 1572872 | tf_op jit(solution)/shard_map/ppermute | solution.py:82
  151.1 25.3 %collective-permute-start.23 = (bf16[1024,256]{1,0:T(8,128)(2,1)}, bf16[1024,256]{1,0:T(8,128)(2,1)S(1)}, u32[]{:S(2)}, u32[]{:S(2)}) collective-permute-start(bf16[1024,256]{1,0:T(8,128)(2,1)} %heads_2.3.refs_4_), channel_id=1, source_target_pairs={{0,3},{1,0},{2,1},{3,2},{4,7},{5,4},{6,5},{7,6},{8,11},{9,8},{10,9... | collective-permute-start | bytes 1572872 | tf_op jit(solution)/shard_map/ppermute | solution.py:82
  153.9 34.3 %collective-permute-start.24 = (bf16[1024,256]{1,0:T(8,128)(2,1)S(1)}, bf16[1024,256]{1,0:T(8,128)(2,1)S(1)}, u32[]{:S(2)}, u32[]{:S(2)}) collective-permute-start(bf16[1024,256]{1,0:T(8,128)(2,1)S(1)} %collective-permute-done.15.refs_1_), channel_id=1, source_target_pairs={{0,1},{1,2},{2,3},{3,0},{4,5},{5,6},{6,7},{7,4},{8,9},{9,10},{10,1... | collective-permute-start | bytes 1572872 | tf_op jit(solution)/shard_map/ppermute | solution.py:82
  189.0 24.5 %collective-permute-start.26 = (bf16[1024,256]{1,0:T(8,128)(2,1)}, bf16[1024,256]{1,0:T(8,128)(2,1)}, u32[]{:S(2)}, u32[]{:S(2)}) collective-permute-start(bf16[1024,256]{1,0:T(8,128)(2,1)} %heads_2.4.refs_0_), channel_id=1, source_target_pairs={{0,3},{1,0},{2,1},{3,2},{4,7},{5,4},{6,5},{7,6},{8,11},{9,8},{10,9... | collective-permute-start | bytes 1572872 | tf_op jit(solution)/shard_map/ppermute | solution.py:82
  192.9 33.6 %collective-permute-start.27 = (bf16[1024,256]{1,0:T(8,128)(2,1)S(1)}, bf16[1024,256]{1,0:T(8,128)(2,1)}, u32[]{:S(2)}, u32[]{:S(2)}) collective-permute-start(bf16[1024,256]{1,0:T(8,128)(2,1)S(1)} %collective-permute-done.22.refs_5_), channel_id=1, source_target_pairs={{0,1},{1,2},{2,3},{3,0},{4,5},{5,6},{6,7},{7,4},{8,9},{9,10},{10,1... | collective-permute-start | bytes 1572872 | tf_op jit(solution)/shard_map/ppermute | solution.py:82
  226.5 20.5 %collective-permute-start.28 = (bf16[1024,256]{1,0:T(8,128)(2,1)}, bf16[1024,256]{1,0:T(8,128)(2,1)}, u32[]{:S(2)}, u32[]{:S(2)}) collective-permute-start(bf16[1024,256]{1,0:T(8,128)(2,1)} %heads_2.5.refs_4_), channel_id=1, source_target_pairs={{0,1},{1,2},{2,3},{3,0},{4,5},{5,6},{6,7},{7,4},{8,9},{9,10},{10,1... | collective-permute-start | bytes 1572872 | tf_op jit(solution)/shard_map/ppermute | solution.py:82
  226.5 24.5 %collective-permute-start.29 = (bf16[1024,256]{1,0:T(8,128)(2,1)}, bf16[1024,256]{1,0:T(8,128)(2,1)}, u32[]{:S(2)}, u32[]{:S(2)}) collective-permute-start(bf16[1024,256]{1,0:T(8,128)(2,1)} %heads_2.5.refs_4_), channel_id=1, source_target_pairs={{0,3},{1,0},{2,1},{3,2},{4,7},{5,4},{6,5},{7,6},{8,11},{9,8},{10,9... | collective-permute-start | bytes 1572872 | tf_op jit(solution)/shard_map/ppermute | solution.py:82
  230.3 32.6 %collective-permute-start.30 = (bf16[1024,256]{1,0:T(8,128)(2,1)}, bf16[1024,256]{1,0:T(8,128)(2,1)}, u32[]{:S(2)}, u32[]{:S(2)}) collective-permute-start(bf16[1024,256]{1,0:T(8,128)(2,1)} %collective-permute-done.25.refs_1_), channel_id=1, source_target_pairs={{0,1},{1,2},{2,3},{3,0},{4,5},{5,6},{6,7},{7,4},{8,9},{9,10},{10,1... | collective-permute-start | bytes 1572872 | tf_op jit(solution)/shard_map/ppermute | solution.py:82
  (35 other events, 445.3 us)
Sparse Core Ops, SparseCore 0:
  9.2 64.2 all-gather.4
  75.4 56.1 all-gather.6
  133.5 45.0 all-gather.8
  180.3 54.3 all-gather.10
